TPU v7x, 256 devices: a whole 4x4x8 slice. The times are simulated.
256 devices in a mesh: aa: 32 (over y, x, z_hi), ga: 8 (over z_lo, core).
Axes of the slice: x: 4, y: 4, z: 8 (z_hi: 2, z_lo: 4; z = z_hi * 4 + z_lo), core: 2. Of those that a mesh axis runs over, the one named last changes fastest.
Arguments:
- activations: bfloat16 [256, 8192], P(None, 'ga'), may hold values from -6 to 6
- out_grads: bfloat16 [256, 28672], P(None, 'aa'), may hold values from -6 to 6
- train_acts: bfloat16 [256, 8192], P(None, 'ga'), may hold values from -6 to 6
- train_grads: bfloat16 [256, 28672], P(None, 'aa'), may hold values from -6 to 6
- basis_in: bfloat16 [8192, 8192], P('ga', 'aa'), may hold values from -0.0625 to 0.0625
- basis_out: bfloat16 [28672, 28672], P('aa', 'ga'), may hold values from -0.03125 to 0.03125
- eigen_diag: bfloat16 [28672, 8192], P('ga', 'aa'), may hold values from 4 to 64
- damp_grid: float32 [16], replicated, may hold values from 0.5 to 8
- damp_pick: int32 [2], replicated, may hold values from 0 to 15
Outputs:
- scores: float32 [2, 256], replicated
Inputs may be any that keep to these rules, and one draw needn't show every extreme that they name: `damp_pick`: indices into damp_grid.
All inputs are finite; a program needn't handle non-finite values.
Results may differ from a plain program's by a relative error of at most 0.0054.
Values may be sent and summed in bfloat16 or wider, within the bound.
No kernel may reach another device: no remote copies, remote signals or barrier semaphores. Data moves between devices by JAX's collectives and lax.ppermute only.
A program may use at most 64 MiB of HBM per device.

v0:
```python
import math

import jax
import jax.numpy as jnp
from jax import lax
from jax.sharding import PartitionSpec as P

D_IN = 8192
D_OUT = 28672


def body(
    activations,
    out_grads,
    train_acts,
    train_grads,
    basis_in,
    basis_out,
    eigen_diag,
    damp_grid,
    damp_pick,
):
    query_rows = activations.shape[0]
    inputs = jnp.concatenate([activations, train_acts], axis=0)
    in_partial = jnp.dot(inputs, basis_in, preferred_element_type=jnp.float32)
    rot_in_all = lax.psum(in_partial, "ga").astype(jnp.bfloat16)
    rot_in = rot_in_all[:query_rows]
    train_in = rot_in_all[query_rows:]
    grads = jnp.concatenate([out_grads, train_grads], axis=0)
    eig_local = basis_out.shape[1]
    rot_out_all = lax.psum(
        lax.dot_general(
            basis_out, grads, (((0,), (1,)), ((), ())), preferred_element_type=jnp.float32
        ),
        "aa",
    ).astype(jnp.bfloat16)
    rot_out = rot_out_all[:, :query_rows]
    train_out = rot_out_all[:, query_rows:]
    seqs = damp_pick.shape[0]
    per_seq = query_rows // seqs
    in_width = rot_in.shape[1]
    rotated = jnp.einsum(
        "est,stj->sej",
        rot_out.reshape(eig_local, seqs, per_seq),
        rot_in.reshape(seqs, per_seq, in_width),
        preferred_element_type=jnp.float32,
    )
    matches = damp_pick[:, None] == jnp.arange(damp_grid.shape[0], dtype=jnp.int32)[None, :]
    damping = jnp.sum(
        jnp.where(matches, damp_grid[None, :], jnp.zeros_like(damp_grid)[None, :]), axis=1
    )
    precond = (rotated / (eigen_diag.astype(jnp.float32)[None] + damping[:, None, None])).astype(
        jnp.bfloat16
    )
    weighted = jnp.einsum("sej,tj->set", precond, train_in, preferred_element_type=jnp.float32)
    local_scores = jnp.sum(weighted * train_out.astype(jnp.float32)[None], axis=1)
    total = lax.psum(local_scores, ("aa", "ga"))
    return total * (1.0 / math.sqrt(D_IN * D_OUT))


def solution(mesh):
    return jax.shard_map(
        body,
        mesh=mesh,
        in_specs=(
            P(None, "ga"),
            P(None, "aa"),
            P(None, "ga"),
            P(None, "aa"),
            P("ga", "aa"),
            P("aa", "ga"),
            P("ga", "aa"),
            P(),
            P(),
        ),
        out_specs=P(),
        check_vma=False,
    )
```

profile of v0, /device:TPU:1, one launch (start us, length us, event | category | flops | bytes accessed | tf_op | source)
XLA Modules:
  0.0 793.0 jit_solution(69807417102731125)
XLA Ops:
  0.0 0.0 copy-start
  0.0 10.1 %convolution_bitcast_fusion = f32[3584,512]{0,1:T(8,128)} fusion(bf16[896,3584]{1,0:T(8,128)(2,1)} %param.14, bf16[256,896]{1,0:T(8,128)(2,1)} %param.12, bf16[256,896]{1,0:T(8,128)(2,1)} %param.10), kind=kOutput, calls=%fused_computation.2 | convolution fusion | flops 3290169344 | bytes 14680064 | tf_op jit(solution)/shard_map/dot_general | solution.py:32
  10.1 646.8 %all-reduce.2 = bf16[3584,512]{0,1:T(8,128)(2,1)} all-reduce(f32[3584,512]{0,1:T(8,128)} %convolution_bitcast_fusion), channel_id=1, replica_groups=mesh['aa'=32,'ga'=8] {'aa'}, use_global_device_ids=true, to_apply=%region_0.0 | all-reduce | flops 1835008 | bytes 11010048 | tf_op jit(solution)/shard_map/psum | solution.py:31
  656.9 4.8 fusion.10
  661.7 5.1 copy.11
  666.9 0.0 copy-start.1
  666.9 0.0 copy-done
  666.9 1.8 fusion
  668.7 0.0 copy-start.2
  668.7 0.0 copy-start.3
  668.7 36.9 %all-reduce.3 = bf16[512,256]{1,0:T(8,128)(2,1)S(1)} all-reduce(f32[512,256]{1,0:T(8,128)S(1)} %fusion), channel_id=1, replica_groups=mesh['aa'=32,'ga'=8] {'ga'}, use_global_device_ids=true, to_apply=%region_1.0 | all-reduce | flops 131072 | bytes 786432 | tf_op jit(solution)/shard_map/psum | solution.py:26
  705.6 0.0 copy-done.1
  705.6 2.1 convert_element_type.17
  707.7 0.0 copy-done.2
  707.7 0.0 copy-done.3
  707.7 0.2 fusion.7
  707.9 6.0 multiply_reduce_fusion
  714.0 78.5 %psum.23 = f32[2,256]{1,0:T(2,128)S(1)} all-reduce(f32[2,256]{1,0:T(2,128)S(1)} %multiply_reduce_fusion), channel_id=1, replica_groups=mesh['aa'=32,'ga'=8] {'aa','ga'}, use_global_device_ids=true, to_apply=%region_4.5 | all-reduce | flops 512 | bytes 4096 | tf_op jit(solution)/shard_map/psum | solution.py:57
  792.4 0.6 broadcast_multiply_fusion
  (1 shorter events, 0.0 us)
Async XLA Ops:
  0.0 666.9 %copy-start = (bf16[1024,256]{1,0:T(8,128)(2,1)S(1)}, bf16[1024,256]{1,0:T(8,128)(2,1)}, u32[]{:S(2)}) copy-start(bf16[1024,256]{1,0:T(8,128)(2,1)} %param.13) | copy-start | bytes 1572868
  666.9 38.8 %copy-start.1 = (bf16[3584,256]{1,0:T(8,128)(2,1)S(1)}, bf16[3584,256]{1,0:T(8,128)(2,1)}, u32[]{:S(2)}) copy-start(bf16[3584,256]{1,0:T(8,128)(2,1)} %param.15) | copy-start | bytes 5505028
  668.7 39.1 %copy-start.2 = (f32[16]{0:T(128)S(1)}, f32[16]{0:T(128)}, u32[]{:S(2)}) copy-start(f32[16]{0:T(128)} %param.16) | copy-start | bytes 196
  668.7 39.1 %copy-start.3 = (s32[2]{0:T(128)S(1)}, s32[2]{0:T(128)}, u32[]{:S(2)}) copy-start(s32[2]{0:T(128)} %param.17) | copy-start | bytes 28
where the time goes:
time: 793 us
  blocking collectives  762 us (96%)
  matrix products  17.9 us (2%)
    psum x1, blocking collectives, body(): lax.psum(lax.dot_general(basis_out, grads, (((0,), (1,)), ((), ())), pref...  647 us
    psum x1, blocking collectives, body(): total = lax.psum(local_scores, ('aa', 'ga'))  78.5 us
    psum x1, blocking collectives, body(): rot_in_all = lax.psum(in_partial, 'ga').astype(jnp.bfloat16)  36.9 us

commit v1 on v0

v1 whole, which is shorter than its diff:
```python
import functools
import itertools
import math

import jax
import jax.numpy as jnp
from jax import lax
from jax.experimental import pallas as pl
from jax.experimental.pallas import tpu as pltpu
from jax.sharding import Mesh, PartitionSpec as P

D_IN = 8192
D_OUT = 28672
SIZES = (4, 4, 2, 4, 2)
ALL = ("y", "x", "zh", "zl", "c")
SCALE = 1.0 / math.sqrt(D_IN * D_OUT)
BF = jnp.bfloat16
F32 = jnp.float32
VLIM = 56 * 1024 * 1024


def flat(place):
    n = 0
    for size, at in zip(SIZES, place):
        n = n * size + at
    return n


def shift(k, first):
    pairs = []
    for y, x, zh, zl, c in itertools.product(*(range(s) for s in SIZES)):
        if (c == 0) == first:
            to = (y, (x + k) % 4, zh, zl, c)
        else:
            to = ((y + k) % 4, x, zh, zl, c)
        pairs.append((flat((y, x, zh, zl, c)), flat(to)))
    return pairs


FIRST = {k: shift(k, True) for k in (1, 2, 3)}
SECOND = {k: shift(k, False) for k in (1, 2, 3)}
HOPS = (2, 1, 3)


def move(value, pairs):
    return lax.ppermute(value, ALL, pairs)


def params():
    return pltpu.CompilerParams(vmem_limit_bytes=VLIM)


def mm_kernel(at, q_ref, t_ref, b_ref, o_ref):
    half = q_ref.shape[0]
    o_ref[:half] = jnp.dot(q_ref[...], b_ref[...], preferred_element_type=F32).astype(o_ref.dtype)
    o_ref[half:] = jnp.dot(t_ref[...], b_ref[...], preferred_element_type=F32).astype(o_ref.dtype)


def block_mm(q, t, basis, block, width, dtype):
    rows, depth = q.shape
    whole = pl.BlockSpec((rows, depth), lambda i, at: (0, 0))
    return pl.pallas_call(
        mm_kernel,
        grid_spec=pltpu.PrefetchScalarGridSpec(
            num_scalar_prefetch=1,
            grid=(1,),
            in_specs=[whole, whole, pl.BlockSpec((depth, width), lambda i, at: (0, at[0]))],
            out_specs=pl.BlockSpec((2 * rows, width), lambda i, at: (0, 0)),
        ),
        out_shape=jax.ShapeDtypeStruct((2 * rows, width), dtype),
        compiler_params=params(),
    )(block.reshape(1), q, t, basis)


def pick_kernel(at, *refs):
    half = len(refs) // 2
    for src, dst in zip(refs[:half], refs[half:]):
        dst[...] = src[...]


def pick_blocks(array, me, rows):
    cols = array.shape[1]
    return pl.pallas_call(
        pick_kernel,
        grid_spec=pltpu.PrefetchScalarGridSpec(
            num_scalar_prefetch=1,
            grid=(1,),
            in_specs=[
                pl.BlockSpec((rows, cols), lambda i, at, k=k: (lax.rem(at[0] + k, 4), 0)) for k in (0, *HOPS)
            ],
            out_specs=[pl.BlockSpec((rows, cols), lambda i, at: (0, 0))] * 4,
        ),
        out_shape=[jax.ShapeDtypeStruct((rows, cols), array.dtype)] * 4,
        compiler_params=params(),
    )(me.reshape(1), array, array, array, array)


def sum_kernel(at, own, a, b, c, o2, o1, o3, keep):
    i = pl.program_id(0)
    total = own[...] + a[...].astype(F32) + b[...].astype(F32) + c[...].astype(F32)
    for n, dst in enumerate((o2, o1, o3)):

        @pl.when(i == n)
        def _():
            dst[...] = total.astype(BF)

    @pl.when(i == 3)
    def _():
        keep[...] = total


def sum_blocks(own, parts, me):
    rows, cols = own.shape
    part = rows // 4

    def at_block(i, at):
        hop = jnp.where(i == 0, 2, jnp.where(i == 1, 1, jnp.where(i == 2, 3, 0)))
        return (lax.rem(at[0] + hop, 4), 0)

    fixed = pl.BlockSpec((part, cols), lambda i, at: (0, 0))
    small = jax.ShapeDtypeStruct((part, cols), BF)
    return pl.pallas_call(
        sum_kernel,
        grid_spec=pltpu.PrefetchScalarGridSpec(
            num_scalar_prefetch=1,
            grid=(4,),
            in_specs=[pl.BlockSpec((part, cols), at_block)] * 4,
            out_specs=[fixed] * 4,
        ),
        out_shape=[small, small, small, jax.ShapeDtypeStruct((part, cols), F32)],
        compiler_params=params(),
    )(me.reshape(1), own, *parts)


def score_kernel(me, pick, grid, p0, p2, p1, p3, e0, e2, e1, e3, r0, r2, r1, r3, out, rot, rot_t, ti_t):
    part = p0.shape[0]
    for k, piece in ((0, p0), (2, p2), (1, p1), (3, p3)):
        row = pl.multiple_of(lax.rem(me[0] + 4 - k, 4) * part, part)
        rot[pl.ds(row, part), :] = piece[...]
    eigs = (e0, e2, e1, e3)
    ins = (r0, r2, r1, r3)
    for n, r in enumerate(ins):
        ti_t[n] = r[256:, :].T
    for n in range(rot.shape[1] // 128):
        rot_t[n * 128 : (n + 1) * 128, :] = rot[:, n * 128 : (n + 1) * 128].T
    damp = [grid[pick[s]] for s in range(2)]

    def chunk(n, sums):
        rows = pl.ds(pl.multiple_of(n * 128, 128), 128)
        weights = [None, None]
        for k in range(4):
            diag = eigs[k][rows, :].astype(F32)
            for s in range(2):
                rotated = jnp.dot(
                    rot_t[rows, s * 128 : (s + 1) * 128],
                    ins[k][s * 128 : (s + 1) * 128, :],
                    preferred_element_type=F32,
                )
                precond = (rotated / (diag + damp[s])).astype(BF)
                w = jnp.dot(precond, ti_t[k], preferred_element_type=F32)
                weights[s] = w if weights[s] is None else weights[s] + w
        train = rot_t[rows, 256:].astype(F32)
        return tuple(
            sums[s] + jnp.sum((weights[s] * train).reshape(16, 8, 256), axis=0) for s in range(2)
        )

    zero = jnp.zeros((8, 256), F32)
    sums = lax.fori_loop(0, rot.shape[1] // 128, chunk, (zero, zero))
    both = jnp.concatenate([jnp.sum(v, axis=0, keepdims=True) for v in sums], axis=0) * SCALE
    out[...] = jnp.broadcast_to(both[None], out.shape)


def score(me, pick, grid, pieces, eigs, ins):
    tokens, cols = pieces[0].shape
    smem = pl.BlockSpec(memory_space=pltpu.SMEM)
    vmem = pl.BlockSpec(memory_space=pltpu.VMEM)
    return pl.pallas_call(
        score_kernel,
        in_specs=[smem] * 3 + [vmem] * 12,
        out_specs=vmem,
        out_shape=jax.ShapeDtypeStruct((16, 2, 256), F32),
        scratch_shapes=[
            pltpu.VMEM((4 * tokens, cols), BF),
            pltpu.VMEM((cols, 4 * tokens), BF),
            pltpu.VMEM((4, 256, 256), BF),
        ],
        compiler_params=params(),
    )(me.reshape(1), pick, grid, *pieces, *eigs, *ins)


def body(acts, out_grads, train_acts, train_grads, basis_in, basis_out, eig, grid, pick):
    y, x, c = lax.axis_index("y"), lax.axis_index("x"), lax.axis_index("c")
    first = jnp.where(c == 0, x, y).astype(jnp.int32)
    second = jnp.where(c == 0, y, x).astype(jnp.int32)
    zero = jnp.zeros((), jnp.int32)
    width = basis_out.shape[1] // 4

    got = []
    for k in HOPS:
        part = block_mm(out_grads, train_grads, basis_out, lax.rem(first + k, 4), width, BF)
        got.append(move(part, FIRST[k]))
    own = block_mm(out_grads, train_grads, basis_out, first, width, F32)
    in_part = block_mm(acts, train_acts, basis_in, zero, basis_in.shape[1], F32)

    split = lax.all_to_all(in_part, ("zl", "c"), 0, 0, tiled=True)
    rows = split.shape[0] // 8
    in_rows = jnp.sum(split.reshape(8, rows, -1), axis=0).astype(BF)
    spread = jnp.broadcast_to(in_rows[None], (8, *in_rows.shape))
    rot_in = lax.all_to_all(spread, ("zl", "c"), 0, 0, tiled=True).reshape(8 * rows, -1)

    s2, s1, s3, keep = sum_blocks(own, got, second)
    got2 = [move(v, SECOND[k]) for k, v in zip(HOPS, (s2, s1, s3))]
    eig_own, *eig_send = pick_blocks(eig, first, width)
    rot_in, *eig_send = lax.optimization_barrier((rot_in, *eig_send, s2))[:4]
    eigs = [eig_own] + [move(v, FIRST[k]) for k, v in zip(HOPS, eig_send)]
    ins = [rot_in] + [move(rot_in, FIRST[k]) for k in HOPS]
    total = keep
    for v in got2:
        total = total + v.astype(F32)
    other = lax.ppermute(total.astype(BF), "zh", [(0, 1), (1, 0)])
    total = (total + other.astype(F32)).astype(BF)
    pieces = [total] + [move(total, SECOND[k]) for k in HOPS]

    part = score(second, pick, grid, pieces, eigs, ins)
    over = jnp.sum(lax.all_to_all(part, ("y", "x"), 0, 0, tiled=True), axis=0)
    over = jnp.broadcast_to(over[None], (16, *over.shape))
    return jnp.sum(lax.all_to_all(over, ("zh", "zl", "c"), 0, 0, tiled=True), axis=0)


def solution(mesh):
    fine = Mesh(mesh.devices.reshape(SIZES), ALL)
    aa, ga = ("y", "x", "zh"), ("zl", "c")
    return jax.shard_map(
        body,
        mesh=fine,
        in_specs=(
            P(None, ga),
            P(None, aa),
            P(None, ga),
            P(None, aa),
            P(ga, aa),
            P(aa, ga),
            P(ga, aa),
            P(),
            P(),
        ),
        out_specs=P(),
        check_vma=False,
    )
```

time: 793 us -> 134 us (0.17)
  blocking collectives: 762 us -> 30.1 us
  starting transfers between devices: 0 us -> 41.3 us
  Pallas kernels: 0 us -> 33.6 us
  waiting for transfers between devices: 0 us -> 23.4 us
  matrix products: 17.9 us -> 0 us
    psum x3 -> x0, blocking collectives: 762 us -> none  [the longest x1 647 us: body(): lax.psum(lax.dot_general(basis_out, grads, (((0,), (1,)), ((), ())), pref...]
    pallas_call x0 -> x8, Pallas kernels: none -> 33.6 us  [the longest x5 18.4 us: block_mm(): pl.pallas_call(mm_kernel, grid_spec=pltpu.PrefetchScalarGridSpec(num_scal...]
    all_to_all x0 -> x2, blocking collectives: none -> 30.1 us  [the longest x1 19.6 us: body(): lax.all_to_all(over, ('zh', 'zl', 'c'), 0, 0, tiled=True)]
    ppermute x0 -> x16, starting transfers between devices: none -> 27.4 us  [the longest x15 22.9 us: move(): return lax.ppermute(value, ALL, pairs)]
    dot_general x3 -> x0, matrix products: 17.9 us -> none  [the longest x1 10.1 us: body(): lax.dot_general(basis_out, grads, (((0,), (1,)), ((), ())), preferred_ele...]
    ppermute x0 -> x16, waiting for transfers between devices: none -> 17.5 us  [the longest x15 17.5 us: move(): return lax.ppermute(value, ALL, pairs)]
    all_to_all x0 -> x2, starting transfers between devices: none -> 14 us  [the longest x1 7.24 us: body(): split = lax.all_to_all(in_part, ('zl', 'c'), 0, 0, tiled=True)]
  transfers between devices with their start and end apart: 0 -> 18, of which waited for: 0 -> 6; matrix products, arithmetic and copies ran while one was open for 0% -> 1% of each run, Pallas kernels for 0% -> 16%
where the time goes in v1:
time: 134 us
  starting transfers between devices  41.3 us (31%)
  Pallas kernels  33.6 us (25%)
  blocking collectives  30.1 us (22%)
  waiting for transfers between devices  23.4 us (17%)
  local copies, waits for them, and re-layouts  3.33 us (2%)
  other arithmetic  1.92 us (1%)
    ppermute x15, starting transfers between devices, move(): return lax.ppermute(value, ALL, pairs)  22.9 us
    all_to_all x1, blocking collectives, body(): lax.all_to_all(over, ('zh', 'zl', 'c'), 0, 0, tiled=True)  19.6 us
    pallas_call x5, Pallas kernels, block_mm(): pl.pallas_call(mm_kernel, grid_spec=pltpu.PrefetchScalarGridSpec(num_scal...  18.4 us
    ppermute x15, waiting for transfers between devices, move(): return lax.ppermute(value, ALL, pairs)  17.5 us
    all_to_all x1, blocking collectives, body(): over = jnp.sum(lax.all_to_all(part, ('y', 'x'), 0, 0, tiled=True), axis=0)  10.5 us
    pallas_call x1, Pallas kernels, score(): pl.pallas_call(score_kernel, in_specs=[smem] * 3 + [vmem] * 12, out_specs...  8.12 us
    all_to_all x1, starting transfers between devices, body(): split = lax.all_to_all(in_part, ('zl', 'c'), 0, 0, tiled=True)  7.24 us
    all_to_all x1, starting transfers between devices, body(): lax.all_to_all(spread, ('zl', 'c'), 0, 0, tiled=True).reshape(8 * rows, -1)  6.71 us
  transfers between devices with their start and end apart: 18, of which 6 were waited for; matrix products, arithmetic and copies ran while one was open for 1% of the time, Pallas kernels for 16%

profile of v1, /device:TPU:1, one launch (start us, length us, event | category | flops | bytes accessed | tf_op | source)
XLA Modules:
  0.0 133.8 jit_solution(7320263370653901579)
XLA Ops:
  0.0 3.9 %shard_map.92 = bf16[512,896]{1,0:T(8,128)(2,1)} custom-call(s32[1]{0:T(128)} %bitcast.2.at, bf16[256,896]{1,0:T(8,128)(2,1)} %q_ref.8, bf16[256,896]{1,0:T(8,128)(2,1)} %t_ref.8, bf16[896,3584]{1,0:T(8,128)(2,1)} %b_ref.8), custom_call_target="tpu_custom_call" | custom-call | tf_op jit(solution)/shard_map/pallas_call | solution.py:62
  3.9 3.7 %collective-permute-start = (bf16[512,896]{1,0:T(8,128)(2,1)}, bf16[512,896]{1,0:T(8,128)(2,1)S(1)}, u32[]{:S(2)}, u32[]{:S(2)}) collective-permute-start(bf16[512,896]{1,0:T(8,128)(2,1)} %shard_map.92), channel_id=1, source_target_pairs={{0,32},{1,129},{2,34},{3,131},{4,36},{5,133},{6,38},{7,135},{8,40}... | collective-permute-start | bytes 2752520 | tf_op jit(solution)/shard_map/ppermute | solution.py:46
  7.6 3.9 %shard_map.93 = bf16[512,896]{1,0:T(8,128)(2,1)} custom-call(s32[1]{0:T(128)} %bitcast.3.at, bf16[256,896]{1,0:T(8,128)(2,1)} %q_ref.8, bf16[256,896]{1,0:T(8,128)(2,1)} %t_ref.8, bf16[896,3584]{1,0:T(8,128)(2,1)} %b_ref.8), custom_call_target="tpu_custom_call" | custom-call | tf_op jit(solution)/shard_map/pallas_call | solution.py:62
  11.9 3.9 %shard_map.94 = bf16[512,896]{1,0:T(8,128)(2,1)} custom-call(s32[1]{0:T(128)} %bitcast.4.at, bf16[256,896]{1,0:T(8,128)(2,1)} %q_ref.8, bf16[256,896]{1,0:T(8,128)(2,1)} %t_ref.8, bf16[896,3584]{1,0:T(8,128)(2,1)} %b_ref.8), custom_call_target="tpu_custom_call" | custom-call | tf_op jit(solution)/shard_map/pallas_call | solution.py:62
  15.7 2.3 %collective-permute-start.2 = (bf16[512,896]{1,0:T(8,128)(2,1)}, bf16[512,896]{1,0:T(8,128)(2,1)S(1)}, u32[]{:S(2)}, u32[]{:S(2)}) collective-permute-start(bf16[512,896]{1,0:T(8,128)(2,1)} %shard_map.94), channel_id=1, source_target_pairs={{0,48},{1,193},{2,50},{3,195},{4,52},{5,197},{6,54},{7,199},{8,56}... | collective-permute-start | bytes 2752520 | tf_op jit(solution)/shard_map/ppermute | solution.py:46
  18.0 2.6 %shard_map.97 = f32[512,256]{1,0:T(8,128)} custom-call(s32[1]{0:T(128)} %constant.31.clone.1.at, bf16[256,1024]{1,0:T(8,128)(2,1)} %q_ref.9, bf16[256,1024]{1,0:T(8,128)(2,1)} %t_ref.9, bf16[1024,256]{1,0:T(8,128)(2,1)} %b_ref.9), custom_call_target="tpu_custom_call" | custom-call | tf_op jit(solution)/shard_map/pallas_call | solution.py:62
  20.6 7.2 %all-to-all-start = ((f32[8,64,256]{2,1,0:T(8,128)}), f32[8,64,256]{2,1,0:T(8,128)S(1)}, u32[]{:S(2)}, u32[]{:S(2)}) async-start(f32[8,64,256]{2,1,0:T(8,128)} %bitcast.7), calls=%async_computation | async-start | bytes 1048576 | tf_op jit(solution)/shard_map/all_to_all | solution.py:205
  27.8 4.2 %shard_map.91.own = f32[512,896]{1,0:T(8,128)} custom-call(s32[1]{0:T(128)} %bitcast.1.at, bf16[256,896]{1,0:T(8,128)(2,1)} %q_ref.8, bf16[256,896]{1,0:T(8,128)(2,1)} %t_ref.8, bf16[896,3584]{1,0:T(8,128)(2,1)} %b_ref.8), custom_call_target="tpu_custom_call" | custom-call | tf_op jit(solution)/shard_map/pallas_call | solution.py:62
  32.1 0.9 copy-done.2
  33.6 4.4 %shard_map.95 = (bf16[128,896]{1,0:T(8,128)(2,1)}, bf16[128,896]{1,0:T(8,128)(2,1)}, bf16[128,896]{1,0:T(8,128)(2,1)}, f32[128,896]{1,0:T(8,128)}) custom-call(s32[1]{0:T(128)} %bitcast.at.me, f32[512,896]{1,0:T(8,128)} %shard_map.91.own, bf16[512,896]{1,0:T(8,128)(2,1)} %copy-done.2, bf16[512,896]{1,0:T(8,128)(2,1)} %copy-done.3, bf16[512,896]{1,0:T(8,128)(2,1)} %copy-done.4), custom_call_target="tpu_custom_call" | custom-call | tf_op jit(solution)/shard_map/pallas_call | solution.py:122
  37.9 1.5 %collective-permute-start.3 = (bf16[128,896]{1,0:T(8,128)(2,1)}, bf16[128,896]{1,0:T(8,128)(2,1)S(1)}, u32[]{:S(2)}, u32[]{:S(2)}) collective-permute-start(bf16[128,896]{1,0:T(8,128)(2,1)} %get-tuple-element.18), channel_id=1, source_target_pairs={{0,128},{1,33},{2,130},{3,35},{4,132},{5,37},{6,134},{7,39},{8,136... | collective-permute-start | bytes 688136 | tf_op jit(solution)/shard_map/ppermute | solution.py:46
  39.8 2.4 %collective-permute-start.5 = (bf16[128,896]{1,0:T(8,128)(2,1)}, bf16[128,896]{1,0:T(8,128)(2,1)S(1)}, u32[]{:S(2)}, u32[]{:S(2)}) collective-permute-start(bf16[128,896]{1,0:T(8,128)(2,1)} %get-tuple-element.20), channel_id=1, source_target_pairs={{0,192},{1,49},{2,194},{3,51},{4,196},{5,53},{6,198},{7,55},{8,200... | collective-permute-start | bytes 688136 | tf_op jit(solution)/shard_map/ppermute | solution.py:46
  42.1 2.7 %collective-permute-done.3 = bf16[128,896]{1,0:T(8,128)(2,1)S(1)} collective-permute-done((bf16[128,896]{1,0:T(8,128)(2,1)}, bf16[128,896]{1,0:T(8,128)(2,1)S(1)}, u32[]{:S(2)}, u32[]{:S(2)}) %collective-permute-start.3) | collective-permute-done | bytes 229408 | tf_op jit(solution)/shard_map/ppermute | solution.py:46
  44.8 2.5 %collective-permute-done.4 = bf16[128,896]{1,0:T(8,128)(2,1)S(1)} collective-permute-done((bf16[128,896]{1,0:T(8,128)(2,1)}, bf16[128,896]{1,0:T(8,128)(2,1)S(1)}, u32[]{:S(2)}, u32[]{:S(2)}) %collective-permute-start.4) | collective-permute-done | bytes 229408 | tf_op jit(solution)/shard_map/ppermute | solution.py:46
  47.3 1.1 fusion
  48.4 4.5 %collective-permute-start.6 = (bf16[128,896]{1,0:T(8,128)(2,1)S(1)}, bf16[128,896]{1,0:T(8,128)(2,1)S(1)}, u32[]{:S(2)}, u32[]{:S(2)}) collective-permute-start(bf16[128,896]{1,0:T(8,128)(2,1)S(1)} %fusion), channel_id=1, source_target_pairs={{0,8},{8,0},{1,9},{9,1},{2,10},{10,2},{3,11},{11,3},{4,12},{12,4},... | collective-permute-start | bytes 688136 | tf_op jit(solution)/shard_map/ppermute | solution.py:220
  53.6 6.7 %all-to-all-start.1 = ((bf16[8,64,256]{2,1,0:T(8,128)(2,1)}), bf16[8,64,256]{2,1,0:T(8,128)(2,1)S(1)}, u32[]{:S(2)}, u32[]{:S(2)}) async-start(bf16[8,64,256]{2,1,0:T(8,128)(2,1)} %broadcast_in_dim.4), calls=%async_computation.1 | async-start | bytes 524288 | tf_op jit(solution)/shard_map/all_to_all | solution.py:209
  60.5 1.5 %collective-permute-start.7 = (bf16[128,896]{1,0:T(8,128)(2,1)S(1)}, bf16[128,896]{1,0:T(8,128)(2,1)S(1)}, u32[]{:S(2)}, u32[]{:S(2)}) collective-permute-start(bf16[128,896]{1,0:T(8,128)(2,1)S(1)} %add_convert_fusion.p0), channel_id=1, source_target_pairs={{0,128},{1,33},{2,130},{3,35},{4,132},{5,37},{6,134},{7,39},{8,136... | collective-permute-start | bytes 688136 | tf_op jit(solution)/shard_map/ppermute | solution.py:46
  62.0 1.1 collective-permute-start.8
  63.1 2.7 %shard_map.96 = (bf16[896,256]{1,0:T(8,128)(2,1)}, bf16[896,256]{1,0:T(8,128)(2,1)}, bf16[896,256]{1,0:T(8,128)(2,1)}, bf16[896,256]{1,0:T(8,128)(2,1)}) custom-call(s32[1]{0:T(128)} %bitcast.1.at, bf16[3584,256]{1,0:T(8,128)(2,1)} %refs_3_.1, bf16[3584,256]{1,0:T(8,128)(2,1)} %refs_3_.1, bf16[3584,256]{1,0:T(8,128)(2,1)} %refs_3_.1, bf16[3584,256]{1,0:T(8,128)(2,1)} %refs_3_.1), custom_call_target="tpu_custom_call" | custom-call | tf_op jit(solution)/shard_map/pallas_call | solution.py:83
  65.8 5.9 %all-to-all-done.1 = bf16[8,64,256]{2,1,0:T(8,128)(2,1)S(1)} async-done(((bf16[8,64,256]{2,1,0:T(8,128)(2,1)}), bf16[8,64,256]{2,1,0:T(8,128)(2,1)S(1)}, u32[]{:S(2)}, u32[]{:S(2)}) %all-to-all-start.1) | async-done | bytes 262176 | tf_op jit(solution)/shard_map/all_to_all | solution.py:209
  71.7 2.4 %collective-permute-start.13 = (bf16[512,256]{1,0:T(8,128)(2,1)S(1)}, bf16[512,256]{1,0:T(8,128)(2,1)S(1)}, u32[]{:S(2)}, u32[]{:S(2)}) collective-permute-start(bf16[512,256]{1,0:T(8,128)(2,1)S(1)} %bitcast.8), channel_id=1, source_target_pairs={{0,32},{1,129},{2,34},{3,131},{4,36},{5,133},{6,38},{7,135},{8,40}... | collective-permute-start | bytes 786440 | tf_op jit(solution)/shard_map/ppermute | solution.py:46
  74.1 0.8 collective-permute-start.9
  74.9 1.1 collective-permute-start.10
  76.2 2.5 %collective-permute-start.12 = (bf16[896,256]{1,0:T(8,128)(2,1)}, bf16[896,256]{1,0:T(8,128)(2,1)S(1)}, u32[]{:S(2)}, u32[]{:S(2)}) collective-permute-start(bf16[896,256]{1,0:T(8,128)(2,1)} %get-tuple-element.27), channel_id=1, source_target_pairs={{0,48},{1,193},{2,50},{3,195},{4,52},{5,197},{6,54},{7,199},{8,56}... | collective-permute-start | bytes 1376264 | tf_op jit(solution)/shard_map/ppermute | solution.py:46
  78.7 3.0 %collective-permute-done.9.p3 = bf16[128,896]{1,0:T(8,128)(2,1)S(1)} collective-permute-done((bf16[128,896]{1,0:T(8,128)(2,1)S(1)}, bf16[128,896]{1,0:T(8,128)(2,1)S(1)}, u32[]{:S(2)}, u32[]{:S(2)}) %collective-permute-start.9) | collective-permute-done | bytes 229408 | tf_op jit(solution)/shard_map/ppermute | solution.py:46
  82.5 1.9 %collective-permute-start.15 = (bf16[512,256]{1,0:T(8,128)(2,1)S(1)}, bf16[512,256]{1,0:T(8,128)(2,1)S(1)}, u32[]{:S(2)}, u32[]{:S(2)}) collective-permute-start(bf16[512,256]{1,0:T(8,128)(2,1)S(1)} %bitcast.10), channel_id=1, source_target_pairs={{0,48},{1,193},{2,50},{3,195},{4,52},{5,197},{6,54},{7,199},{8,56}... | collective-permute-start | bytes 786440 | tf_op jit(solution)/shard_map/ppermute | solution.py:46
  84.4 7.6 %collective-permute-done.14.r1 = bf16[512,256]{1,0:T(8,128)(2,1)S(1)} collective-permute-done((bf16[512,256]{1,0:T(8,128)(2,1)S(1)}, bf16[512,256]{1,0:T(8,128)(2,1)S(1)}, u32[]{:S(2)}, u32[]{:S(2)}) %collective-permute-start.14) | collective-permute-done | bytes 262176 | tf_op jit(solution)/shard_map/ppermute | solution.py:46
  91.9 1.7 %collective-permute-done.15.r3 = bf16[512,256]{1,0:T(8,128)(2,1)S(1)} collective-permute-done((bf16[512,256]{1,0:T(8,128)(2,1)S(1)}, bf16[512,256]{1,0:T(8,128)(2,1)S(1)}, u32[]{:S(2)}, u32[]{:S(2)}) %collective-permute-start.15) | collective-permute-done | bytes 262176 | tf_op jit(solution)/shard_map/ppermute | solution.py:46
  94.9 8.1 %shard_map.98 = f32[16,2,256]{2,1,0:T(2,128)} custom-call(s32[1]{0:T(128)} %bitcast.at.me, s32[2]{0:T(128)} %pick.1, f32[16]{0:T(128)} %grid.1, bf16[128,896]{1,0:T(8,128)(2,1)} %copy-done.5, bf16[128,896]{1,0:T(8,128)(2,1)} %copy-done.12, bf16[128,896]{1,0:T(8,128)(2,1)} %copy-done.13, bf16[128,896]{1,0:T(8,128)(2,1)} %copy-done.14, ...), custom_call_target="tpu_custom_call" | custom-call | tf_op jit(solution)/shard_map/pallas_call | solution.py:177
  103.0 10.5 %all_to_all.24 = f32[16,2,256]{2,1,0:T(2,128)S(1)} all-to-all(f32[16,2,256]{2,1,0:T(2,128)} %shard_map.98), channel_id=1, replica_groups=mesh['y'=4,'x'=4,'zh'=2,'zl'=4,'c'=2] {'y','x'}, dimensions={0} | all-to-all | bytes 65536 | tf_op jit(solution)/shard_map/all_to_all | solution.py:225
  113.6 19.6 %all_to_all.25 = f32[16,2,256]{2,1,0:T(2,128)S(1)} all-to-all(f32[16,2,256]{2,1,0:T(2,128)S(1)} %broadcast_in_dim.5), channel_id=1, replica_groups=mesh['y'=4,'x'=4,'zh'=2,'zl'=4,'c'=2] {'zh','zl','c'}, dimensions={0} | all-to-all | bytes 65536 | tf_op jit(solution)/shard_map/all_to_all | solution.py:227
  (51 shorter events, 4.9 us)
Async XLA Ops:
  3.9 28.2 %collective-permute-start = (bf16[512,896]{1,0:T(8,128)(2,1)}, bf16[512,896]{1,0:T(8,128)(2,1)S(1)}, u32[]{:S(2)}, u32[]{:S(2)}) collective-permute-start(bf16[512,896]{1,0:T(8,128)(2,1)} %shard_map.92), channel_id=1, source_target_pairs={{0,32},{1,129},{2,34},{3,131},{4,36},{5,133},{6,38},{7,135},{8,40}... | collective-permute-start | bytes 2752520 | tf_op jit(solution)/shard_map/ppermute | solution.py:46
  11.5 20.6 %collective-permute-start.1 = (bf16[512,896]{1,0:T(8,128)(2,1)}, bf16[512,896]{1,0:T(8,128)(2,1)S(1)}, u32[]{:S(2)}, u32[]{:S(2)}) collective-permute-start(bf16[512,896]{1,0:T(8,128)(2,1)} %shard_map.93), channel_id=1, source_target_pairs={{0,16},{1,65},{2,18},{3,67},{4,20},{5,69},{6,22},{7,71},{8,24},{9,... | collective-permute-start | bytes 2752520 | tf_op jit(solution)/shard_map/ppermute | solution.py:46
  15.7 16.3 %collective-permute-start.2 = (bf16[512,896]{1,0:T(8,128)(2,1)}, bf16[512,896]{1,0:T(8,128)(2,1)S(1)}, u32[]{:S(2)}, u32[]{:S(2)}) collective-permute-start(bf16[512,896]{1,0:T(8,128)(2,1)} %shard_map.94), channel_id=1, source_target_pairs={{0,48},{1,193},{2,50},{3,195},{4,52},{5,197},{6,54},{7,199},{8,56}... | collective-permute-start | bytes 2752520 | tf_op jit(solution)/shard_map/ppermute | solution.py:46
  20.6 32.3 %all-to-all-start = ((f32[8,64,256]{2,1,0:T(8,128)}), f32[8,64,256]{2,1,0:T(8,128)S(1)}, u32[]{:S(2)}, u32[]{:S(2)}) async-start(f32[8,64,256]{2,1,0:T(8,128)} %bitcast.7), calls=%async_computation | async-start | bytes 1048576 | tf_op jit(solution)/shard_map/all_to_all | solution.py:205
  32.0 0.9 copy-start.2
  32.0 1.2 copy-start.3
  32.1 1.5 %copy-start.4 = (bf16[512,896]{1,0:T(8,128)(2,1)}, bf16[512,896]{1,0:T(8,128)(2,1)S(1)}, u32[]{:S(2)}) copy-start(bf16[512,896]{1,0:T(8,128)(2,1)S(1)} %collective-permute-done.2.c) | copy-start | bytes 2752516
  37.9 22.4 %copy-start = (f32[128,896]{1,0:T(8,128)S(1)}, f32[128,896]{1,0:T(8,128)}, u32[]{:S(2)}) copy-start(f32[128,896]{1,0:T(8,128)} %get-tuple-element.17) | copy-start | bytes 1376260
  37.9 6.9 %collective-permute-start.3 = (bf16[128,896]{1,0:T(8,128)(2,1)}, bf16[128,896]{1,0:T(8,128)(2,1)S(1)}, u32[]{:S(2)}, u32[]{:S(2)}) collective-permute-start(bf16[128,896]{1,0:T(8,128)(2,1)} %get-tuple-element.18), channel_id=1, source_target_pairs={{0,128},{1,33},{2,130},{3,35},{4,132},{5,37},{6,134},{7,39},{8,136... | collective-permute-start | bytes 688136 | tf_op jit(solution)/shard_map/ppermute | solution.py:46
  39.4 7.8 %collective-permute-start.4 = (bf16[128,896]{1,0:T(8,128)(2,1)}, bf16[128,896]{1,0:T(8,128)(2,1)S(1)}, u32[]{:S(2)}, u32[]{:S(2)}) collective-permute-start(bf16[128,896]{1,0:T(8,128)(2,1)} %get-tuple-element.19), channel_id=1, source_target_pairs={{0,64},{1,17},{2,66},{3,19},{4,68},{5,21},{6,70},{7,23},{8,72},{9,... | collective-permute-start | bytes 688136 | tf_op jit(solution)/shard_map/ppermute | solution.py:46
  39.8 7.5 %collective-permute-start.5 = (bf16[128,896]{1,0:T(8,128)(2,1)}, bf16[128,896]{1,0:T(8,128)(2,1)S(1)}, u32[]{:S(2)}, u32[]{:S(2)}) collective-permute-start(bf16[128,896]{1,0:T(8,128)(2,1)} %get-tuple-element.20), channel_id=1, source_target_pairs={{0,192},{1,49},{2,194},{3,51},{4,196},{5,53},{6,198},{7,55},{8,200... | collective-permute-start | bytes 688136 | tf_op jit(solution)/shard_map/ppermute | solution.py:46
  48.4 11.9 %collective-permute-start.6 = (bf16[128,896]{1,0:T(8,128)(2,1)S(1)}, bf16[128,896]{1,0:T(8,128)(2,1)S(1)}, u32[]{:S(2)}, u32[]{:S(2)}) collective-permute-start(bf16[128,896]{1,0:T(8,128)(2,1)S(1)} %fusion), channel_id=1, source_target_pairs={{0,8},{8,0},{1,9},{9,1},{2,10},{10,2},{3,11},{11,3},{4,12},{12,4},... | collective-permute-start | bytes 688136 | tf_op jit(solution)/shard_map/ppermute | solution.py:220
  53.6 18.1 %all-to-all-start.1 = ((bf16[8,64,256]{2,1,0:T(8,128)(2,1)}), bf16[8,64,256]{2,1,0:T(8,128)(2,1)S(1)}, u32[]{:S(2)}, u32[]{:S(2)}) async-start(bf16[8,64,256]{2,1,0:T(8,128)(2,1)} %broadcast_in_dim.4), calls=%async_computation.1 | async-start | bytes 524288 | tf_op jit(solution)/shard_map/all_to_all | solution.py:209
  60.5 13.6 %copy-start.5 = (bf16[128,896]{1,0:T(8,128)(2,1)}, bf16[128,896]{1,0:T(8,128)(2,1)S(1)}, u32[]{:S(2)}) copy-start(bf16[128,896]{1,0:T(8,128)(2,1)S(1)} %add_convert_fusion.p0) | copy-start | bytes 688132
  60.5 15.5 %collective-permute-start.7 = (bf16[128,896]{1,0:T(8,128)(2,1)S(1)}, bf16[128,896]{1,0:T(8,128)(2,1)S(1)}, u32[]{:S(2)}, u32[]{:S(2)}) collective-permute-start(bf16[128,896]{1,0:T(8,128)(2,1)S(1)} %add_convert_fusion.p0), channel_id=1, source_target_pairs={{0,128},{1,33},{2,130},{3,35},{4,132},{5,37},{6,134},{7,39},{8,136... | collective-permute-start | bytes 688136 | tf_op jit(solution)/shard_map/ppermute | solution.py:46
  62.0 14.2 %collective-permute-start.8 = (bf16[128,896]{1,0:T(8,128)(2,1)S(1)}, bf16[128,896]{1,0:T(8,128)(2,1)S(1)}, u32[]{:S(2)}, u32[]{:S(2)}) collective-permute-start(bf16[128,896]{1,0:T(8,128)(2,1)S(1)} %add_convert_fusion.p0), channel_id=1, source_target_pairs={{0,64},{1,17},{2,66},{3,19},{4,68},{5,21},{6,70},{7,23},{8,72},{9,... | collective-permute-start | bytes 688136 | tf_op jit(solution)/shard_map/ppermute | solution.py:46
  71.7 22.0 %copy-start.1 = (bf16[8,64,256]{2,1,0:T(8,128)(2,1)}, bf16[8,64,256]{2,1,0:T(8,128)(2,1)S(1)}, u32[]{:S(2)}) copy-start(bf16[8,64,256]{2,1,0:T(8,128)(2,1)S(1)} %all-to-all-done.1) | copy-start | bytes 786436
  71.7 10.8 %collective-permute-start.13 = (bf16[512,256]{1,0:T(8,128)(2,1)S(1)}, bf16[512,256]{1,0:T(8,128)(2,1)S(1)}, u32[]{:S(2)}, u32[]{:S(2)}) collective-permute-start(bf16[512,256]{1,0:T(8,128)(2,1)S(1)} %bitcast.8), channel_id=1, source_target_pairs={{0,32},{1,129},{2,34},{3,131},{4,36},{5,133},{6,38},{7,135},{8,40}... | collective-permute-start | bytes 786440 | tf_op jit(solution)/shard_map/ppermute | solution.py:46
  74.1 7.6 %collective-permute-start.9 = (bf16[128,896]{1,0:T(8,128)(2,1)S(1)}, bf16[128,896]{1,0:T(8,128)(2,1)S(1)}, u32[]{:S(2)}, u32[]{:S(2)}) collective-permute-start(bf16[128,896]{1,0:T(8,128)(2,1)S(1)} %add_convert_fusion.p0), channel_id=1, source_target_pairs={{0,192},{1,49},{2,194},{3,51},{4,196},{5,53},{6,198},{7,55},{8,200... | collective-permute-start | bytes 688136 | tf_op jit(solution)/shard_map/ppermute | solution.py:46
  74.9 18.8 %collective-permute-start.10 = (bf16[896,256]{1,0:T(8,128)(2,1)}, bf16[896,256]{1,0:T(8,128)(2,1)S(1)}, u32[]{:S(2)}, u32[]{:S(2)}) collective-permute-start(bf16[896,256]{1,0:T(8,128)(2,1)} %get-tuple-element.25), channel_id=1, source_target_pairs={{0,32},{1,129},{2,34},{3,131},{4,36},{5,133},{6,38},{7,135},{8,40}... | collective-permute-start | bytes 1376264 | tf_op jit(solution)/shard_map/ppermute | solution.py:46
  76.0 17.7 %copy-start.12 = (bf16[128,896]{1,0:T(8,128)(2,1)}, bf16[128,896]{1,0:T(8,128)(2,1)S(1)}, u32[]{:S(2)}) copy-start(bf16[128,896]{1,0:T(8,128)(2,1)S(1)} %collective-permute-done.7.p2) | copy-start | bytes 688132
  76.0 17.7 %collective-permute-start.11 = (bf16[896,256]{1,0:T(8,128)(2,1)}, bf16[896,256]{1,0:T(8,128)(2,1)S(1)}, u32[]{:S(2)}, u32[]{:S(2)}) collective-permute-start(bf16[896,256]{1,0:T(8,128)(2,1)} %get-tuple-element.26), channel_id=1, source_target_pairs={{0,16},{1,65},{2,18},{3,67},{4,20},{5,69},{6,22},{7,71},{8,24},{9,... | collective-permute-start | bytes 1376264 | tf_op jit(solution)/shard_map/ppermute | solution.py:46
  76.2 17.6 %copy-start.13 = (bf16[128,896]{1,0:T(8,128)(2,1)}, bf16[128,896]{1,0:T(8,128)(2,1)S(1)}, u32[]{:S(2)}) copy-start(bf16[128,896]{1,0:T(8,128)(2,1)S(1)} %collective-permute-done.8.p1) | copy-start | bytes 688132
  76.2 17.5 %collective-permute-start.12 = (bf16[896,256]{1,0:T(8,128)(2,1)}, bf16[896,256]{1,0:T(8,128)(2,1)S(1)}, u32[]{:S(2)}, u32[]{:S(2)}) collective-permute-start(bf16[896,256]{1,0:T(8,128)(2,1)} %get-tuple-element.27), channel_id=1, source_target_pairs={{0,48},{1,193},{2,50},{3,195},{4,52},{5,197},{6,54},{7,199},{8,56}... | collective-permute-start | bytes 1376264 | tf_op jit(solution)/shard_map/ppermute | solution.py:46
  81.7 12.1 %copy-start.14 = (bf16[128,896]{1,0:T(8,128)(2,1)}, bf16[128,896]{1,0:T(8,128)(2,1)S(1)}, u32[]{:S(2)}) copy-start(bf16[128,896]{1,0:T(8,128)(2,1)S(1)} %collective-permute-done.9.p3) | copy-start | bytes 688132
  81.7 10.3 %collective-permute-start.14 = (bf16[512,256]{1,0:T(8,128)(2,1)S(1)}, bf16[512,256]{1,0:T(8,128)(2,1)S(1)}, u32[]{:S(2)}, u32[]{:S(2)}) collective-permute-start(bf16[512,256]{1,0:T(8,128)(2,1)S(1)} %bitcast.9), channel_id=1, source_target_pairs={{0,16},{1,65},{2,18},{3,67},{4,20},{5,69},{6,22},{7,71},{8,24},{9,... | collective-permute-start | bytes 786440 | tf_op jit(solution)/shard_map/ppermute | solution.py:46
  82.5 11.3 %copy-start.9 = (bf16[512,256]{1,0:T(8,128)(2,1)}, bf16[512,256]{1,0:T(8,128)(2,1)S(1)}, u32[]{:S(2)}) copy-start(bf16[512,256]{1,0:T(8,128)(2,1)S(1)} %collective-permute-done.13.r2) | copy-start | bytes 786436
  82.5 11.2 %collective-permute-start.15 = (bf16[512,256]{1,0:T(8,128)(2,1)S(1)}, bf16[512,256]{1,0:T(8,128)(2,1)S(1)}, u32[]{:S(2)}, u32[]{:S(2)}) collective-permute-start(bf16[512,256]{1,0:T(8,128)(2,1)S(1)} %bitcast.10), channel_id=1, source_target_pairs={{0,48},{1,193},{2,50},{3,195},{4,52},{5,197},{6,54},{7,199},{8,56}... | collective-permute-start | bytes 786440 | tf_op jit(solution)/shard_map/ppermute | solution.py:46
  91.9 1.8 %copy-start.10 = (bf16[512,256]{1,0:T(8,128)(2,1)}, bf16[512,256]{1,0:T(8,128)(2,1)S(1)}, u32[]{:S(2)}) copy-start(bf16[512,256]{1,0:T(8,128)(2,1)S(1)} %collective-permute-done.14.r1) | copy-start | bytes 786436
  93.7 0.9 copy-start.6
  93.7 1.0 copy-start.7
  93.7 1.2 copy-start.8
  (1 other events, 0.7 us)

commit v2 on v1

v2 whole, which is shorter than its diff:
```python
import functools
import itertools
import math

import jax
import jax.numpy as jnp
from jax import lax
from jax.experimental import pallas as pl
from jax.experimental.pallas import tpu as pltpu
from jax.sharding import Mesh, PartitionSpec as P

D_IN = 8192
D_OUT = 28672
SIZES = (4, 4, 2, 4, 2)
ALL = ("y", "x", "zh", "zl", "c")
SCALE = 1.0 / math.sqrt(D_IN * D_OUT)
BF = jnp.bfloat16
F32 = jnp.float32
MIB = 1024 * 1024


def flat(place):
    n = 0
    for size, at in zip(SIZES, place):
        n = n * size + at
    return n


def shift(k, first):
    pairs = []
    for y, x, zh, zl, c in itertools.product(*(range(s) for s in SIZES)):
        if (c == 0) == first:
            to = (y, (x + k) % 4, zh, zl, c)
        else:
            to = ((y + k) % 4, x, zh, zl, c)
        pairs.append((flat((y, x, zh, zl, c)), flat(to)))
    return pairs


FIRST = {k: shift(k, True) for k in (1, 2, 3)}
SECOND = {k: shift(k, False) for k in (1, 2, 3)}
HOPS = (2, 1, 3)


def move(value, pairs):
    return lax.ppermute(value, ALL, pairs)


def params(mib, us):
    return {
        "compiler_params": pltpu.CompilerParams(vmem_limit_bytes=mib * MIB),
        "cost_estimate": pl.CostEstimate(flops=int(us * 1.15e9), bytes_accessed=0, transcendentals=0),
    }


SMEM = pl.BlockSpec(memory_space=pltpu.SMEM)
VMEM = pl.BlockSpec(memory_space=pltpu.VMEM)


def lead_kernel(hops, at, q_hbm, t_hbm, b_hbm, *refs):
    outs, (q, t, b, sems) = refs[: 2 * len(hops)], refs[2 * len(hops) :]
    width = outs[0].shape[1]
    loads = [pltpu.make_async_copy(q_hbm, q, sems.at[0]), pltpu.make_async_copy(t_hbm, t, sems.at[1])]
    for n, k in enumerate(hops):
        cols = pl.ds(pl.multiple_of(lax.rem(at[0] + k, 4) * width, width), width)
        loads.append(pltpu.make_async_copy(b_hbm.at[:, cols], b.at[n], sems.at[2 + n]))
    for n in (0, 2, 1, *range(3, len(loads))):
        loads[n].start()
    for n in range(len(hops)):
        loads[2 + n].wait()
        for m, rows in enumerate((q, t)):
            if n == 0:
                loads[m].wait()
            dst = outs[2 * n + m]
            dst[...] = jnp.dot(rows[...], b[n], preferred_element_type=F32).astype(dst.dtype)


def lead_mm(q, t, basis, me, hops, width):
    rows, depth = q.shape
    hbm = pl.BlockSpec(memory_space=pltpu.HBM)
    return pl.pallas_call(
        functools.partial(lead_kernel, hops),
        in_specs=[SMEM, hbm, hbm, hbm],
        out_specs=[VMEM] * (2 * len(hops)),
        out_shape=[jax.ShapeDtypeStruct((rows, width), BF)] * (2 * len(hops)),
        scratch_shapes=[
            pltpu.VMEM((rows, depth), BF),
            pltpu.VMEM((rows, depth), BF),
            pltpu.VMEM((len(hops), depth, width), BF),
            pltpu.SemaphoreType.DMA((2 + len(hops),)),
        ],
        **params(58, 5),
    )(me.reshape(1), q, t, basis)


def open_kernel(at, core_at, q_hbm, t_hbm, b_hbm, aq_hbm, at_hbm, bi_hbm, oq, ot, mine, other, q, t, b, aq, ta, bi, sems):
    width = oq.shape[1]
    cols = pl.ds(pl.multiple_of(lax.rem(at[0] + 2, 4) * width, width), width)
    pairs = ((aq_hbm, aq), (at_hbm, ta), (bi_hbm, bi), (q_hbm, q), (b_hbm.at[:, cols], b), (t_hbm, t))
    loads = [pltpu.make_async_copy(src, dst, sems.at[n]) for n, (src, dst) in enumerate(pairs)]
    for load in loads:
        load.start()
    for load in loads[:3]:
        load.wait()
    for core in range(2):

        @pl.when(core_at[0] == core)
        def _():
            mine[...] = jnp.dot((aq, ta)[core][...], bi[...], preferred_element_type=F32)
            other[...] = jnp.dot((ta, aq)[core][...], bi[...], preferred_element_type=F32)

    loads[3].wait()
    loads[4].wait()
    oq[...] = jnp.dot(q[...], b[...], preferred_element_type=F32).astype(oq.dtype)
    loads[5].wait()
    ot[...] = jnp.dot(t[...], b[...], preferred_element_type=F32).astype(ot.dtype)


def open_mm(first, core, grads, basis_out, acts, basis_in, width):
    (rows, depth), (in_depth, in_width) = grads[0].shape, basis_in.shape
    hbm = pl.BlockSpec(memory_space=pltpu.HBM)
    return pl.pallas_call(
        open_kernel,
        in_specs=[SMEM] * 2 + [hbm] * 6,
        out_specs=[VMEM] * 4,
        out_shape=[jax.ShapeDtypeStruct((rows, width), BF)] * 2 + [jax.ShapeDtypeStruct((rows, in_width), F32)] * 2,
        scratch_shapes=[
            pltpu.VMEM((rows, depth), BF),
            pltpu.VMEM((rows, depth), BF),
            pltpu.VMEM((depth, width), BF),
            pltpu.VMEM((rows, in_depth), BF),
            pltpu.VMEM((rows, in_depth), BF),
            pltpu.VMEM((in_depth, in_width), BF),
            pltpu.SemaphoreType.DMA((6,)),
        ],
        **params(58, 4.5),
    )(first.reshape(1), core.reshape(1), *grads, basis_out, *acts, basis_in)


def mm_kernel(hops, at, q_ref, t_ref, b_ref, *outs):
    width = outs[0].shape[1]
    blocks = b_ref.shape[1] // width
    for n, k in enumerate(hops):
        if blocks == 1:
            basis = b_ref[...]
        else:
            basis = b_ref[:, pl.ds(pl.multiple_of(lax.rem(at[0] + k, blocks) * width, width), width)]
        for ref, dst in ((q_ref, outs[2 * n]), (t_ref, outs[2 * n + 1])):
            dst[...] = jnp.dot(ref[...], basis, preferred_element_type=F32).astype(dst.dtype)


def block_mm(q, t, basis, me, hops, width, dtypes):
    return pl.pallas_call(
        functools.partial(mm_kernel, hops),
        in_specs=[SMEM, VMEM, VMEM, VMEM],
        out_specs=[VMEM] * (2 * len(hops)),
        out_shape=[jax.ShapeDtypeStruct((q.shape[0], width), d) for d in dtypes for _ in range(2)],
        **params(20, 4),
    )(me.reshape(1), q, t, basis)


def pick_kernel(at, *refs):
    half = len(refs) // 2
    for src, dst in zip(refs[:half], refs[half:]):
        dst[...] = src[...]


def pick_blocks(array, me, rows):
    cols = array.shape[1]
    return pl.pallas_call(
        pick_kernel,
        grid_spec=pltpu.PrefetchScalarGridSpec(
            num_scalar_prefetch=1,
            grid=(1,),
            in_specs=[
                pl.BlockSpec((rows, cols), lambda i, at, k=k: (lax.rem(at[0] + k, 4), 0)) for k in (0, *HOPS)
            ],
            out_specs=[pl.BlockSpec((rows, cols), lambda i, at: (0, 0))] * 4,
        ),
        out_shape=[jax.ShapeDtypeStruct((rows, cols), array.dtype)] * 4,
        **params(16, 1.2),
    )(me.reshape(1), array, array, array, array)


def sum_kernel(at, own_q, own_t, q1, q2, t1, t2, o2, o1, o3, keep):
    part = keep.shape[0] // 2
    for hop, dst in ((2, o2), (1, o1), (3, o3), (0, keep)):
        rows = pl.ds(pl.multiple_of(lax.rem(at[0] + hop, 4) * part, part), part)
        for n, (a, b, c) in enumerate(((own_q, q1, q2), (own_t, t1, t2))):
            total = a[rows, :] + b[rows, :].astype(F32) + c[rows, :].astype(F32)
            dst[n * part : (n + 1) * part, :] = total.astype(dst.dtype)


def sum_blocks(me, *parts):
    rows, cols = parts[0].shape
    small = jax.ShapeDtypeStruct((rows // 2, cols), BF)
    return pl.pallas_call(
        sum_kernel,
        in_specs=[SMEM] + [VMEM] * 6,
        out_specs=[VMEM] * 4,
        out_shape=[small, small, small, jax.ShapeDtypeStruct((rows // 2, cols), F32)],
        **params(12, 1.6),
    )(me.reshape(1), *parts)


def gather_rows(me, pieces, whole):
    part = pieces[0].shape[0] // 2
    for k, piece in zip((0, *HOPS), pieces):
        row = lax.rem(me[0] + 4 - k, 4) * part
        whole[pl.ds(pl.multiple_of(row, part), part), :] = piece[:part, :]
        whole[pl.ds(pl.multiple_of(row + 4 * part, part), part), :] = piece[part:, :]


def add_kernel(*refs):
    *parts, out = refs
    total = parts[0][...].astype(F32)
    for part in parts[1:]:
        total = total + part[...].astype(F32)
    out[...] = total.astype(out.dtype)


def add(dtype, *parts, us=0.1):
    return pl.pallas_call(
        add_kernel,
        in_specs=[VMEM] * len(parts),
        out_specs=VMEM,
        out_shape=jax.ShapeDtypeStruct(parts[0].shape, dtype),
        **params(8, us),
    )(*parts)


def pack_kernel(at, mine, other, e2, e1, e3, o2, o1, o3, rot_in):
    part = mine.shape[0]
    rot_in[pl.ds(pl.multiple_of(at[0] * part, part), part), :] = mine[...]
    rot_in[pl.ds(pl.multiple_of((1 - at[0]) * part, part), part), :] = other[...]
    rows = e2.shape[0]
    for src, dst in ((e2, o2), (e1, o1), (e3, o3)):
        dst[:rows, :] = src[...]
        dst[rows:, :] = rot_in[...]


def pack(me, mine, other, eigs):
    rows, cols = mine.shape
    both = jax.ShapeDtypeStruct((eigs[0].shape[0] + 2 * rows, cols), mine.dtype)
    return pl.pallas_call(
        pack_kernel,
        in_specs=[SMEM] + [VMEM] * 5,
        out_specs=[VMEM] * 4,
        out_shape=[both] * 3 + [jax.ShapeDtypeStruct((2 * rows, cols), mine.dtype)],
        **params(12, 0.2),
    )(me.reshape(1), mine, other, *eigs)


def score_kernel(me, pick, grid, *refs):
    pieces, eig_own, in_own, packs = refs[:4], refs[4], refs[5], refs[6:9]
    out, rot, rot_t, ti_t = refs[9:]
    gather_rows(me, pieces, rot)
    width = eig_own.shape[0]
    eigs = [eig_own] + [p.at[:width, :] for p in packs]
    ins = [in_own] + [p.at[width:, :] for p in packs]
    for n in range(4):
        ti_t[n] = ins[n][256:, :].T
    for n in range(rot.shape[1] // 128):
        rot_t[n * 128 : (n + 1) * 128, :] = rot[:, n * 128 : (n + 1) * 128].T
    damp = [grid[pick[s]] for s in range(2)]
    weights = [None, None]
    for k in range(4):
        diag = eigs[k][...].astype(F32)
        for s in range(2):
            tokens = slice(s * 128, (s + 1) * 128)
            rotated = jnp.dot(rot_t[:, tokens], ins[k][tokens, :], preferred_element_type=F32)
            precond = (rotated / (diag + damp[s])).astype(BF)
            w = jnp.dot(precond, ti_t[k], preferred_element_type=F32)
            weights[s] = w if weights[s] is None else weights[s] + w
    train = rot_t[:, 256:].astype(F32)
    both = jnp.concatenate([jnp.sum(w * train, axis=0, keepdims=True) for w in weights], axis=0) * SCALE
    out[...] = jnp.broadcast_to(both[None], out.shape)


def score(me, pick, grid, pieces, eig, rot_in, packs):
    tokens, cols = pieces[0].shape
    return pl.pallas_call(
        score_kernel,
        in_specs=[SMEM] * 3 + [VMEM] * 9,
        out_specs=VMEM,
        out_shape=jax.ShapeDtypeStruct((16, 2, 256), F32),
        scratch_shapes=[
            pltpu.VMEM((4 * tokens, cols), BF),
            pltpu.VMEM((cols, 4 * tokens), BF),
            pltpu.VMEM((4, 256, 256), BF),
        ],
        **params(24, 3),
    )(me.reshape(1), pick, grid, *pieces, eig, rot_in, *packs)


def tie(value, *after):
    return lax.optimization_barrier((value, *after))[0]


def swap(value, axis, bit):
    size = 2 if axis in ("c", "zh") else 4
    return lax.ppermute(value, axis, [(i, i ^ bit) for i in range(size)])


def body(acts, out_grads, train_acts, train_grads, basis_in, basis_out, eig, grid, pick):
    y, x, c = lax.axis_index("y"), lax.axis_index("x"), lax.axis_index("c").astype(jnp.int32)
    first = jnp.where(c == 0, x, y).astype(jnp.int32)
    second = jnp.where(c == 0, y, x).astype(jnp.int32)
    width = basis_out.shape[1] // 4

    grads = (out_grads, train_grads)
    two_q, two_t, mine, other = open_mm(first, c, grads, basis_out, (acts, train_acts), basis_in, width)
    relay_q, relay_t = move(two_q, FIRST[1]), move(two_t, FIRST[3])
    in_chip = add(F32, mine, swap(other, "c", 1))
    up_q, up_t, down_q, down_t = lead_mm(*grads, basis_out, tie(first, two_q), (1, 3), width)
    from_down_t, from_up_q = move(up_t, FIRST[1]), move(down_q, FIRST[3])
    in_half = add(F32, in_chip, swap(in_chip, "zl", 1))
    up_q, down_t = add(BF, tie(up_q, in_chip), relay_q), add(BF, tie(down_t, in_chip), relay_t)
    from_down_q, from_up_t = move(up_q, FIRST[1]), move(down_t, FIRST[3])
    own_q, own_t = block_mm(*grads, basis_out, tie(first, up_q, down_t), (0,), width, (F32,))
    eig_own, *eig_send = pick_blocks(eig, tie(first, own_q), width)
    far_half = swap(add(BF, in_half), "zl", 2)

    *send, keep = sum_blocks(second, own_q, own_t, from_down_q, from_up_q, from_down_t, from_up_t)
    got = [move(v, SECOND[k]) for k, v in zip(HOPS, send)]
    in_half = add(BF, in_half, tie(far_half, send[0]))
    in_other = swap(in_half, "c", 1)
    *packs, rot_in = pack(c, in_half, in_other, eig_send)
    total = add(F32, tie(keep, rot_in), *got)
    near = add(BF, total)
    packs = [move(v, FIRST[k]) for k, v in zip(HOPS, packs)]
    total = tie(add(BF, total, swap(near, "zh", 1), us=4), packs[1])
    pieces = [total] + [move(total, SECOND[k]) for k in HOPS]
    part = score(second, pick, grid, pieces, eig_own, rot_in, packs)

    over = jnp.sum(lax.all_to_all(part, ("y", "x"), 0, 0, tiled=True), axis=0)
    over = jnp.broadcast_to(over[None], (16, *over.shape))
    return jnp.sum(lax.all_to_all(over, ("zh", "zl", "c"), 0, 0, tiled=True), axis=0)


def solution(mesh):
    fine = Mesh(mesh.devices.reshape(SIZES), ALL)
    aa, ga = ("y", "x", "zh"), ("zl", "c")
    return jax.shard_map(
        body,
        mesh=fine,
        in_specs=(
            P(None, ga),
            P(None, aa),
            P(None, ga),
            P(None, aa),
            P(ga, aa),
            P(aa, ga),
            P(ga, aa),
            P(),
            P(),
        ),
        out_specs=P(),
        check_vma=False,
    )
```

time: 134 us -> 105 us (0.78)
  Pallas kernels: 33.6 us -> 15.8 us
  starting transfers between devices: 41.3 us -> 34.3 us
  blocking collectives: 30.1 us -> 27.3 us
  waiting for transfers between devices: 23.4 us -> 21.6 us
  local copies, waits for them, and re-layouts: 3.33 us -> 4.89 us
    pallas_call x7 -> x15, Pallas kernels: 30.8 us -> 15.7 us  [the longest x1 5.11 us: lead_mm(): pl.pallas_call(functools.partial(lead_kernel, hops), in_specs=[SMEM, hbm,...]
    all_to_all x2 -> x0, starting transfers between devices: 14 us -> none  [the longest x1 7.24 us: body(): split = lax.all_to_all(in_part, ('zl', 'c'), 0, 0, tiled=True)]
    ppermute x1 -> x5, starting transfers between devices: 4.49 us -> 14.2 us  [swap(): return lax.ppermute(value, axis, [(i, i ^ bit) for i in range(size)])]
    all_to_all x2 -> x0, waiting for transfers between devices: 5.87 us -> none  [the longest x1 5.86 us: body(): lax.all_to_all(spread, ('zl', 'c'), 0, 0, tiled=True).reshape(8 * rows, -1)]
    all_to_all x1, blocking collectives: 19.6 us -> 15.6 us  [body(): lax.all_to_all(over, ('zh', 'zl', 'c'), 0, 0, tiled=True)]
    ppermute x1 -> x5, waiting for transfers between devices: 0.01 us -> 3.49 us  [swap(): return lax.ppermute(value, axis, [(i, i ^ bit) for i in range(size)])]
    ppermute x15, starting transfers between devices: 22.9 us -> 20.1 us  [move(): return lax.ppermute(value, ALL, pairs)]
    pallas_call x1, Pallas kernels: 2.72 us -> 0.12 us  [pick_blocks(): pl.pallas_call(pick_kernel, grid_spec=pltpu.PrefetchScalarGridSpec(num_sc...]
  transfers between devices with their start and end apart: 18 -> 20, of which waited for: 6 -> 7; matrix products, arithmetic and copies ran while one was open for 1% -> 0% of each run, Pallas kernels for 16% -> 8%
where the time goes in v2:
time: 105 us
  starting transfers between devices  34.3 us (33%)
  blocking collectives  27.3 us (26%)
  waiting for transfers between devices  21.6 us (21%)
  Pallas kernels  15.8 us (15%)
  local copies, waits for them, and re-layouts  4.89 us (5%)
    ppermute x15, starting transfers between devices, move(): return lax.ppermute(value, ALL, pairs)  20.1 us
    ppermute x15, waiting for transfers between devices, move(): return lax.ppermute(value, ALL, pairs)  18.1 us
    all_to_all x1, blocking collectives, body(): lax.all_to_all(over, ('zh', 'zl', 'c'), 0, 0, tiled=True)  15.6 us
    ppermute x5, starting transfers between devices, swap(): return lax.ppermute(value, axis, [(i, i ^ bit) for i in range(size)])  14.2 us
    all_to_all x1, blocking collectives, body(): over = jnp.sum(lax.all_to_all(part, ('y', 'x'), 0, 0, tiled=True), axis=0)  11.7 us
    pallas_call x1, Pallas kernels, lead_mm(): pl.pallas_call(functools.partial(lead_kernel, hops), in_specs=[SMEM, hbm,...  5.11 us
    unnamed x18, local copies, waits for them, and re-layouts  4.88 us
    pallas_call x1, Pallas kernels, open_mm(): pl.pallas_call(open_kernel, in_specs=[SMEM] * 2 + [hbm] * 6, out_specs=[V...  4.37 us
  transfers between devices with their start and end apart: 20, of which 7 were waited for; matrix products, arithmetic and copies ran while one was open for 0% of the time, Pallas kernels for 8%

profile of v2, /device:TPU:1, one launch (start us, length us, event | category | flops | bytes accessed | tf_op | source)
XLA Modules:
  0.0 104.8 jit_solution(8345742470123005514)
XLA Ops:
  0.0 4.4 %shard_map.91 = (bf16[256,896]{1,0:T(8,128)(2,1)}, bf16[256,896]{1,0:T(8,128)(2,1)}, f32[256,256]{1,0:T(8,128)}, f32[256,256]{1,0:T(8,128)}) custom-call(s32[1]{0:T(128)} %bitcast.1.at, s32[1]{0:T(128)} %bitcast.2.core_at.at, bf16[256,896]{1,0:T(8,128)(2,1)} %q_ref.1, bf16[256,896]{1,0:T(8,128)(2,1)} %t_ref.1, bf16[896,3584]{1,0:T(8,128)(2,1)} %b_ref.1, ...), custom_call_target="tpu_custom_call" | custom-call | flops 5175000064 | tf_op jit(solution)/shard_map/pallas_call | solution.py:122
  4.4 3.3 %collective-permute-start = (f32[256,256]{1,0:T(8,128)}, f32[256,256]{1,0:T(8,128)S(1)}, u32[]{:S(2)}, u32[]{:S(2)}) collective-permute-start(f32[256,256]{1,0:T(8,128)} %get-tuple-element.39), channel_id=1, source_target_pairs={{0,1},{1,0},{2,3},{3,2},{4,5},{5,4},{6,7},{7,6},{8,9},{9,8},{10,11... | collective-permute-start | bytes 786440 | tf_op jit(solution)/shard_map/ppermute | solution.py:302
  7.7 1.0 collective-permute-start.2
  9.2 5.1 %shard_map.92 = (bf16[256,896]{1,0:T(8,128)(2,1)}, bf16[256,896]{1,0:T(8,128)(2,1)}, bf16[256,896]{1,0:T(8,128)(2,1)}, bf16[256,896]{1,0:T(8,128)(2,1)}) custom-call(s32[1]{0:T(128)} %bitcast.3.at, bf16[256,896]{1,0:T(8,128)(2,1)} %q_ref.1, bf16[256,896]{1,0:T(8,128)(2,1)} %t_ref.1, bf16[896,3584]{1,0:T(8,128)(2,1)} %b_ref.1), custom_call_target="tpu_custom_call" | custom-call | flops 5750000128 | tf_op jit(solution)/shard_map/pallas_call | solution.py:81
  14.3 2.3 %collective-permute-start.4 = (bf16[256,896]{1,0:T(8,128)(2,1)}, bf16[256,896]{1,0:T(8,128)(2,1)S(1)}, u32[]{:S(2)}, u32[]{:S(2)}) collective-permute-start(bf16[256,896]{1,0:T(8,128)(2,1)} %get-tuple-element.47), channel_id=1, source_target_pairs={{0,48},{1,193},{2,50},{3,195},{4,52},{5,197},{6,54},{7,199},{8,56}... | collective-permute-start | bytes 1376264 | tf_op jit(solution)/shard_map/ppermute | solution.py:46
  16.7 1.0 copy-done.2
  17.8 2.7 %collective-permute-start.6 = (bf16[256,896]{1,0:T(8,128)(2,1)S(1)}, bf16[256,896]{1,0:T(8,128)(2,1)S(1)}, u32[]{:S(2)}, u32[]{:S(2)}) collective-permute-start(bf16[256,896]{1,0:T(8,128)(2,1)S(1)} %shard_map.95), channel_id=1, source_target_pairs={{0,48},{1,193},{2,50},{3,195},{4,52},{5,197},{6,54},{7,199},{8,56}... | collective-permute-start | bytes 1376264 | tf_op jit(solution)/shard_map/ppermute | solution.py:46
  20.5 1.0 copy-done.1
  21.8 1.7 %collective-permute-start.7 = (f32[256,256]{1,0:T(8,128)S(1)}, f32[256,256]{1,0:T(8,128)S(1)}, u32[]{:S(2)}, u32[]{:S(2)}) collective-permute-start(f32[256,256]{1,0:T(8,128)S(1)} %shard_map.93.refs_0_), channel_id=1, source_target_pairs={{0,2},{2,0},{4,6},{6,4},{1,3},{3,1},{5,7},{7,5},{8,10},{10,8},{12,... | collective-permute-start | bytes 786440 | tf_op jit(solution)/shard_map/ppermute | solution.py:302
  23.5 2.8 %copy-done.4 = bf16[896,3584]{1,0:T(8,128)(2,1)S(1)} copy-done((bf16[896,3584]{1,0:T(8,128)(2,1)S(1)}, bf16[896,3584]{1,0:T(8,128)(2,1)}, u32[]{:S(2)}) %copy-start.4) | copy-done | bytes 6422552
  26.3 1.2 %shard_map.96 = (f32[256,896]{1,0:T(8,128)S(1)}, f32[256,896]{1,0:T(8,128)S(1)}) custom-call(s32[1]{0:T(128)} %bitcast.4.at, bf16[256,896]{1,0:T(8,128)(2,1)S(1)} %copy-done.5, bf16[256,896]{1,0:T(8,128)(2,1)S(1)} %copy-done.6, bf16[896,3584]{1,0:T(8,128)(2,1)S(1)} %copy-done.4), custom_call_target="tpu_custom_call" | custom-call | flops 4600000000 | tf_op jit(solution)/shard_map/pallas_call | solution.py:153
  27.6 1.3 %collective-permute-done.7.refs_1_ = f32[256,256]{1,0:T(8,128)S(1)} collective-permute-done((f32[256,256]{1,0:T(8,128)S(1)}, f32[256,256]{1,0:T(8,128)S(1)}, u32[]{:S(2)}, u32[]{:S(2)}) %collective-permute-start.7) | collective-permute-done | bytes 262176 | tf_op jit(solution)/shard_map/ppermute | solution.py:302
  28.9 3.1 %collective-permute-start.8 = (bf16[256,256]{1,0:T(8,128)(2,1)S(1)}, bf16[256,256]{1,0:T(8,128)(2,1)S(1)}, u32[]{:S(2)}, u32[]{:S(2)}) collective-permute-start(bf16[256,256]{1,0:T(8,128)(2,1)S(1)} %shard_map.99), channel_id=1, source_target_pairs={{0,4},{2,6},{4,0},{6,2},{1,5},{3,7},{5,1},{7,3},{8,12},{10,14},{12... | collective-permute-start | bytes 393224 | tf_op jit(solution)/shard_map/ppermute | solution.py:302
  32.0 1.3 %shard_map.97 = (bf16[128,896]{1,0:T(8,128)(2,1)S(1)}, bf16[128,896]{1,0:T(8,128)(2,1)S(1)}, bf16[128,896]{1,0:T(8,128)(2,1)S(1)}, f32[128,896]{1,0:T(8,128)S(1)}) custom-call(s32[1]{0:T(128)} %bitcast.at.me, f32[256,896]{1,0:T(8,128)S(1)} %get-tuple-element.45.own_q, f32[256,896]{1,0:T(8,128)S(1)} %get-tuple-element.46.own_t, ...), custom_call_target="tpu_custom_call" | custom-call | flops 1840000000 | tf_op jit(solution)/shard_map/pallas_call | solution.py:197
  33.4 1.9 %collective-permute-start.11 = (bf16[128,896]{1,0:T(8,128)(2,1)S(1)}, bf16[128,896]{1,0:T(8,128)(2,1)S(1)}, u32[]{:S(2)}, u32[]{:S(2)}) collective-permute-start(bf16[128,896]{1,0:T(8,128)(2,1)S(1)} %get-tuple-element.58), channel_id=1, source_target_pairs={{0,64},{1,17},{2,66},{3,19},{4,68},{5,21},{6,70},{7,23},{8,72},{9,... | collective-permute-start | bytes 688136 | tf_op jit(solution)/shard_map/ppermute | solution.py:46
  35.2 1.0 collective-permute-start.12
  36.3 2.8 %collective-permute-start.10 = (bf16[128,896]{1,0:T(8,128)(2,1)S(1)}, bf16[128,896]{1,0:T(8,128)(2,1)S(1)}, u32[]{:S(2)}, u32[]{:S(2)}) collective-permute-start(bf16[128,896]{1,0:T(8,128)(2,1)S(1)} %get-tuple-element.50), channel_id=1, source_target_pairs={{0,128},{1,33},{2,130},{3,35},{4,132},{5,37},{6,134},{7,39},{8,136... | collective-permute-start | bytes 688136 | tf_op jit(solution)/shard_map/ppermute | solution.py:46
  39.1 1.2 %collective-permute-start.9 = (bf16[256,256]{1,0:T(8,128)(2,1)S(1)}, bf16[256,256]{1,0:T(8,128)(2,1)S(1)}, u32[]{:S(2)}, u32[]{:S(2)}) collective-permute-start(bf16[256,256]{1,0:T(8,128)(2,1)S(1)} %shard_map.100.mine), channel_id=1, source_target_pairs={{0,1},{1,0},{2,3},{3,2},{4,5},{5,4},{6,7},{7,6},{8,9},{9,8},{10,11... | collective-permute-start | bytes 393224 | tf_op jit(solution)/shard_map/ppermute | solution.py:302
  41.4 1.2 %collective-permute-start.14 = (bf16[1408,256]{1,0:T(8,128)(2,1)S(1)}, bf16[1408,256]{1,0:T(8,128)(2,1)S(1)}, u32[]{:S(2)}, u32[]{:S(2)}) collective-permute-start(bf16[1408,256]{1,0:T(8,128)(2,1)S(1)} %get-tuple-element.60), channel_id=1, source_target_pairs={{0,16},{1,65},{2,18},{3,67},{4,20},{5,69},{6,22},{7,71},{8,24},{9,... | collective-permute-start | bytes 2162696 | tf_op jit(solution)/shard_map/ppermute | solution.py:46
  42.6 1.2 %collective-permute-done.10.refs_1_ = bf16[128,896]{1,0:T(8,128)(2,1)S(1)} collective-permute-done((bf16[128,896]{1,0:T(8,128)(2,1)S(1)}, bf16[128,896]{1,0:T(8,128)(2,1)S(1)}, u32[]{:S(2)}, u32[]{:S(2)}) %collective-permute-start.10) | collective-permute-done | bytes 229408 | tf_op jit(solution)/shard_map/ppermute | solution.py:46
  43.9 4.9 %collective-permute-start.13 = (bf16[128,896]{1,0:T(8,128)(2,1)S(1)}, bf16[128,896]{1,0:T(8,128)(2,1)S(1)}, u32[]{:S(2)}, u32[]{:S(2)}) collective-permute-start(bf16[128,896]{1,0:T(8,128)(2,1)S(1)} %shard_map.104), channel_id=1, source_target_pairs={{0,8},{8,0},{1,9},{9,1},{2,10},{10,2},{3,11},{11,3},{4,12},{12,4},... | collective-permute-start | bytes 688136 | tf_op jit(solution)/shard_map/ppermute | solution.py:302
  48.8 1.5 %collective-permute-start.18 = (bf16[1408,256]{1,0:T(8,128)(2,1)S(1)}, bf16[1408,256]{1,0:T(8,128)(2,1)S(1)}, u32[]{:S(2)}, u32[]{:S(2)}) collective-permute-start(bf16[1408,256]{1,0:T(8,128)(2,1)S(1)} %get-tuple-element.63), channel_id=1, source_target_pairs={{0,32},{1,129},{2,34},{3,131},{4,36},{5,133},{6,38},{7,135},{8,40}... | collective-permute-start | bytes 2162696 | tf_op jit(solution)/shard_map/ppermute | solution.py:46
  50.4 1.2 %collective-permute-start.19 = (bf16[1408,256]{1,0:T(8,128)(2,1)S(1)}, bf16[1408,256]{1,0:T(8,128)(2,1)S(1)}, u32[]{:S(2)}, u32[]{:S(2)}) collective-permute-start(bf16[1408,256]{1,0:T(8,128)(2,1)S(1)} %get-tuple-element.64), channel_id=1, source_target_pairs={{0,48},{1,193},{2,50},{3,195},{4,52},{5,197},{6,54},{7,199},{8,56}... | collective-permute-start | bytes 2162696 | tf_op jit(solution)/shard_map/ppermute | solution.py:46
  51.5 1.3 %collective-permute-done.13.refs_1_ = bf16[128,896]{1,0:T(8,128)(2,1)S(1)} collective-permute-done((bf16[128,896]{1,0:T(8,128)(2,1)S(1)}, bf16[128,896]{1,0:T(8,128)(2,1)S(1)}, u32[]{:S(2)}, u32[]{:S(2)}) %collective-permute-start.13) | collective-permute-done | bytes 229408 | tf_op jit(solution)/shard_map/ppermute | solution.py:302
  52.9 1.0 collective-permute-done.14.refs_7_
  53.9 2.2 %collective-permute-start.17 = (bf16[128,896]{1,0:T(8,128)(2,1)S(1)}, bf16[128,896]{1,0:T(8,128)(2,1)S(1)}, u32[]{:S(2)}, u32[]{:S(2)}) collective-permute-start(bf16[128,896]{1,0:T(8,128)(2,1)S(1)} %shard_map.105.refs_0_), channel_id=1, source_target_pairs={{0,192},{1,49},{2,194},{3,51},{4,196},{5,53},{6,198},{7,55},{8,200... | collective-permute-start | bytes 688136 | tf_op jit(solution)/shard_map/ppermute | solution.py:46
  56.1 1.7 %collective-permute-start.15 = (bf16[128,896]{1,0:T(8,128)(2,1)S(1)}, bf16[128,896]{1,0:T(8,128)(2,1)S(1)}, u32[]{:S(2)}, u32[]{:S(2)}) collective-permute-start(bf16[128,896]{1,0:T(8,128)(2,1)S(1)} %shard_map.105.refs_0_), channel_id=1, source_target_pairs={{0,128},{1,33},{2,130},{3,35},{4,132},{5,37},{6,134},{7,39},{8,136... | collective-permute-start | bytes 688136 | tf_op jit(solution)/shard_map/ppermute | solution.py:46
  57.8 3.8 %collective-permute-done.18.refs_6_ = bf16[1408,256]{1,0:T(8,128)(2,1)S(1)} collective-permute-done((bf16[1408,256]{1,0:T(8,128)(2,1)S(1)}, bf16[1408,256]{1,0:T(8,128)(2,1)S(1)}, u32[]{:S(2)}, u32[]{:S(2)}) %collective-permute-start.18) | collective-permute-done | bytes 720928 | tf_op jit(solution)/shard_map/ppermute | solution.py:46
  61.6 12.2 %collective-permute-done.19.refs_8_ = bf16[1408,256]{1,0:T(8,128)(2,1)S(1)} collective-permute-done((bf16[1408,256]{1,0:T(8,128)(2,1)S(1)}, bf16[1408,256]{1,0:T(8,128)(2,1)S(1)}, u32[]{:S(2)}, u32[]{:S(2)}) %collective-permute-start.19) | collective-permute-done | bytes 720928 | tf_op jit(solution)/shard_map/ppermute | solution.py:46
  73.8 3.0 %shard_map.106 = f32[16,2,256]{2,1,0:T(2,128)S(1)} custom-call(s32[1]{0:T(128)} %bitcast.at.me, s32[2]{0:T(128)S(1)} %copy-done.7, f32[16]{0:T(128)S(1)} %copy-done.8, bf16[128,896]{1,0:T(8,128)(2,1)S(1)} %shard_map.105.refs_0_, bf16[128,896]{1,0:T(8,128)(2,1)S(1)} %collective-permute-done.15.refs_1_, bf16[128,896]{1,0:T(8,128)(2,1)S(1)} %collective-permute-done.16.refs_2_, ...), custom_call_target="tpu_custom_call" | custom-call | flops 3449999872 | tf_op jit(solution)/shard_map/pallas_call | solution.py:282
  76.8 11.7 %all_to_all.10 = f32[16,2,256]{2,1,0:T(2,128)S(1)} all-to-all(f32[16,2,256]{2,1,0:T(2,128)S(1)} %shard_map.106), channel_id=1, replica_groups=mesh['y'=4,'x'=4,'zh'=2,'zl'=4,'c'=2] {'y','x'}, dimensions={0} | all-to-all | bytes 65536 | tf_op jit(solution)/shard_map/all_to_all | solution.py:336
  88.5 15.6 %all_to_all.11 = f32[16,2,256]{2,1,0:T(2,128)S(1)} all-to-all(f32[16,2,256]{2,1,0:T(2,128)S(1)} %broadcast_in_dim.2), channel_id=1, replica_groups=mesh['y'=4,'x'=4,'zh'=2,'zl'=4,'c'=2] {'zh','zl','c'}, dimensions={0} | all-to-all | bytes 65536 | tf_op jit(solution)/shard_map/all_to_all | solution.py:338
  (47 shorter events, 2.9 us)
Async XLA Ops:
  4.4 12.2 %collective-permute-start = (f32[256,256]{1,0:T(8,128)}, f32[256,256]{1,0:T(8,128)S(1)}, u32[]{:S(2)}, u32[]{:S(2)}) collective-permute-start(f32[256,256]{1,0:T(8,128)} %get-tuple-element.39), channel_id=1, source_target_pairs={{0,1},{1,0},{2,3},{3,2},{4,5},{5,4},{6,7},{7,6},{8,9},{9,8},{10,11... | collective-permute-start | bytes 786440 | tf_op jit(solution)/shard_map/ppermute | solution.py:302
  7.7 8.9 %collective-permute-start.2 = (bf16[256,896]{1,0:T(8,128)(2,1)}, bf16[256,896]{1,0:T(8,128)(2,1)S(1)}, u32[]{:S(2)}, u32[]{:S(2)}) collective-permute-start(bf16[256,896]{1,0:T(8,128)(2,1)} %get-tuple-element.43), channel_id=1, source_target_pairs={{0,48},{1,193},{2,50},{3,195},{4,52},{5,197},{6,54},{7,199},{8,56}... | collective-permute-start | bytes 1376264 | tf_op jit(solution)/shard_map/ppermute | solution.py:46
  8.7 11.8 %collective-permute-start.1 = (bf16[256,896]{1,0:T(8,128)(2,1)}, bf16[256,896]{1,0:T(8,128)(2,1)S(1)}, u32[]{:S(2)}, u32[]{:S(2)}) collective-permute-start(bf16[256,896]{1,0:T(8,128)(2,1)} %get-tuple-element.35), channel_id=1, source_target_pairs={{0,16},{1,65},{2,18},{3,67},{4,20},{5,69},{6,22},{7,71},{8,24},{9,... | collective-permute-start | bytes 1376264 | tf_op jit(solution)/shard_map/ppermute | solution.py:46
  9.2 7.4 %copy-start.3 = (f32[256,256]{1,0:T(8,128)S(1)}, f32[256,256]{1,0:T(8,128)}, u32[]{:S(2)}) copy-start(f32[256,256]{1,0:T(8,128)} %get-tuple-element.38.refs_0_) | copy-start | bytes 786436
  9.2 14.3 %copy-start.5 = (bf16[256,896]{1,0:T(8,128)(2,1)S(1)}, bf16[256,896]{1,0:T(8,128)(2,1)}, u32[]{:S(2)}) copy-start(bf16[256,896]{1,0:T(8,128)(2,1)} %q_ref.1) | copy-start | bytes 1376260
  9.2 14.3 %copy-start.6 = (bf16[256,896]{1,0:T(8,128)(2,1)S(1)}, bf16[256,896]{1,0:T(8,128)(2,1)}, u32[]{:S(2)}) copy-start(bf16[256,896]{1,0:T(8,128)(2,1)} %t_ref.1) | copy-start | bytes 1376260
  14.3 17.7 %collective-permute-start.4 = (bf16[256,896]{1,0:T(8,128)(2,1)}, bf16[256,896]{1,0:T(8,128)(2,1)S(1)}, u32[]{:S(2)}, u32[]{:S(2)}) collective-permute-start(bf16[256,896]{1,0:T(8,128)(2,1)} %get-tuple-element.47), channel_id=1, source_target_pairs={{0,48},{1,193},{2,50},{3,195},{4,52},{5,197},{6,54},{7,199},{8,56}... | collective-permute-start | bytes 1376264 | tf_op jit(solution)/shard_map/ppermute | solution.py:46
  16.6 15.4 %collective-permute-start.5 = (bf16[256,896]{1,0:T(8,128)(2,1)}, bf16[256,896]{1,0:T(8,128)(2,1)S(1)}, u32[]{:S(2)}, u32[]{:S(2)}) collective-permute-start(bf16[256,896]{1,0:T(8,128)(2,1)} %get-tuple-element.48), channel_id=1, source_target_pairs={{0,16},{1,65},{2,18},{3,67},{4,20},{5,69},{6,22},{7,71},{8,24},{9,... | collective-permute-start | bytes 1376264 | tf_op jit(solution)/shard_map/ppermute | solution.py:46
  16.6 1.0 copy-start.2
  17.8 14.2 %collective-permute-start.6 = (bf16[256,896]{1,0:T(8,128)(2,1)S(1)}, bf16[256,896]{1,0:T(8,128)(2,1)S(1)}, u32[]{:S(2)}, u32[]{:S(2)}) collective-permute-start(bf16[256,896]{1,0:T(8,128)(2,1)S(1)} %shard_map.95), channel_id=1, source_target_pairs={{0,48},{1,193},{2,50},{3,195},{4,52},{5,197},{6,54},{7,199},{8,56}... | collective-permute-start | bytes 1376264 | tf_op jit(solution)/shard_map/ppermute | solution.py:46
  20.5 1.0 copy-start.1
  21.7 10.4 %collective-permute-start.3 = (bf16[256,896]{1,0:T(8,128)(2,1)S(1)}, bf16[256,896]{1,0:T(8,128)(2,1)}, u32[]{:S(2)}, u32[]{:S(2)}) collective-permute-start(bf16[256,896]{1,0:T(8,128)(2,1)S(1)} %shard_map.94), channel_id=1, source_target_pairs={{0,16},{1,65},{2,18},{3,67},{4,20},{5,69},{6,22},{7,71},{8,24},{9,... | collective-permute-start | bytes 1376264 | tf_op jit(solution)/shard_map/ppermute | solution.py:46
  21.8 7.1 %collective-permute-start.7 = (f32[256,256]{1,0:T(8,128)S(1)}, f32[256,256]{1,0:T(8,128)S(1)}, u32[]{:S(2)}, u32[]{:S(2)}) collective-permute-start(f32[256,256]{1,0:T(8,128)S(1)} %shard_map.93.refs_0_), channel_id=1, source_target_pairs={{0,2},{2,0},{4,6},{6,4},{1,3},{3,1},{5,7},{7,5},{8,10},{10,8},{12,... | collective-permute-start | bytes 786440 | tf_op jit(solution)/shard_map/ppermute | solution.py:302
  23.5 2.8 %copy-start.4 = (bf16[896,3584]{1,0:T(8,128)(2,1)S(1)}, bf16[896,3584]{1,0:T(8,128)(2,1)}, u32[]{:S(2)}) copy-start(bf16[896,3584]{1,0:T(8,128)(2,1)} %b_ref.1) | copy-start | bytes 19267588
  27.6 12.7 %copy-start = (bf16[3584,256]{1,0:T(8,128)(2,1)S(1)}, bf16[3584,256]{1,0:T(8,128)(2,1)}, u32[]{:S(2)}) copy-start(bf16[3584,256]{1,0:T(8,128)(2,1)} %refs_3_.1) | copy-start | bytes 5505028
  28.9 10.1 %collective-permute-start.8 = (bf16[256,256]{1,0:T(8,128)(2,1)S(1)}, bf16[256,256]{1,0:T(8,128)(2,1)S(1)}, u32[]{:S(2)}, u32[]{:S(2)}) collective-permute-start(bf16[256,256]{1,0:T(8,128)(2,1)S(1)} %shard_map.99), channel_id=1, source_target_pairs={{0,4},{2,6},{4,0},{6,2},{1,5},{3,7},{5,1},{7,3},{8,12},{10,14},{12... | collective-permute-start | bytes 393224 | tf_op jit(solution)/shard_map/ppermute | solution.py:302
  33.4 9.2 %collective-permute-start.11 = (bf16[128,896]{1,0:T(8,128)(2,1)S(1)}, bf16[128,896]{1,0:T(8,128)(2,1)S(1)}, u32[]{:S(2)}, u32[]{:S(2)}) collective-permute-start(bf16[128,896]{1,0:T(8,128)(2,1)S(1)} %get-tuple-element.58), channel_id=1, source_target_pairs={{0,64},{1,17},{2,66},{3,19},{4,68},{5,21},{6,70},{7,23},{8,72},{9,... | collective-permute-start | bytes 688136 | tf_op jit(solution)/shard_map/ppermute | solution.py:46
  35.2 7.3 %collective-permute-start.12 = (bf16[128,896]{1,0:T(8,128)(2,1)S(1)}, bf16[128,896]{1,0:T(8,128)(2,1)S(1)}, u32[]{:S(2)}, u32[]{:S(2)}) collective-permute-start(bf16[128,896]{1,0:T(8,128)(2,1)S(1)} %get-tuple-element.59), channel_id=1, source_target_pairs={{0,192},{1,49},{2,194},{3,51},{4,196},{5,53},{6,198},{7,55},{8,200... | collective-permute-start | bytes 688136 | tf_op jit(solution)/shard_map/ppermute | solution.py:46
  36.3 7.5 %collective-permute-start.10 = (bf16[128,896]{1,0:T(8,128)(2,1)S(1)}, bf16[128,896]{1,0:T(8,128)(2,1)S(1)}, u32[]{:S(2)}, u32[]{:S(2)}) collective-permute-start(bf16[128,896]{1,0:T(8,128)(2,1)S(1)} %get-tuple-element.50), channel_id=1, source_target_pairs={{0,128},{1,33},{2,130},{3,35},{4,132},{5,37},{6,134},{7,39},{8,136... | collective-permute-start | bytes 688136 | tf_op jit(solution)/shard_map/ppermute | solution.py:46
  39.1 2.1 %collective-permute-start.9 = (bf16[256,256]{1,0:T(8,128)(2,1)S(1)}, bf16[256,256]{1,0:T(8,128)(2,1)S(1)}, u32[]{:S(2)}, u32[]{:S(2)}) collective-permute-start(bf16[256,256]{1,0:T(8,128)(2,1)S(1)} %shard_map.100.mine), channel_id=1, source_target_pairs={{0,1},{1,0},{2,3},{3,2},{4,5},{5,4},{6,7},{7,6},{8,9},{9,8},{10,11... | collective-permute-start | bytes 393224 | tf_op jit(solution)/shard_map/ppermute | solution.py:302
  41.4 12.5 %collective-permute-start.14 = (bf16[1408,256]{1,0:T(8,128)(2,1)S(1)}, bf16[1408,256]{1,0:T(8,128)(2,1)S(1)}, u32[]{:S(2)}, u32[]{:S(2)}) collective-permute-start(bf16[1408,256]{1,0:T(8,128)(2,1)S(1)} %get-tuple-element.60), channel_id=1, source_target_pairs={{0,16},{1,65},{2,18},{3,67},{4,20},{5,69},{6,22},{7,71},{8,24},{9,... | collective-permute-start | bytes 2162696 | tf_op jit(solution)/shard_map/ppermute | solution.py:46
  43.9 9.0 %collective-permute-start.13 = (bf16[128,896]{1,0:T(8,128)(2,1)S(1)}, bf16[128,896]{1,0:T(8,128)(2,1)S(1)}, u32[]{:S(2)}, u32[]{:S(2)}) collective-permute-start(bf16[128,896]{1,0:T(8,128)(2,1)S(1)} %shard_map.104), channel_id=1, source_target_pairs={{0,8},{8,0},{1,9},{9,1},{2,10},{10,2},{3,11},{11,3},{4,12},{12,4},... | collective-permute-start | bytes 688136 | tf_op jit(solution)/shard_map/ppermute | solution.py:302
  48.8 12.8 %collective-permute-start.18 = (bf16[1408,256]{1,0:T(8,128)(2,1)S(1)}, bf16[1408,256]{1,0:T(8,128)(2,1)S(1)}, u32[]{:S(2)}, u32[]{:S(2)}) collective-permute-start(bf16[1408,256]{1,0:T(8,128)(2,1)S(1)} %get-tuple-element.63), channel_id=1, source_target_pairs={{0,32},{1,129},{2,34},{3,131},{4,36},{5,133},{6,38},{7,135},{8,40}... | collective-permute-start | bytes 2162696 | tf_op jit(solution)/shard_map/ppermute | solution.py:46
  50.4 23.4 %copy-start.7 = (s32[2]{0:T(128)S(1)}, s32[2]{0:T(128)}, u32[]{:S(2)}) copy-start(s32[2]{0:T(128)} %pick.1) | copy-start | bytes 28
  50.4 23.4 %copy-start.8 = (f32[16]{0:T(128)S(1)}, f32[16]{0:T(128)}, u32[]{:S(2)}) copy-start(f32[16]{0:T(128)} %grid.1) | copy-start | bytes 196
  50.4 23.4 %collective-permute-start.19 = (bf16[1408,256]{1,0:T(8,128)(2,1)S(1)}, bf16[1408,256]{1,0:T(8,128)(2,1)S(1)}, u32[]{:S(2)}, u32[]{:S(2)}) collective-permute-start(bf16[1408,256]{1,0:T(8,128)(2,1)S(1)} %get-tuple-element.64), channel_id=1, source_target_pairs={{0,48},{1,193},{2,50},{3,195},{4,52},{5,197},{6,54},{7,199},{8,56}... | collective-permute-start | bytes 2162696 | tf_op jit(solution)/shard_map/ppermute | solution.py:46
  53.9 19.9 %collective-permute-start.17 = (bf16[128,896]{1,0:T(8,128)(2,1)S(1)}, bf16[128,896]{1,0:T(8,128)(2,1)S(1)}, u32[]{:S(2)}, u32[]{:S(2)}) collective-permute-start(bf16[128,896]{1,0:T(8,128)(2,1)S(1)} %shard_map.105.refs_0_), channel_id=1, source_target_pairs={{0,192},{1,49},{2,194},{3,51},{4,196},{5,53},{6,198},{7,55},{8,200... | collective-permute-start | bytes 688136 | tf_op jit(solution)/shard_map/ppermute | solution.py:46
  56.0 17.7 %collective-permute-start.16 = (bf16[128,896]{1,0:T(8,128)(2,1)S(1)}, bf16[128,896]{1,0:T(8,128)(2,1)S(1)}, u32[]{:S(2)}, u32[]{:S(2)}) collective-permute-start(bf16[128,896]{1,0:T(8,128)(2,1)S(1)} %shard_map.105.refs_0_), channel_id=1, source_target_pairs={{0,64},{1,17},{2,66},{3,19},{4,68},{5,21},{6,70},{7,23},{8,72},{9,... | collective-permute-start | bytes 688136 | tf_op jit(solution)/shard_map/ppermute | solution.py:46
  56.1 17.7 %collective-permute-start.15 = (bf16[128,896]{1,0:T(8,128)(2,1)S(1)}, bf16[128,896]{1,0:T(8,128)(2,1)S(1)}, u32[]{:S(2)}, u32[]{:S(2)}) collective-permute-start(bf16[128,896]{1,0:T(8,128)(2,1)S(1)} %shard_map.105.refs_0_), channel_id=1, source_target_pairs={{0,128},{1,33},{2,130},{3,35},{4,132},{5,37},{6,134},{7,39},{8,136... | collective-permute-start | bytes 688136 | tf_op jit(solution)/shard_map/ppermute | solution.py:46

commit v3 on v2

--- a/solution.py
+++ b/solution.py
@@ -173,7 +173,7 @@
             num_scalar_prefetch=1,
             grid=(1,),
             in_specs=[
-                pl.BlockSpec((rows, cols), lambda i, at, k=k: (lax.rem(at[0] + k, 4), 0)) for k in (0, *HOPS)
+                pl.BlockSpec((rows, cols), lambda i, at, k=k: (lax.rem(at[0] + k, 4), 0)) for k in range(4)
             ],
             out_specs=[pl.BlockSpec((rows, cols), lambda i, at: (0, 0))] * 4,
         ),
@@ -229,35 +229,62 @@
     )(*parts)
 
 
-def pack_kernel(at, mine, other, e2, e1, e3, o2, o1, o3, rot_in):
+def pack_kernel(at, mine, other, e1, e2, e3, up, down, rot_in):
     part = mine.shape[0]
     rot_in[pl.ds(pl.multiple_of(at[0] * part, part), part), :] = mine[...]
     rot_in[pl.ds(pl.multiple_of((1 - at[0]) * part, part), part), :] = other[...]
-    rows = e2.shape[0]
-    for src, dst in ((e2, o2), (e1, o1), (e3, o3)):
-        dst[:rows, :] = src[...]
-        dst[rows:, :] = rot_in[...]
-
-
-def pack(me, mine, other, eigs):
+    rows = e1.shape[0]
+    half = rows // 2
+    for n, (eig, dst) in enumerate(((e1, up), (e3, down))):
+        dst[:rows, :] = eig[...]
+        dst[rows : rows + part, :] = rot_in[(1 - n) * part : (2 - n) * part, :]
+        dst[rows + part : rows + 2 * part, :] = rot_in[n * part : (n + 1) * part, :]
+        dst[rows + 2 * part :, :] = e2[n * half : (n + 1) * half, :]
+
+
+def pack(me, mine, other, e1, e2, e3):
     rows, cols = mine.shape
-    both = jax.ShapeDtypeStruct((eigs[0].shape[0] + 2 * rows, cols), mine.dtype)
+    both = jax.ShapeDtypeStruct((e1.shape[0] * 3 // 2 + 2 * rows, cols), mine.dtype)
     return pl.pallas_call(
         pack_kernel,
         in_specs=[SMEM] + [VMEM] * 5,
-        out_specs=[VMEM] * 4,
-        out_shape=[both] * 3 + [jax.ShapeDtypeStruct((2 * rows, cols), mine.dtype)],
+        out_specs=[VMEM] * 3,
+        out_shape=[both] * 2 + [jax.ShapeDtypeStruct((2 * rows, cols), mine.dtype)],
         **params(12, 0.2),
-    )(me.reshape(1), mine, other, *eigs)
+    )(me.reshape(1), mine, other, e1, e2, e3)
+
+
+def onward_kernel(low, high, up, down):
+    rows = up.shape[0]
+    up[...] = low[low.shape[0] - rows :, :]
+    down[...] = high[high.shape[0] - rows :, :]
+
+
+def onward(low, high, rows):
+    out = jax.ShapeDtypeStruct((rows, low.shape[1]), low.dtype)
+    return pl.pallas_call(
+        onward_kernel,
+        in_specs=[VMEM] * 2,
+        out_specs=[VMEM] * 2,
+        out_shape=[out] * 2,
+        **params(8, 0.1),
+    )(low, high)
 
 
 def score_kernel(me, pick, grid, *refs):
-    pieces, eig_own, in_own, packs = refs[:4], refs[4], refs[5], refs[6:9]
-    out, rot, rot_t, ti_t = refs[9:]
+    pieces, eig_own, in_own, low, high, far_low, far_high = refs[:4], *refs[4:10]
+    out, rot, rot_t, ti_t, eig_far, in_near = refs[10:]
     gather_rows(me, pieces, rot)
     width = eig_own.shape[0]
-    eigs = [eig_own] + [p.at[:width, :] for p in packs]
-    ins = [in_own] + [p.at[width:, :] for p in packs]
+    part = in_own.shape[0] // 2
+    in_near[0, :part, :] = low[width + part : width + 2 * part, :]
+    in_near[0, part:, :] = low[width : width + part, :]
+    in_near[1, :part, :] = far_low[:part, :]
+    in_near[1, part:, :] = far_high[:part, :]
+    eig_far[: width // 2, :] = far_low[part:, :]
+    eig_far[width // 2 :, :] = far_high[part:, :]
+    eigs = [eig_own, low.at[:width, :], high.at[:width, :], eig_far]
+    ins = [in_own, in_near.at[0], high.at[width : width + 2 * part, :], in_near.at[1]]
     for n in range(4):
         ti_t[n] = ins[n][256:, :].T
     for n in range(rot.shape[1] // 128):
@@ -277,20 +304,22 @@
     out[...] = jnp.broadcast_to(both[None], out.shape)
 
 
-def score(me, pick, grid, pieces, eig, rot_in, packs):
+def score(me, pick, grid, pieces, eig, rot_in, messages):
     tokens, cols = pieces[0].shape
     return pl.pallas_call(
         score_kernel,
-        in_specs=[SMEM] * 3 + [VMEM] * 9,
+        in_specs=[SMEM] * 3 + [VMEM] * 10,
         out_specs=VMEM,
         out_shape=jax.ShapeDtypeStruct((16, 2, 256), F32),
         scratch_shapes=[
             pltpu.VMEM((4 * tokens, cols), BF),
             pltpu.VMEM((cols, 4 * tokens), BF),
             pltpu.VMEM((4, 256, 256), BF),
+            pltpu.VMEM(eig.shape, BF),
+            pltpu.VMEM((2, *rot_in.shape), BF),
         ],
         **params(24, 3),
-    )(me.reshape(1), pick, grid, *pieces, eig, rot_in, *packs)
+    )(me.reshape(1), pick, grid, *pieces, eig, rot_in, *messages)
 
 
 def tie(value, *after):
@@ -319,23 +348,25 @@
     from_down_q, from_up_t = move(up_q, FIRST[1]), move(down_t, FIRST[3])
     own_q, own_t = block_mm(*grads, basis_out, tie(first, up_q, down_t), (0,), width, (F32,))
     eig_own, *eig_send = pick_blocks(eig, tie(first, own_q), width)
-    far_half = swap(add(BF, in_half), "zl", 2)
+    far_half = swap(add(BF, in_half, us=0.1), "zl", 2)
 
     *send, keep = sum_blocks(second, own_q, own_t, from_down_q, from_up_q, from_down_t, from_up_t)
     got = [move(v, SECOND[k]) for k, v in zip(HOPS, send)]
     in_half = add(BF, in_half, tie(far_half, send[0]))
     in_other = swap(in_half, "c", 1)
-    *packs, rot_in = pack(c, in_half, in_other, eig_send)
-    total = add(F32, tie(keep, rot_in), *got)
+    up, down, rot_in = pack(c, in_half, in_other, *eig_send)
+    total = add(F32, tie(keep, rot_in), *got, us=8)
     near = add(BF, total)
-    packs = [move(v, FIRST[k]) for k, v in zip(HOPS, packs)]
-    total = tie(add(BF, total, swap(near, "zh", 1), us=4), packs[1])
+    low, high = move(up, FIRST[1]), move(down, FIRST[3])
+    up, down = onward(low, high, width // 2 + in_half.shape[0])
+    messages = low, high, move(up, FIRST[1]), move(down, FIRST[3])
+    total = add(BF, total, swap(near, "zh", 1), us=4)
     pieces = [total] + [move(total, SECOND[k]) for k in HOPS]
-    part = score(second, pick, grid, pieces, eig_own, rot_in, packs)
-
-    over = jnp.sum(lax.all_to_all(part, ("y", "x"), 0, 0, tiled=True), axis=0)
+    part = score(second, pick, grid, pieces, eig_own, rot_in, messages)
+
+    over = jnp.sum(lax.all_to_all(part, ("zh", "zl", "c"), 0, 0, tiled=True), axis=0)
     over = jnp.broadcast_to(over[None], (16, *over.shape))
-    return jnp.sum(lax.all_to_all(over, ("zh", "zl", "c"), 0, 0, tiled=True), axis=0)
+    return jnp.sum(lax.all_to_all(over, ("y", "x"), 0, 0, tiled=True), axis=0)
 
 
 def solution(mesh):

time: 105 us -> 101 us (0.962)
  waiting for transfers between devices: 21.6 us -> 15.8 us
  starting transfers between devices: 34.3 us -> 37.8 us
  blocking collectives: 27.3 us -> 25.6 us
    ppermute x15 -> x16, waiting for transfers between devices: 18.1 us -> 13.6 us  [move(): return lax.ppermute(value, ALL, pairs)]
    ppermute x15 -> x16, starting transfers between devices: 20.1 us -> 22.1 us  [move(): return lax.ppermute(value, ALL, pairs)]
    all_to_all x2, blocking collectives: 27.3 us -> 25.6 us  [the longest x1 16.4 us: body(): lax.all_to_all(part, ('zh', 'zl', 'c'), 0, 0, tiled=True)]
    ppermute x5, starting transfers between devices: 14.2 us -> 15.7 us  [swap(): return lax.ppermute(value, axis, [(i, i ^ bit) for i in range(size)])]
    ppermute x5, waiting for transfers between devices: 3.49 us -> 2.17 us  [swap(): return lax.ppermute(value, axis, [(i, i ^ bit) for i in range(size)])]
    pallas_call x1 -> x2, Pallas kernels: 3.03 us -> 3.07 us  [the longest x1 3.03 us: score(): pl.pallas_call(score_kernel, in_specs=[SMEM] * 3 + [VMEM] * 10, out_specs...]
  transfers between devices with their start and end apart: 20 -> 21, of which waited for: 7 -> 5; matrix products, arithmetic and copies ran while one was open for 0% -> 0% of each run, Pallas kernels for 8% -> 8%
where the time goes in v3:
time: 101 us
  starting transfers between devices  37.8 us (37%)
  blocking collectives  25.6 us (25%)
  Pallas kernels  15.9 us (16%)
  waiting for transfers between devices  15.8 us (16%)
  local copies, waits for them, and re-layouts  4.89 us (5%)
    ppermute x16, starting transfers between devices, move(): return lax.ppermute(value, ALL, pairs)  22.1 us
    all_to_all x1, blocking collectives, body(): lax.all_to_all(part, ('zh', 'zl', 'c'), 0, 0, tiled=True)  16.4 us
    ppermute x5, starting transfers between devices, swap(): return lax.ppermute(value, axis, [(i, i ^ bit) for i in range(size)])  15.7 us
    ppermute x16, waiting for transfers between devices, move(): return lax.ppermute(value, ALL, pairs)  13.6 us
    all_to_all x1, blocking collectives, body(): return jnp.sum(lax.all_to_all(over, ('y', 'x'), 0, 0, tiled=True), axis=0)  9.27 us
    pallas_call x1, Pallas kernels, lead_mm(): pl.pallas_call(functools.partial(lead_kernel, hops), in_specs=[SMEM, hbm,...  5.12 us
    unnamed x18, local copies, waits for them, and re-layouts  4.88 us
    pallas_call x1, Pallas kernels, open_mm(): pl.pallas_call(open_kernel, in_specs=[SMEM] * 2 + [hbm] * 6, out_specs=[V...  4.37 us
  transfers between devices with their start and end apart: 21, of which 5 were waited for; matrix products, arithmetic and copies ran while one was open for 0% of the time, Pallas kernels for 8%

profile of v3, /device:TPU:1, one launch (start us, length us, event | category | flops | bytes accessed | tf_op | source)
XLA Modules:
  0.0 100.8 jit_solution(14507424037681673145)
XLA Ops:
  0.0 4.4 %shard_map.91 = (bf16[256,896]{1,0:T(8,128)(2,1)}, bf16[256,896]{1,0:T(8,128)(2,1)}, f32[256,256]{1,0:T(8,128)}, f32[256,256]{1,0:T(8,128)}) custom-call(s32[1]{0:T(128)} %bitcast.1.at, s32[1]{0:T(128)} %bitcast.2.core_at.at, bf16[256,896]{1,0:T(8,128)(2,1)} %q_ref.1, bf16[256,896]{1,0:T(8,128)(2,1)} %t_ref.1, bf16[896,3584]{1,0:T(8,128)(2,1)} %b_ref.1, ...), custom_call_target="tpu_custom_call" | custom-call | flops 5175000064 | tf_op jit(solution)/shard_map/pallas_call | solution.py:122
  4.4 3.3 %collective-permute-start = (f32[256,256]{1,0:T(8,128)}, f32[256,256]{1,0:T(8,128)S(1)}, u32[]{:S(2)}, u32[]{:S(2)}) collective-permute-start(f32[256,256]{1,0:T(8,128)} %get-tuple-element.39), channel_id=1, source_target_pairs={{0,1},{1,0},{2,3},{3,2},{4,5},{5,4},{6,7},{7,6},{8,9},{9,8},{10,11... | collective-permute-start | bytes 786440 | tf_op jit(solution)/shard_map/ppermute | solution.py:331
  7.7 1.0 collective-permute-start.2
  9.2 5.1 %shard_map.92 = (bf16[256,896]{1,0:T(8,128)(2,1)}, bf16[256,896]{1,0:T(8,128)(2,1)}, bf16[256,896]{1,0:T(8,128)(2,1)}, bf16[256,896]{1,0:T(8,128)(2,1)}) custom-call(s32[1]{0:T(128)} %bitcast.3.at, bf16[256,896]{1,0:T(8,128)(2,1)} %q_ref.1, bf16[256,896]{1,0:T(8,128)(2,1)} %t_ref.1, bf16[896,3584]{1,0:T(8,128)(2,1)} %b_ref.1), custom_call_target="tpu_custom_call" | custom-call | flops 5750000128 | tf_op jit(solution)/shard_map/pallas_call | solution.py:81
  14.3 2.3 %collective-permute-start.4 = (bf16[256,896]{1,0:T(8,128)(2,1)}, bf16[256,896]{1,0:T(8,128)(2,1)S(1)}, u32[]{:S(2)}, u32[]{:S(2)}) collective-permute-start(bf16[256,896]{1,0:T(8,128)(2,1)} %get-tuple-element.47), channel_id=1, source_target_pairs={{0,48},{1,193},{2,50},{3,195},{4,52},{5,197},{6,54},{7,199},{8,56}... | collective-permute-start | bytes 1376264 | tf_op jit(solution)/shard_map/ppermute | solution.py:46
  16.7 1.0 %copy-done.2 = bf16[256,896]{1,0:T(8,128)(2,1)S(1)} copy-done((bf16[256,896]{1,0:T(8,128)(2,1)S(1)}, bf16[256,896]{1,0:T(8,128)(2,1)}, u32[]{:S(2)}) %copy-start.2) | copy-done | bytes 458776
  17.8 2.7 %collective-permute-start.6 = (bf16[256,896]{1,0:T(8,128)(2,1)S(1)}, bf16[256,896]{1,0:T(8,128)(2,1)S(1)}, u32[]{:S(2)}, u32[]{:S(2)}) collective-permute-start(bf16[256,896]{1,0:T(8,128)(2,1)S(1)} %shard_map.95), channel_id=1, source_target_pairs={{0,48},{1,193},{2,50},{3,195},{4,52},{5,197},{6,54},{7,199},{8,56}... | collective-permute-start | bytes 1376264 | tf_op jit(solution)/shard_map/ppermute | solution.py:46
  20.5 1.0 %copy-done.1 = bf16[256,896]{1,0:T(8,128)(2,1)S(1)} copy-done((bf16[256,896]{1,0:T(8,128)(2,1)S(1)}, bf16[256,896]{1,0:T(8,128)(2,1)}, u32[]{:S(2)}) %copy-start.1) | copy-done | bytes 458776
  21.8 1.7 %collective-permute-start.7 = (f32[256,256]{1,0:T(8,128)S(1)}, f32[256,256]{1,0:T(8,128)S(1)}, u32[]{:S(2)}, u32[]{:S(2)}) collective-permute-start(f32[256,256]{1,0:T(8,128)S(1)} %shard_map.93.refs_0_), channel_id=1, source_target_pairs={{0,2},{2,0},{4,6},{6,4},{1,3},{3,1},{5,7},{7,5},{8,10},{10,8},{12,... | collective-permute-start | bytes 786440 | tf_op jit(solution)/shard_map/ppermute | solution.py:331
  23.5 2.8 %copy-done.4 = bf16[896,3584]{1,0:T(8,128)(2,1)S(1)} copy-done((bf16[896,3584]{1,0:T(8,128)(2,1)S(1)}, bf16[896,3584]{1,0:T(8,128)(2,1)}, u32[]{:S(2)}) %copy-start.4) | copy-done | bytes 6422552
  26.3 1.2 %shard_map.96 = (f32[256,896]{1,0:T(8,128)S(1)}, f32[256,896]{1,0:T(8,128)S(1)}) custom-call(s32[1]{0:T(128)} %bitcast.4.at, bf16[256,896]{1,0:T(8,128)(2,1)S(1)} %copy-done.5, bf16[256,896]{1,0:T(8,128)(2,1)S(1)} %copy-done.6, bf16[896,3584]{1,0:T(8,128)(2,1)S(1)} %copy-done.4), custom_call_target="tpu_custom_call" | custom-call | flops 4600000000 | tf_op jit(solution)/shard_map/pallas_call | solution.py:153
  27.6 1.3 %collective-permute-done.7.refs_1_ = f32[256,256]{1,0:T(8,128)S(1)} collective-permute-done((f32[256,256]{1,0:T(8,128)S(1)}, f32[256,256]{1,0:T(8,128)S(1)}, u32[]{:S(2)}, u32[]{:S(2)}) %collective-permute-start.7) | collective-permute-done | bytes 262176 | tf_op jit(solution)/shard_map/ppermute | solution.py:331
  28.9 3.1 %collective-permute-start.8 = (bf16[256,256]{1,0:T(8,128)(2,1)S(1)}, bf16[256,256]{1,0:T(8,128)(2,1)S(1)}, u32[]{:S(2)}, u32[]{:S(2)}) collective-permute-start(bf16[256,256]{1,0:T(8,128)(2,1)S(1)} %shard_map.99), channel_id=1, source_target_pairs={{0,4},{2,6},{4,0},{6,2},{1,5},{3,7},{5,1},{7,3},{8,12},{10,14},{12... | collective-permute-start | bytes 393224 | tf_op jit(solution)/shard_map/ppermute | solution.py:331
  32.0 1.3 %shard_map.97 = (bf16[128,896]{1,0:T(8,128)(2,1)S(1)}, bf16[128,896]{1,0:T(8,128)(2,1)S(1)}, bf16[128,896]{1,0:T(8,128)(2,1)S(1)}, f32[128,896]{1,0:T(8,128)S(1)}) custom-call(s32[1]{0:T(128)} %bitcast.at.me, f32[256,896]{1,0:T(8,128)S(1)} %get-tuple-element.45.own_q, f32[256,896]{1,0:T(8,128)S(1)} %get-tuple-element.46.own_t, ...), custom_call_target="tpu_custom_call" | custom-call | flops 1840000000 | tf_op jit(solution)/shard_map/pallas_call | solution.py:197
  33.4 1.9 %collective-permute-start.11 = (bf16[128,896]{1,0:T(8,128)(2,1)S(1)}, bf16[128,896]{1,0:T(8,128)(2,1)S(1)}, u32[]{:S(2)}, u32[]{:S(2)}) collective-permute-start(bf16[128,896]{1,0:T(8,128)(2,1)S(1)} %get-tuple-element.58), channel_id=1, source_target_pairs={{0,64},{1,17},{2,66},{3,19},{4,68},{5,21},{6,70},{7,23},{8,72},{9,... | collective-permute-start | bytes 688136 | tf_op jit(solution)/shard_map/ppermute | solution.py:46
  35.2 1.0 %collective-permute-start.12 = (bf16[128,896]{1,0:T(8,128)(2,1)S(1)}, bf16[128,896]{1,0:T(8,128)(2,1)S(1)}, u32[]{:S(2)}, u32[]{:S(2)}) collective-permute-start(bf16[128,896]{1,0:T(8,128)(2,1)S(1)} %get-tuple-element.59), channel_id=1, source_target_pairs={{0,192},{1,49},{2,194},{3,51},{4,196},{5,53},{6,198},{7,55},{8,200... | collective-permute-start | bytes 688136 | tf_op jit(solution)/shard_map/ppermute | solution.py:46
  36.3 2.8 %collective-permute-start.10 = (bf16[128,896]{1,0:T(8,128)(2,1)S(1)}, bf16[128,896]{1,0:T(8,128)(2,1)S(1)}, u32[]{:S(2)}, u32[]{:S(2)}) collective-permute-start(bf16[128,896]{1,0:T(8,128)(2,1)S(1)} %get-tuple-element.50), channel_id=1, source_target_pairs={{0,128},{1,33},{2,130},{3,35},{4,132},{5,37},{6,134},{7,39},{8,136... | collective-permute-start | bytes 688136 | tf_op jit(solution)/shard_map/ppermute | solution.py:46
  39.1 1.2 %collective-permute-start.9 = (bf16[256,256]{1,0:T(8,128)(2,1)S(1)}, bf16[256,256]{1,0:T(8,128)(2,1)S(1)}, u32[]{:S(2)}, u32[]{:S(2)}) collective-permute-start(bf16[256,256]{1,0:T(8,128)(2,1)S(1)} %shard_map.100.mine), channel_id=1, source_target_pairs={{0,1},{1,0},{2,3},{3,2},{4,5},{5,4},{6,7},{7,6},{8,9},{9,8},{10,11... | collective-permute-start | bytes 393224 | tf_op jit(solution)/shard_map/ppermute | solution.py:331
  40.4 0.9 collective-permute-done.9.other
  41.4 1.2 %collective-permute-start.17 = (bf16[1856,256]{1,0:T(8,128)(2,1)S(1)}, bf16[1856,256]{1,0:T(8,128)(2,1)S(1)}, u32[]{:S(2)}, u32[]{:S(2)}) collective-permute-start(bf16[1856,256]{1,0:T(8,128)(2,1)S(1)} %get-tuple-element.61), channel_id=1, source_target_pairs={{0,16},{1,65},{2,18},{3,67},{4,20},{5,69},{6,22},{7,71},{8,24},{9,... | collective-permute-start | bytes 2850824 | tf_op jit(solution)/shard_map/ppermute | solution.py:46
  42.6 1.6 %collective-permute-start.18 = (bf16[1856,256]{1,0:T(8,128)(2,1)S(1)}, bf16[1856,256]{1,0:T(8,128)(2,1)S(1)}, u32[]{:S(2)}, u32[]{:S(2)}) collective-permute-start(bf16[1856,256]{1,0:T(8,128)(2,1)S(1)} %get-tuple-element.62), channel_id=1, source_target_pairs={{0,48},{1,193},{2,50},{3,195},{4,52},{5,197},{6,54},{7,199},{8,56}... | collective-permute-start | bytes 2850824 | tf_op jit(solution)/shard_map/ppermute | solution.py:46
  44.3 6.5 %collective-permute-start.13 = (bf16[128,896]{1,0:T(8,128)(2,1)S(1)}, bf16[128,896]{1,0:T(8,128)(2,1)S(1)}, u32[]{:S(2)}, u32[]{:S(2)}) collective-permute-start(bf16[128,896]{1,0:T(8,128)(2,1)S(1)} %shard_map.104), channel_id=1, source_target_pairs={{0,8},{8,0},{1,9},{9,1},{2,10},{10,2},{3,11},{11,3},{4,12},{12,4},... | collective-permute-start | bytes 688136 | tf_op jit(solution)/shard_map/ppermute | solution.py:331
  50.7 5.6 %collective-permute-done.17.low.refs_6_ = bf16[1856,256]{1,0:T(8,128)(2,1)S(1)} collective-permute-done((bf16[1856,256]{1,0:T(8,128)(2,1)S(1)}, bf16[1856,256]{1,0:T(8,128)(2,1)S(1)}, u32[]{:S(2)}, u32[]{:S(2)}) %collective-permute-start.17) | collective-permute-done | bytes 950304 | tf_op jit(solution)/shard_map/ppermute | solution.py:46
  56.4 1.2 %collective-permute-start.19 = (bf16[704,256]{1,0:T(8,128)(2,1)S(1)}, bf16[704,256]{1,0:T(8,128)(2,1)S(1)}, u32[]{:S(2)}, u32[]{:S(2)}) collective-permute-start(bf16[704,256]{1,0:T(8,128)(2,1)S(1)} %get-tuple-element.63), channel_id=1, source_target_pairs={{0,16},{1,65},{2,18},{3,67},{4,20},{5,69},{6,22},{7,71},{8,24},{9,... | collective-permute-start | bytes 1081352 | tf_op jit(solution)/shard_map/ppermute | solution.py:46
  57.6 1.5 %collective-permute-start.20 = (bf16[704,256]{1,0:T(8,128)(2,1)S(1)}, bf16[704,256]{1,0:T(8,128)(2,1)S(1)}, u32[]{:S(2)}, u32[]{:S(2)}) collective-permute-start(bf16[704,256]{1,0:T(8,128)(2,1)S(1)} %get-tuple-element.64), channel_id=1, source_target_pairs={{0,48},{1,193},{2,50},{3,195},{4,52},{5,197},{6,54},{7,199},{8,56}... | collective-permute-start | bytes 1081352 | tf_op jit(solution)/shard_map/ppermute | solution.py:46
  59.2 2.6 %collective-permute-start.16 = (bf16[128,896]{1,0:T(8,128)(2,1)S(1)}, bf16[128,896]{1,0:T(8,128)(2,1)S(1)}, u32[]{:S(2)}, u32[]{:S(2)}) collective-permute-start(bf16[128,896]{1,0:T(8,128)(2,1)S(1)} %shard_map.105.refs_0_), channel_id=1, source_target_pairs={{0,192},{1,49},{2,194},{3,51},{4,196},{5,53},{6,198},{7,55},{8,200... | collective-permute-start | bytes 688136 | tf_op jit(solution)/shard_map/ppermute | solution.py:46
  61.8 1.7 %collective-permute-start.14 = (bf16[128,896]{1,0:T(8,128)(2,1)S(1)}, bf16[128,896]{1,0:T(8,128)(2,1)S(1)}, u32[]{:S(2)}, u32[]{:S(2)}) collective-permute-start(bf16[128,896]{1,0:T(8,128)(2,1)S(1)} %shard_map.105.refs_0_), channel_id=1, source_target_pairs={{0,128},{1,33},{2,130},{3,35},{4,132},{5,37},{6,134},{7,39},{8,136... | collective-permute-start | bytes 688136 | tf_op jit(solution)/shard_map/ppermute | solution.py:46
  63.5 4.8 %collective-permute-done.16.refs_3_ = bf16[128,896]{1,0:T(8,128)(2,1)S(1)} collective-permute-done((bf16[128,896]{1,0:T(8,128)(2,1)S(1)}, bf16[128,896]{1,0:T(8,128)(2,1)S(1)}, u32[]{:S(2)}, u32[]{:S(2)}) %collective-permute-start.16) | collective-permute-done | bytes 229408 | tf_op jit(solution)/shard_map/ppermute | solution.py:46
  68.3 3.1 %collective-permute-done.14.refs_1_ = bf16[128,896]{1,0:T(8,128)(2,1)S(1)} collective-permute-done((bf16[128,896]{1,0:T(8,128)(2,1)S(1)}, bf16[128,896]{1,0:T(8,128)(2,1)S(1)}, u32[]{:S(2)}, u32[]{:S(2)}) %collective-permute-start.14) | collective-permute-done | bytes 229408 | tf_op jit(solution)/shard_map/ppermute | solution.py:46
  71.5 3.0 %shard_map.107 = f32[16,2,256]{2,1,0:T(2,128)S(1)} custom-call(s32[1]{0:T(128)} %bitcast.at.me, s32[2]{0:T(128)S(1)} %copy-done.7, f32[16]{0:T(128)S(1)} %copy-done.8, bf16[128,896]{1,0:T(8,128)(2,1)S(1)} %shard_map.105.refs_0_, bf16[128,896]{1,0:T(8,128)(2,1)S(1)} %collective-permute-done.14.refs_1_, bf16[128,896]{1,0:T(8,128)(2,1)S(1)} %collective-permute-done.15.refs_2_, ...), custom_call_target="tpu_custom_call" | custom-call | flops 3449999872 | tf_op jit(solution)/shard_map/pallas_call | solution.py:309
  74.5 16.4 %all_to_all.10 = f32[16,2,256]{2,1,0:T(2,128)S(1)} all-to-all(f32[16,2,256]{2,1,0:T(2,128)S(1)} %shard_map.107), channel_id=1, replica_groups=mesh['y'=4,'x'=4,'zh'=2,'zl'=4,'c'=2] {'zh','zl','c'}, dimensions={0} | all-to-all | bytes 65536 | tf_op jit(solution)/shard_map/all_to_all | solution.py:367
  90.9 9.3 %all_to_all.11 = f32[16,2,256]{2,1,0:T(2,128)S(1)} all-to-all(f32[16,2,256]{2,1,0:T(2,128)S(1)} %broadcast_in_dim.2), channel_id=1, replica_groups=mesh['y'=4,'x'=4,'zh'=2,'zl'=4,'c'=2] {'y','x'}, dimensions={0} | all-to-all | bytes 65536 | tf_op jit(solution)/shard_map/all_to_all | solution.py:369
  (50 shorter events, 2.1 us)
Async XLA Ops:
  4.4 12.2 %collective-permute-start = (f32[256,256]{1,0:T(8,128)}, f32[256,256]{1,0:T(8,128)S(1)}, u32[]{:S(2)}, u32[]{:S(2)}) collective-permute-start(f32[256,256]{1,0:T(8,128)} %get-tuple-element.39), channel_id=1, source_target_pairs={{0,1},{1,0},{2,3},{3,2},{4,5},{5,4},{6,7},{7,6},{8,9},{9,8},{10,11... | collective-permute-start | bytes 786440 | tf_op jit(solution)/shard_map/ppermute | solution.py:331
  7.7 8.9 %collective-permute-start.2 = (bf16[256,896]{1,0:T(8,128)(2,1)}, bf16[256,896]{1,0:T(8,128)(2,1)S(1)}, u32[]{:S(2)}, u32[]{:S(2)}) collective-permute-start(bf16[256,896]{1,0:T(8,128)(2,1)} %get-tuple-element.43), channel_id=1, source_target_pairs={{0,48},{1,193},{2,50},{3,195},{4,52},{5,197},{6,54},{7,199},{8,56}... | collective-permute-start | bytes 1376264 | tf_op jit(solution)/shard_map/ppermute | solution.py:46
  8.7 11.8 %collective-permute-start.1 = (bf16[256,896]{1,0:T(8,128)(2,1)}, bf16[256,896]{1,0:T(8,128)(2,1)S(1)}, u32[]{:S(2)}, u32[]{:S(2)}) collective-permute-start(bf16[256,896]{1,0:T(8,128)(2,1)} %get-tuple-element.35), channel_id=1, source_target_pairs={{0,16},{1,65},{2,18},{3,67},{4,20},{5,69},{6,22},{7,71},{8,24},{9,... | collective-permute-start | bytes 1376264 | tf_op jit(solution)/shard_map/ppermute | solution.py:46
  9.2 7.4 %copy-start.3 = (f32[256,256]{1,0:T(8,128)S(1)}, f32[256,256]{1,0:T(8,128)}, u32[]{:S(2)}) copy-start(f32[256,256]{1,0:T(8,128)} %get-tuple-element.38.refs_0_) | copy-start | bytes 786436
  9.2 14.3 %copy-start.5 = (bf16[256,896]{1,0:T(8,128)(2,1)S(1)}, bf16[256,896]{1,0:T(8,128)(2,1)}, u32[]{:S(2)}) copy-start(bf16[256,896]{1,0:T(8,128)(2,1)} %q_ref.1) | copy-start | bytes 1376260
  9.2 14.3 %copy-start.6 = (bf16[256,896]{1,0:T(8,128)(2,1)S(1)}, bf16[256,896]{1,0:T(8,128)(2,1)}, u32[]{:S(2)}) copy-start(bf16[256,896]{1,0:T(8,128)(2,1)} %t_ref.1) | copy-start | bytes 1376260
  14.3 17.7 %collective-permute-start.4 = (bf16[256,896]{1,0:T(8,128)(2,1)}, bf16[256,896]{1,0:T(8,128)(2,1)S(1)}, u32[]{:S(2)}, u32[]{:S(2)}) collective-permute-start(bf16[256,896]{1,0:T(8,128)(2,1)} %get-tuple-element.47), channel_id=1, source_target_pairs={{0,48},{1,193},{2,50},{3,195},{4,52},{5,197},{6,54},{7,199},{8,56}... | collective-permute-start | bytes 1376264 | tf_op jit(solution)/shard_map/ppermute | solution.py:46
  16.6 15.4 %collective-permute-start.5 = (bf16[256,896]{1,0:T(8,128)(2,1)}, bf16[256,896]{1,0:T(8,128)(2,1)S(1)}, u32[]{:S(2)}, u32[]{:S(2)}) collective-permute-start(bf16[256,896]{1,0:T(8,128)(2,1)} %get-tuple-element.48), channel_id=1, source_target_pairs={{0,16},{1,65},{2,18},{3,67},{4,20},{5,69},{6,22},{7,71},{8,24},{9,... | collective-permute-start | bytes 1376264 | tf_op jit(solution)/shard_map/ppermute | solution.py:46
  16.7 1.0 %copy-start.2 = (bf16[256,896]{1,0:T(8,128)(2,1)S(1)}, bf16[256,896]{1,0:T(8,128)(2,1)}, u32[]{:S(2)}) copy-start(bf16[256,896]{1,0:T(8,128)(2,1)} %get-tuple-element.42.refs_0_) | copy-start | bytes 1376260
  17.8 14.2 %collective-permute-start.6 = (bf16[256,896]{1,0:T(8,128)(2,1)S(1)}, bf16[256,896]{1,0:T(8,128)(2,1)S(1)}, u32[]{:S(2)}, u32[]{:S(2)}) collective-permute-start(bf16[256,896]{1,0:T(8,128)(2,1)S(1)} %shard_map.95), channel_id=1, source_target_pairs={{0,48},{1,193},{2,50},{3,195},{4,52},{5,197},{6,54},{7,199},{8,56}... | collective-permute-start | bytes 1376264 | tf_op jit(solution)/shard_map/ppermute | solution.py:46
  20.5 1.0 %copy-start.1 = (bf16[256,896]{1,0:T(8,128)(2,1)S(1)}, bf16[256,896]{1,0:T(8,128)(2,1)}, u32[]{:S(2)}) copy-start(bf16[256,896]{1,0:T(8,128)(2,1)} %get-tuple-element.40.refs_0_) | copy-start | bytes 1376260
  21.7 10.4 %collective-permute-start.3 = (bf16[256,896]{1,0:T(8,128)(2,1)S(1)}, bf16[256,896]{1,0:T(8,128)(2,1)}, u32[]{:S(2)}, u32[]{:S(2)}) collective-permute-start(bf16[256,896]{1,0:T(8,128)(2,1)S(1)} %shard_map.94), channel_id=1, source_target_pairs={{0,16},{1,65},{2,18},{3,67},{4,20},{5,69},{6,22},{7,71},{8,24},{9,... | collective-permute-start | bytes 1376264 | tf_op jit(solution)/shard_map/ppermute | solution.py:46
  21.8 7.1 %collective-permute-start.7 = (f32[256,256]{1,0:T(8,128)S(1)}, f32[256,256]{1,0:T(8,128)S(1)}, u32[]{:S(2)}, u32[]{:S(2)}) collective-permute-start(f32[256,256]{1,0:T(8,128)S(1)} %shard_map.93.refs_0_), channel_id=1, source_target_pairs={{0,2},{2,0},{4,6},{6,4},{1,3},{3,1},{5,7},{7,5},{8,10},{10,8},{12,... | collective-permute-start | bytes 786440 | tf_op jit(solution)/shard_map/ppermute | solution.py:331
  23.5 2.8 %copy-start.4 = (bf16[896,3584]{1,0:T(8,128)(2,1)S(1)}, bf16[896,3584]{1,0:T(8,128)(2,1)}, u32[]{:S(2)}) copy-start(bf16[896,3584]{1,0:T(8,128)(2,1)} %b_ref.1) | copy-start | bytes 19267588
  27.6 12.7 %copy-start = (bf16[3584,256]{1,0:T(8,128)(2,1)S(1)}, bf16[3584,256]{1,0:T(8,128)(2,1)}, u32[]{:S(2)}) copy-start(bf16[3584,256]{1,0:T(8,128)(2,1)} %refs_3_.1) | copy-start | bytes 5505028
  28.9 10.1 %collective-permute-start.8 = (bf16[256,256]{1,0:T(8,128)(2,1)S(1)}, bf16[256,256]{1,0:T(8,128)(2,1)S(1)}, u32[]{:S(2)}, u32[]{:S(2)}) collective-permute-start(bf16[256,256]{1,0:T(8,128)(2,1)S(1)} %shard_map.99), channel_id=1, source_target_pairs={{0,4},{2,6},{4,0},{6,2},{1,5},{3,7},{5,1},{7,3},{8,12},{10,14},{12... | collective-permute-start | bytes 393224 | tf_op jit(solution)/shard_map/ppermute | solution.py:331
  33.4 10.8 %collective-permute-start.11 = (bf16[128,896]{1,0:T(8,128)(2,1)S(1)}, bf16[128,896]{1,0:T(8,128)(2,1)S(1)}, u32[]{:S(2)}, u32[]{:S(2)}) collective-permute-start(bf16[128,896]{1,0:T(8,128)(2,1)S(1)} %get-tuple-element.58), channel_id=1, source_target_pairs={{0,64},{1,17},{2,66},{3,19},{4,68},{5,21},{6,70},{7,23},{8,72},{9,... | collective-permute-start | bytes 688136 | tf_op jit(solution)/shard_map/ppermute | solution.py:46
  35.2 8.9 %collective-permute-start.12 = (bf16[128,896]{1,0:T(8,128)(2,1)S(1)}, bf16[128,896]{1,0:T(8,128)(2,1)S(1)}, u32[]{:S(2)}, u32[]{:S(2)}) collective-permute-start(bf16[128,896]{1,0:T(8,128)(2,1)S(1)} %get-tuple-element.59), channel_id=1, source_target_pairs={{0,192},{1,49},{2,194},{3,51},{4,196},{5,53},{6,198},{7,55},{8,200... | collective-permute-start | bytes 688136 | tf_op jit(solution)/shard_map/ppermute | solution.py:46
  36.3 7.8 %collective-permute-start.10 = (bf16[128,896]{1,0:T(8,128)(2,1)S(1)}, bf16[128,896]{1,0:T(8,128)(2,1)S(1)}, u32[]{:S(2)}, u32[]{:S(2)}) collective-permute-start(bf16[128,896]{1,0:T(8,128)(2,1)S(1)} %get-tuple-element.50), channel_id=1, source_target_pairs={{0,128},{1,33},{2,130},{3,35},{4,132},{5,37},{6,134},{7,39},{8,136... | collective-permute-start | bytes 688136 | tf_op jit(solution)/shard_map/ppermute | solution.py:46
  39.1 2.1 %collective-permute-start.9 = (bf16[256,256]{1,0:T(8,128)(2,1)S(1)}, bf16[256,256]{1,0:T(8,128)(2,1)S(1)}, u32[]{:S(2)}, u32[]{:S(2)}) collective-permute-start(bf16[256,256]{1,0:T(8,128)(2,1)S(1)} %shard_map.100.mine), channel_id=1, source_target_pairs={{0,1},{1,0},{2,3},{3,2},{4,5},{5,4},{6,7},{7,6},{8,9},{9,8},{10,11... | collective-permute-start | bytes 393224 | tf_op jit(solution)/shard_map/ppermute | solution.py:331
  41.4 15.0 %collective-permute-start.17 = (bf16[1856,256]{1,0:T(8,128)(2,1)S(1)}, bf16[1856,256]{1,0:T(8,128)(2,1)S(1)}, u32[]{:S(2)}, u32[]{:S(2)}) collective-permute-start(bf16[1856,256]{1,0:T(8,128)(2,1)S(1)} %get-tuple-element.61), channel_id=1, source_target_pairs={{0,16},{1,65},{2,18},{3,67},{4,20},{5,69},{6,22},{7,71},{8,24},{9,... | collective-permute-start | bytes 2850824 | tf_op jit(solution)/shard_map/ppermute | solution.py:46
  42.6 13.8 %collective-permute-start.18 = (bf16[1856,256]{1,0:T(8,128)(2,1)S(1)}, bf16[1856,256]{1,0:T(8,128)(2,1)S(1)}, u32[]{:S(2)}, u32[]{:S(2)}) collective-permute-start(bf16[1856,256]{1,0:T(8,128)(2,1)S(1)} %get-tuple-element.62), channel_id=1, source_target_pairs={{0,48},{1,193},{2,50},{3,195},{4,52},{5,197},{6,54},{7,199},{8,56}... | collective-permute-start | bytes 2850824 | tf_op jit(solution)/shard_map/ppermute | solution.py:46
  44.3 14.9 %collective-permute-start.13 = (bf16[128,896]{1,0:T(8,128)(2,1)S(1)}, bf16[128,896]{1,0:T(8,128)(2,1)S(1)}, u32[]{:S(2)}, u32[]{:S(2)}) collective-permute-start(bf16[128,896]{1,0:T(8,128)(2,1)S(1)} %shard_map.104), channel_id=1, source_target_pairs={{0,8},{8,0},{1,9},{9,1},{2,10},{10,2},{3,11},{11,3},{4,12},{12,4},... | collective-permute-start | bytes 688136 | tf_op jit(solution)/shard_map/ppermute | solution.py:331
  56.4 15.1 %collective-permute-start.19 = (bf16[704,256]{1,0:T(8,128)(2,1)S(1)}, bf16[704,256]{1,0:T(8,128)(2,1)S(1)}, u32[]{:S(2)}, u32[]{:S(2)}) collective-permute-start(bf16[704,256]{1,0:T(8,128)(2,1)S(1)} %get-tuple-element.63), channel_id=1, source_target_pairs={{0,16},{1,65},{2,18},{3,67},{4,20},{5,69},{6,22},{7,71},{8,24},{9,... | collective-permute-start | bytes 1081352 | tf_op jit(solution)/shard_map/ppermute | solution.py:46
  57.6 13.9 %copy-start.7 = (s32[2]{0:T(128)S(1)}, s32[2]{0:T(128)}, u32[]{:S(2)}) copy-start(s32[2]{0:T(128)} %pick.1) | copy-start | bytes 28
  57.6 13.9 %copy-start.8 = (f32[16]{0:T(128)S(1)}, f32[16]{0:T(128)}, u32[]{:S(2)}) copy-start(f32[16]{0:T(128)} %grid.1) | copy-start | bytes 196
  57.6 13.9 %collective-permute-start.20 = (bf16[704,256]{1,0:T(8,128)(2,1)S(1)}, bf16[704,256]{1,0:T(8,128)(2,1)S(1)}, u32[]{:S(2)}, u32[]{:S(2)}) collective-permute-start(bf16[704,256]{1,0:T(8,128)(2,1)S(1)} %get-tuple-element.64), channel_id=1, source_target_pairs={{0,48},{1,193},{2,50},{3,195},{4,52},{5,197},{6,54},{7,199},{8,56}... | collective-permute-start | bytes 1081352 | tf_op jit(solution)/shard_map/ppermute | solution.py:46
  59.2 9.1 %collective-permute-start.16 = (bf16[128,896]{1,0:T(8,128)(2,1)S(1)}, bf16[128,896]{1,0:T(8,128)(2,1)S(1)}, u32[]{:S(2)}, u32[]{:S(2)}) collective-permute-start(bf16[128,896]{1,0:T(8,128)(2,1)S(1)} %shard_map.105.refs_0_), channel_id=1, source_target_pairs={{0,192},{1,49},{2,194},{3,51},{4,196},{5,53},{6,198},{7,55},{8,200... | collective-permute-start | bytes 688136 | tf_op jit(solution)/shard_map/ppermute | solution.py:46
  61.8 6.5 %collective-permute-start.15 = (bf16[128,896]{1,0:T(8,128)(2,1)S(1)}, bf16[128,896]{1,0:T(8,128)(2,1)S(1)}, u32[]{:S(2)}, u32[]{:S(2)}) collective-permute-start(bf16[128,896]{1,0:T(8,128)(2,1)S(1)} %shard_map.105.refs_0_), channel_id=1, source_target_pairs={{0,64},{1,17},{2,66},{3,19},{4,68},{5,21},{6,70},{7,23},{8,72},{9,... | collective-permute-start | bytes 688136 | tf_op jit(solution)/shard_map/ppermute | solution.py:46
  61.8 9.7 %collective-permute-start.14 = (bf16[128,896]{1,0:T(8,128)(2,1)S(1)}, bf16[128,896]{1,0:T(8,128)(2,1)S(1)}, u32[]{:S(2)}, u32[]{:S(2)}) collective-permute-start(bf16[128,896]{1,0:T(8,128)(2,1)S(1)} %shard_map.105.refs_0_), channel_id=1, source_target_pairs={{0,128},{1,33},{2,130},{3,35},{4,132},{5,37},{6,134},{7,39},{8,136... | collective-permute-start | bytes 688136 | tf_op jit(solution)/shard_map/ppermute | solution.py:46

commit v4 on v3

--- a/solution.py
+++ b/solution.py
@@ -229,62 +229,72 @@
     )(*parts)
 
 
-def pack_kernel(at, mine, other, e1, e2, e3, up, down, rot_in):
-    part = mine.shape[0]
-    rot_in[pl.ds(pl.multiple_of(at[0] * part, part), part), :] = mine[...]
-    rot_in[pl.ds(pl.multiple_of((1 - at[0]) * part, part), part), :] = other[...]
+def pack_kernel(e1, e2, e3, up, down):
     rows = e1.shape[0]
     half = rows // 2
     for n, (eig, dst) in enumerate(((e1, up), (e3, down))):
         dst[:rows, :] = eig[...]
-        dst[rows : rows + part, :] = rot_in[(1 - n) * part : (2 - n) * part, :]
-        dst[rows + part : rows + 2 * part, :] = rot_in[n * part : (n + 1) * part, :]
-        dst[rows + 2 * part :, :] = e2[n * half : (n + 1) * half, :]
-
-
-def pack(me, mine, other, e1, e2, e3):
-    rows, cols = mine.shape
-    both = jax.ShapeDtypeStruct((e1.shape[0] * 3 // 2 + 2 * rows, cols), mine.dtype)
+        dst[rows:, :] = e2[n * half : (n + 1) * half, :]
+
+
+def pack(e1, e2, e3):
+    rows, cols = e1.shape
     return pl.pallas_call(
         pack_kernel,
-        in_specs=[SMEM] + [VMEM] * 5,
-        out_specs=[VMEM] * 3,
-        out_shape=[both] * 2 + [jax.ShapeDtypeStruct((2 * rows, cols), mine.dtype)],
+        in_specs=[VMEM] * 3,
+        out_specs=[VMEM] * 2,
+        out_shape=[jax.ShapeDtypeStruct((rows * 3 // 2, cols), e1.dtype)] * 2,
         **params(12, 0.2),
-    )(me.reshape(1), mine, other, e1, e2, e3)
-
-
-def onward_kernel(low, high, up, down):
-    rows = up.shape[0]
-    up[...] = low[low.shape[0] - rows :, :]
-    down[...] = high[high.shape[0] - rows :, :]
-
-
-def onward(low, high, rows):
-    out = jax.ShapeDtypeStruct((rows, low.shape[1]), low.dtype)
+    )(e1, e2, e3)
+
+
+def join_kernel(at, mine, other, whole):
+    part = mine.shape[0]
+    whole[pl.ds(pl.multiple_of(at[0] * part, part), part), :] = mine[...]
+    whole[pl.ds(pl.multiple_of((1 - at[0]) * part, part), part), :] = other[...]
+
+
+def join(me, mine, other):
+    return pl.pallas_call(
+        join_kernel,
+        in_specs=[SMEM, VMEM, VMEM],
+        out_specs=VMEM,
+        out_shape=jax.ShapeDtypeStruct((2 * mine.shape[0], mine.shape[1]), mine.dtype),
+        **params(8, 0.1),
+    )(me.reshape(1), mine, other)
+
+
+def onward_kernel(low, in_low, high, in_high, up, down):
+    part = in_low.shape[0] // 2
+    half = up.shape[0] - part
+    for n, (eig, rot_in, dst) in enumerate(((low, in_low, up), (high, in_high, down))):
+        dst[:part, :] = rot_in[n * part : (n + 1) * part, :]
+        dst[part:, :] = eig[2 * half :, :]
+
+
+def onward(low, in_low, high, in_high):
+    out = jax.ShapeDtypeStruct((low.shape[0] // 3 + in_low.shape[0] // 2, low.shape[1]), low.dtype)
     return pl.pallas_call(
         onward_kernel,
-        in_specs=[VMEM] * 2,
+        in_specs=[VMEM] * 4,
         out_specs=[VMEM] * 2,
         out_shape=[out] * 2,
         **params(8, 0.1),
-    )(low, high)
+    )(low, in_low, high, in_high)
 
 
 def score_kernel(me, pick, grid, *refs):
-    pieces, eig_own, in_own, low, high, far_low, far_high = refs[:4], *refs[4:10]
-    out, rot, rot_t, ti_t, eig_far, in_near = refs[10:]
+    pieces, eig_own, in_own, low, in_low, high, in_high, far_low, far_high = refs[:4], *refs[4:12]
+    out, rot, rot_t, ti_t, eig_far, in_far = refs[12:]
     gather_rows(me, pieces, rot)
     width = eig_own.shape[0]
     part = in_own.shape[0] // 2
-    in_near[0, :part, :] = low[width + part : width + 2 * part, :]
-    in_near[0, part:, :] = low[width : width + part, :]
-    in_near[1, :part, :] = far_low[:part, :]
-    in_near[1, part:, :] = far_high[:part, :]
+    in_far[:part, :] = far_low[:part, :]
+    in_far[part:, :] = far_high[:part, :]
     eig_far[: width // 2, :] = far_low[part:, :]
     eig_far[width // 2 :, :] = far_high[part:, :]
     eigs = [eig_own, low.at[:width, :], high.at[:width, :], eig_far]
-    ins = [in_own, in_near.at[0], high.at[width : width + 2 * part, :], in_near.at[1]]
+    ins = [in_own, in_low, in_high, in_far]
     for n in range(4):
         ti_t[n] = ins[n][256:, :].T
     for n in range(rot.shape[1] // 128):
@@ -308,7 +318,7 @@
     tokens, cols = pieces[0].shape
     return pl.pallas_call(
         score_kernel,
-        in_specs=[SMEM] * 3 + [VMEM] * 10,
+        in_specs=[SMEM] * 3 + [VMEM] * 12,
         out_specs=VMEM,
         out_shape=jax.ShapeDtypeStruct((16, 2, 256), F32),
         scratch_shapes=[
@@ -316,7 +326,7 @@
             pltpu.VMEM((cols, 4 * tokens), BF),
             pltpu.VMEM((4, 256, 256), BF),
             pltpu.VMEM(eig.shape, BF),
-            pltpu.VMEM((2, *rot_in.shape), BF),
+            pltpu.VMEM(rot_in.shape, BF),
         ],
         **params(24, 3),
     )(me.reshape(1), pick, grid, *pieces, eig, rot_in, *messages)
@@ -344,22 +354,24 @@
     up_q, up_t, down_q, down_t = lead_mm(*grads, basis_out, tie(first, two_q), (1, 3), width)
     from_down_t, from_up_q = move(up_t, FIRST[1]), move(down_q, FIRST[3])
     in_half = add(F32, in_chip, swap(in_chip, "zl", 1))
-    up_q, down_t = add(BF, tie(up_q, in_chip), relay_q), add(BF, tie(down_t, in_chip), relay_t)
+    up_q, down_t = add(BF, up_q, relay_q), add(BF, down_t, relay_t)
     from_down_q, from_up_t = move(up_q, FIRST[1]), move(down_t, FIRST[3])
+    eig_own, *eigs = pick_blocks(eig, tie(first, up_q), width)
+    up, down = pack(*eigs)
+    low = move(tie(up, from_down_t, from_up_q), FIRST[1])
+    high = move(tie(down, from_down_t, from_up_q), FIRST[3])
     own_q, own_t = block_mm(*grads, basis_out, tie(first, up_q, down_t), (0,), width, (F32,))
-    eig_own, *eig_send = pick_blocks(eig, tie(first, own_q), width)
-    far_half = swap(add(BF, in_half, us=0.1), "zl", 2)
+    far_half = swap(add(BF, in_half), "zl", 2)
 
     *send, keep = sum_blocks(second, own_q, own_t, from_down_q, from_up_q, from_down_t, from_up_t)
     got = [move(v, SECOND[k]) for k, v in zip(HOPS, send)]
     in_half = add(BF, in_half, tie(far_half, send[0]))
-    in_other = swap(in_half, "c", 1)
-    up, down, rot_in = pack(c, in_half, in_other, *eig_send)
+    rot_in = join(c, in_half, swap(in_half, "c", 1))
+    in_low, in_high = move(rot_in, FIRST[1]), move(rot_in, FIRST[3])
     total = add(F32, tie(keep, rot_in), *got, us=8)
     near = add(BF, total)
-    low, high = move(up, FIRST[1]), move(down, FIRST[3])
-    up, down = onward(low, high, width // 2 + in_half.shape[0])
-    messages = low, high, move(up, FIRST[1]), move(down, FIRST[3])
+    up, down = onward(low, in_low, high, in_high)
+    messages = low, in_low, high, in_high, move(up, FIRST[1]), move(down, FIRST[3])
     total = add(BF, total, swap(near, "zh", 1), us=4)
     pieces = [total] + [move(total, SECOND[k]) for k in HOPS]
     part = score(second, pick, grid, pieces, eig_own, rot_in, messages)

time: 101 us -> 99.4 us (0.984)
  starting transfers between devices: 37.8 us -> 40.1 us
  waiting for transfers between devices: 15.8 us -> 13.7 us
  Pallas kernels: 15.9 us -> 14.8 us
    ppermute x16 -> x18, waiting for transfers between devices: 13.6 us -> 8.02 us  [move(): return lax.ppermute(value, ALL, pairs)]
    ppermute x5, waiting for transfers between devices: 2.17 us -> 5.68 us  [swap(): return lax.ppermute(value, axis, [(i, i ^ bit) for i in range(size)])]
    ppermute x16 -> x18, starting transfers between devices: 22.1 us -> 24.7 us  [move(): return lax.ppermute(value, ALL, pairs)]
    all_to_all x1, blocking collectives: 16.4 us -> 15.2 us  [body(): lax.all_to_all(part, ('zh', 'zl', 'c'), 0, 0, tiled=True)]
    pallas_call x3 -> x4, Pallas kernels: 3.21 us -> 3.18 us  [the longest x1 3.02 us: score(): pl.pallas_call(score_kernel, in_specs=[SMEM] * 3 + [VMEM] * 12, out_specs...]
  transfers between devices with their start and end apart: 21 -> 23, of which waited for: 5 -> 7; matrix products, arithmetic and copies ran while one was open for 0% -> 0% of each run, Pallas kernels for 8% -> 7%
where the time goes in v4:
time: 99.4 us; the launch traced here: 99.1 us
  starting transfers between devices  40.1 us (40%)
  blocking collectives  24.7 us (25%)
  Pallas kernels  14.8 us (15%)
  waiting for transfers between devices  13.7 us (14%)
  local copies, waits for them, and re-layouts  4.9 us (5%)
    ppermute x18, starting transfers between devices, move(): return lax.ppermute(value, ALL, pairs)  24.7 us
    ppermute x5, starting transfers between devices, swap(): return lax.ppermute(value, axis, [(i, i ^ bit) for i in range(size)])  15.4 us
    all_to_all x1, blocking collectives, body(): lax.all_to_all(part, ('zh', 'zl', 'c'), 0, 0, tiled=True)  15.2 us
    all_to_all x1, blocking collectives, body(): return jnp.sum(lax.all_to_all(over, ('y', 'x'), 0, 0, tiled=True), axis=0)  9.5 us
    ppermute x18, waiting for transfers between devices, move(): return lax.ppermute(value, ALL, pairs)  8.02 us
    ppermute x5, waiting for transfers between devices, swap(): return lax.ppermute(value, axis, [(i, i ^ bit) for i in range(size)])  5.68 us
    pallas_call x1, Pallas kernels, lead_mm(): pl.pallas_call(functools.partial(lead_kernel, hops), in_specs=[SMEM, hbm,...  5.11 us
    unnamed x18, local copies, waits for them, and re-layouts  4.88 us
  transfers between devices with their start and end apart: 23, of which 7 were waited for; matrix products, arithmetic and copies ran while one was open for 0% of the time, Pallas kernels for 7%

profile of v4, /device:TPU:1, one launch (start us, length us, event | category | flops | bytes accessed | tf_op | source)
XLA Modules:
  0.0 99.1 jit_solution(15791347069391036269)
XLA Ops:
  0.0 4.4 %shard_map.91 = (bf16[256,896]{1,0:T(8,128)(2,1)}, bf16[256,896]{1,0:T(8,128)(2,1)}, f32[256,256]{1,0:T(8,128)}, f32[256,256]{1,0:T(8,128)}) custom-call(s32[1]{0:T(128)} %bitcast.1.at, s32[1]{0:T(128)} %bitcast.2.core_at.at, bf16[256,896]{1,0:T(8,128)(2,1)} %q_ref.1, bf16[256,896]{1,0:T(8,128)(2,1)} %t_ref.1, bf16[896,3584]{1,0:T(8,128)(2,1)} %b_ref.1, ...), custom_call_target="tpu_custom_call" | custom-call | flops 5175000064 | tf_op jit(solution)/shard_map/pallas_call | solution.py:122
  4.4 2.2 %collective-permute-start = (bf16[256,896]{1,0:T(8,128)(2,1)}, bf16[256,896]{1,0:T(8,128)(2,1)S(1)}, u32[]{:S(2)}, u32[]{:S(2)}) collective-permute-start(bf16[256,896]{1,0:T(8,128)(2,1)} %get-tuple-element.34), channel_id=1, source_target_pairs={{0,16},{1,65},{2,18},{3,67},{4,20},{5,69},{6,22},{7,71},{8,24},{9,... | collective-permute-start | bytes 1376264 | tf_op jit(solution)/shard_map/ppermute | solution.py:46
  6.6 1.5 %collective-permute-start.1 = (bf16[256,896]{1,0:T(8,128)(2,1)}, bf16[256,896]{1,0:T(8,128)(2,1)S(1)}, u32[]{:S(2)}, u32[]{:S(2)}) collective-permute-start(bf16[256,896]{1,0:T(8,128)(2,1)} %get-tuple-element.38), channel_id=1, source_target_pairs={{0,48},{1,193},{2,50},{3,195},{4,52},{5,197},{6,54},{7,199},{8,56}... | collective-permute-start | bytes 1376264 | tf_op jit(solution)/shard_map/ppermute | solution.py:46
  8.1 2.8 %collective-permute-start.6 = (f32[256,256]{1,0:T(8,128)}, f32[256,256]{1,0:T(8,128)S(1)}, u32[]{:S(2)}, u32[]{:S(2)}) collective-permute-start(f32[256,256]{1,0:T(8,128)} %get-tuple-element.46), channel_id=1, source_target_pairs={{0,1},{1,0},{2,3},{3,2},{4,5},{5,4},{6,7},{7,6},{8,9},{9,8},{10,11... | collective-permute-start | bytes 786440 | tf_op jit(solution)/shard_map/ppermute | solution.py:341
  10.9 5.1 %shard_map.92 = (bf16[256,896]{1,0:T(8,128)(2,1)}, bf16[256,896]{1,0:T(8,128)(2,1)}, bf16[256,896]{1,0:T(8,128)(2,1)}, bf16[256,896]{1,0:T(8,128)(2,1)}) custom-call(s32[1]{0:T(128)} %bitcast.3.at, bf16[256,896]{1,0:T(8,128)(2,1)} %q_ref.1, bf16[256,896]{1,0:T(8,128)(2,1)} %t_ref.1, bf16[896,3584]{1,0:T(8,128)(2,1)} %b_ref.1), custom_call_target="tpu_custom_call" | custom-call | flops 5750000128 | tf_op jit(solution)/shard_map/pallas_call | solution.py:81
  16.1 1.1 %collective-permute-start.3 = (bf16[256,896]{1,0:T(8,128)(2,1)}, bf16[256,896]{1,0:T(8,128)(2,1)S(1)}, u32[]{:S(2)}, u32[]{:S(2)}) collective-permute-start(bf16[256,896]{1,0:T(8,128)(2,1)} %get-tuple-element.42), channel_id=1, source_target_pairs={{0,48},{1,193},{2,50},{3,195},{4,52},{5,197},{6,54},{7,199},{8,56}... | collective-permute-start | bytes 1376264 | tf_op jit(solution)/shard_map/ppermute | solution.py:46
  17.6 1.0 %copy-done.2 = bf16[256,896]{1,0:T(8,128)(2,1)S(1)} copy-done((bf16[256,896]{1,0:T(8,128)(2,1)S(1)}, bf16[256,896]{1,0:T(8,128)(2,1)}, u32[]{:S(2)}) %copy-start.2) | copy-done | bytes 458776
  18.8 1.0 %copy-done.1 = bf16[256,896]{1,0:T(8,128)(2,1)S(1)} copy-done((bf16[256,896]{1,0:T(8,128)(2,1)S(1)}, bf16[256,896]{1,0:T(8,128)(2,1)}, u32[]{:S(2)}) %copy-start.1) | copy-done | bytes 458776
  20.0 2.7 %collective-permute-start.5 = (bf16[256,896]{1,0:T(8,128)(2,1)S(1)}, bf16[256,896]{1,0:T(8,128)(2,1)S(1)}, u32[]{:S(2)}, u32[]{:S(2)}) collective-permute-start(bf16[256,896]{1,0:T(8,128)(2,1)S(1)} %shard_map.94), channel_id=1, source_target_pairs={{0,48},{1,193},{2,50},{3,195},{4,52},{5,197},{6,54},{7,199},{8,56}... | collective-permute-start | bytes 1376264 | tf_op jit(solution)/shard_map/ppermute | solution.py:46
  22.7 1.3 %collective-permute-start.7 = (f32[256,256]{1,0:T(8,128)S(1)}, f32[256,256]{1,0:T(8,128)S(1)}, u32[]{:S(2)}, u32[]{:S(2)}) collective-permute-start(f32[256,256]{1,0:T(8,128)S(1)} %shard_map.97.refs_0_), channel_id=1, source_target_pairs={{0,2},{2,0},{4,6},{6,4},{1,3},{3,1},{5,7},{7,5},{8,10},{10,8},{12,... | collective-permute-start | bytes 786440 | tf_op jit(solution)/shard_map/ppermute | solution.py:341
  24.0 2.8 %copy-done.4 = bf16[896,3584]{1,0:T(8,128)(2,1)S(1)} copy-done((bf16[896,3584]{1,0:T(8,128)(2,1)S(1)}, bf16[896,3584]{1,0:T(8,128)(2,1)}, u32[]{:S(2)}) %copy-start.4) | copy-done | bytes 6422552
  26.8 1.2 %shard_map.95 = (f32[256,896]{1,0:T(8,128)S(1)}, f32[256,896]{1,0:T(8,128)S(1)}) custom-call(s32[1]{0:T(128)} %bitcast.4.at, bf16[256,896]{1,0:T(8,128)(2,1)S(1)} %copy-done.5, bf16[256,896]{1,0:T(8,128)(2,1)S(1)} %copy-done.6, bf16[896,3584]{1,0:T(8,128)(2,1)S(1)} %copy-done.4), custom_call_target="tpu_custom_call" | custom-call | flops 4600000000 | tf_op jit(solution)/shard_map/pallas_call | solution.py:153
  28.1 1.6 %collective-permute-done.7.refs_1_ = f32[256,256]{1,0:T(8,128)S(1)} collective-permute-done((f32[256,256]{1,0:T(8,128)S(1)}, f32[256,256]{1,0:T(8,128)S(1)}, u32[]{:S(2)}, u32[]{:S(2)}) %collective-permute-start.7) | collective-permute-done | bytes 262176 | tf_op jit(solution)/shard_map/ppermute | solution.py:341
  29.8 3.9 %collective-permute-start.8 = (bf16[256,256]{1,0:T(8,128)(2,1)S(1)}, bf16[256,256]{1,0:T(8,128)(2,1)S(1)}, u32[]{:S(2)}, u32[]{:S(2)}) collective-permute-start(bf16[256,256]{1,0:T(8,128)(2,1)S(1)} %shard_map.99), channel_id=1, source_target_pairs={{0,4},{2,6},{4,0},{6,2},{1,5},{3,7},{5,1},{7,3},{8,12},{10,14},{12... | collective-permute-start | bytes 393224 | tf_op jit(solution)/shard_map/ppermute | solution.py:341
  34.1 2.0 %collective-permute-start.10 = (bf16[128,896]{1,0:T(8,128)(2,1)S(1)}, bf16[128,896]{1,0:T(8,128)(2,1)S(1)}, u32[]{:S(2)}, u32[]{:S(2)}) collective-permute-start(bf16[128,896]{1,0:T(8,128)(2,1)S(1)} %get-tuple-element.47), channel_id=1, source_target_pairs={{0,128},{1,33},{2,130},{3,35},{4,132},{5,37},{6,134},{7,39},{8,136... | collective-permute-start | bytes 688136 | tf_op jit(solution)/shard_map/ppermute | solution.py:46
  36.1 2.7 %collective-permute-start.12 = (bf16[128,896]{1,0:T(8,128)(2,1)S(1)}, bf16[128,896]{1,0:T(8,128)(2,1)S(1)}, u32[]{:S(2)}, u32[]{:S(2)}) collective-permute-start(bf16[128,896]{1,0:T(8,128)(2,1)S(1)} %get-tuple-element.51), channel_id=1, source_target_pairs={{0,192},{1,49},{2,194},{3,51},{4,196},{5,53},{6,198},{7,55},{8,200... | collective-permute-start | bytes 688136 | tf_op jit(solution)/shard_map/ppermute | solution.py:46
  38.7 1.0 collective-permute-done.8.refs_1_
  39.8 1.3 %collective-permute-start.9 = (bf16[256,256]{1,0:T(8,128)(2,1)S(1)}, bf16[256,256]{1,0:T(8,128)(2,1)S(1)}, u32[]{:S(2)}, u32[]{:S(2)}) collective-permute-start(bf16[256,256]{1,0:T(8,128)(2,1)S(1)} %shard_map.100.mine), channel_id=1, source_target_pairs={{0,1},{1,0},{2,3},{3,2},{4,5},{5,4},{6,7},{7,6},{8,9},{9,8},{10,11... | collective-permute-start | bytes 393224 | tf_op jit(solution)/shard_map/ppermute | solution.py:341
  41.4 0.7 collective-permute-done.9.other
  42.1 2.0 %collective-permute-start.19 = (bf16[1344,256]{1,0:T(8,128)(2,1)S(1)}, bf16[1344,256]{1,0:T(8,128)(2,1)S(1)}, u32[]{:S(2)}, u32[]{:S(2)}) collective-permute-start(bf16[1344,256]{1,0:T(8,128)(2,1)S(1)} %get-tuple-element.60), channel_id=1, source_target_pairs={{0,48},{1,193},{2,50},{3,195},{4,52},{5,197},{6,54},{7,199},{8,56}... | collective-permute-start | bytes 2064392 | tf_op jit(solution)/shard_map/ppermute | solution.py:46
  44.2 2.7 %collective-permute-start.20 = (bf16[512,256]{1,0:T(8,128)(2,1)S(1)}, bf16[512,256]{1,0:T(8,128)(2,1)S(1)}, u32[]{:S(2)}, u32[]{:S(2)}) collective-permute-start(bf16[512,256]{1,0:T(8,128)(2,1)S(1)} %shard_map.101.refs_5_), channel_id=1, source_target_pairs={{0,48},{1,193},{2,50},{3,195},{4,52},{5,197},{6,54},{7,199},{8,56}... | collective-permute-start | bytes 786440 | tf_op jit(solution)/shard_map/ppermute | solution.py:46
  47.0 6.1 %collective-permute-start.13 = (bf16[128,896]{1,0:T(8,128)(2,1)S(1)}, bf16[128,896]{1,0:T(8,128)(2,1)S(1)}, u32[]{:S(2)}, u32[]{:S(2)}) collective-permute-start(bf16[128,896]{1,0:T(8,128)(2,1)S(1)} %shard_map.103), channel_id=1, source_target_pairs={{0,8},{8,0},{1,9},{9,1},{2,10},{10,2},{3,11},{11,3},{4,12},{12,4},... | collective-permute-start | bytes 688136 | tf_op jit(solution)/shard_map/ppermute | solution.py:341
  53.1 2.4 %collective-permute-done.18.in_low.refs_7_ = bf16[512,256]{1,0:T(8,128)(2,1)S(1)} collective-permute-done((bf16[512,256]{1,0:T(8,128)(2,1)S(1)}, bf16[512,256]{1,0:T(8,128)(2,1)S(1)}, u32[]{:S(2)}, u32[]{:S(2)}) %collective-permute-start.18) | collective-permute-done | bytes 262176 | tf_op jit(solution)/shard_map/ppermute | solution.py:46
  55.7 2.8 %collective-permute-start.22 = (bf16[704,256]{1,0:T(8,128)(2,1)S(1)}, bf16[704,256]{1,0:T(8,128)(2,1)S(1)}, u32[]{:S(2)}, u32[]{:S(2)}) collective-permute-start(bf16[704,256]{1,0:T(8,128)(2,1)S(1)} %get-tuple-element.62), channel_id=1, source_target_pairs={{0,48},{1,193},{2,50},{3,195},{4,52},{5,197},{6,54},{7,199},{8,56}... | collective-permute-start | bytes 1081352 | tf_op jit(solution)/shard_map/ppermute | solution.py:46
  58.4 2.4 %collective-permute-done.13.refs_1_ = bf16[128,896]{1,0:T(8,128)(2,1)S(1)} collective-permute-done((bf16[128,896]{1,0:T(8,128)(2,1)S(1)}, bf16[128,896]{1,0:T(8,128)(2,1)S(1)}, u32[]{:S(2)}, u32[]{:S(2)}) %collective-permute-start.13) | collective-permute-done | bytes 229408 | tf_op jit(solution)/shard_map/ppermute | solution.py:341
  60.8 1.6 %collective-permute-start.14 = (bf16[128,896]{1,0:T(8,128)(2,1)S(1)}, bf16[128,896]{1,0:T(8,128)(2,1)S(1)}, u32[]{:S(2)}, u32[]{:S(2)}) collective-permute-start(bf16[128,896]{1,0:T(8,128)(2,1)S(1)} %shard_map.104.refs_0_), channel_id=1, source_target_pairs={{0,128},{1,33},{2,130},{3,35},{4,132},{5,37},{6,134},{7,39},{8,136... | collective-permute-start | bytes 688136 | tf_op jit(solution)/shard_map/ppermute | solution.py:46
  62.9 2.2 %collective-permute-start.16 = (bf16[128,896]{1,0:T(8,128)(2,1)S(1)}, bf16[128,896]{1,0:T(8,128)(2,1)S(1)}, u32[]{:S(2)}, u32[]{:S(2)}) collective-permute-start(bf16[128,896]{1,0:T(8,128)(2,1)S(1)} %shard_map.104.refs_0_), channel_id=1, source_target_pairs={{0,192},{1,49},{2,194},{3,51},{4,196},{5,53},{6,198},{7,55},{8,200... | collective-permute-start | bytes 688136 | tf_op jit(solution)/shard_map/ppermute | solution.py:46
  65.1 3.4 %collective-permute-done.14.refs_1_ = bf16[128,896]{1,0:T(8,128)(2,1)S(1)} collective-permute-done((bf16[128,896]{1,0:T(8,128)(2,1)S(1)}, bf16[128,896]{1,0:T(8,128)(2,1)S(1)}, u32[]{:S(2)}, u32[]{:S(2)}) %collective-permute-start.14) | collective-permute-done | bytes 229408 | tf_op jit(solution)/shard_map/ppermute | solution.py:46
  68.5 2.2 %collective-permute-done.15.refs_2_ = bf16[128,896]{1,0:T(8,128)(2,1)S(1)} collective-permute-done((bf16[128,896]{1,0:T(8,128)(2,1)S(1)}, bf16[128,896]{1,0:T(8,128)(2,1)S(1)}, u32[]{:S(2)}, u32[]{:S(2)}) %collective-permute-start.15) | collective-permute-done | bytes 229408 | tf_op jit(solution)/shard_map/ppermute | solution.py:46
  70.7 3.0 %shard_map.108 = f32[16,2,256]{2,1,0:T(2,128)S(1)} custom-call(s32[1]{0:T(128)} %bitcast.at.me, s32[2]{0:T(128)S(1)} %copy-done.7, f32[16]{0:T(128)S(1)} %copy-done.8, bf16[128,896]{1,0:T(8,128)(2,1)S(1)} %shard_map.104.refs_0_, bf16[128,896]{1,0:T(8,128)(2,1)S(1)} %collective-permute-done.14.refs_1_, bf16[128,896]{1,0:T(8,128)(2,1)S(1)} %collective-permute-done.15.refs_2_, ...), custom_call_target="tpu_custom_call" | custom-call | flops 3449999872 | tf_op jit(solution)/shard_map/pallas_call | solution.py:319
  73.8 15.2 %all_to_all.10 = f32[16,2,256]{2,1,0:T(2,128)S(1)} all-to-all(f32[16,2,256]{2,1,0:T(2,128)S(1)} %shard_map.108), channel_id=1, replica_groups=mesh['y'=4,'x'=4,'zh'=2,'zl'=4,'c'=2] {'zh','zl','c'}, dimensions={0} | all-to-all | bytes 65536 | tf_op jit(solution)/shard_map/all_to_all | solution.py:379
  89.0 9.5 %all_to_all.11 = f32[16,2,256]{2,1,0:T(2,128)S(1)} all-to-all(f32[16,2,256]{2,1,0:T(2,128)S(1)} %broadcast_in_dim.2), channel_id=1, replica_groups=mesh['y'=4,'x'=4,'zh'=2,'zl'=4,'c'=2] {'y','x'}, dimensions={0} | all-to-all | bytes 65536 | tf_op jit(solution)/shard_map/all_to_all | solution.py:381
  (55 shorter events, 3.1 us)
Async XLA Ops:
  4.4 13.2 %collective-permute-start = (bf16[256,896]{1,0:T(8,128)(2,1)}, bf16[256,896]{1,0:T(8,128)(2,1)S(1)}, u32[]{:S(2)}, u32[]{:S(2)}) collective-permute-start(bf16[256,896]{1,0:T(8,128)(2,1)} %get-tuple-element.34), channel_id=1, source_target_pairs={{0,16},{1,65},{2,18},{3,67},{4,20},{5,69},{6,22},{7,71},{8,24},{9,... | collective-permute-start | bytes 1376264 | tf_op jit(solution)/shard_map/ppermute | solution.py:46
  6.6 12.2 %collective-permute-start.1 = (bf16[256,896]{1,0:T(8,128)(2,1)}, bf16[256,896]{1,0:T(8,128)(2,1)S(1)}, u32[]{:S(2)}, u32[]{:S(2)}) collective-permute-start(bf16[256,896]{1,0:T(8,128)(2,1)} %get-tuple-element.38), channel_id=1, source_target_pairs={{0,48},{1,193},{2,50},{3,195},{4,52},{5,197},{6,54},{7,199},{8,56}... | collective-permute-start | bytes 1376264 | tf_op jit(solution)/shard_map/ppermute | solution.py:46
  8.1 14.6 %collective-permute-start.6 = (f32[256,256]{1,0:T(8,128)}, f32[256,256]{1,0:T(8,128)S(1)}, u32[]{:S(2)}, u32[]{:S(2)}) collective-permute-start(f32[256,256]{1,0:T(8,128)} %get-tuple-element.46), channel_id=1, source_target_pairs={{0,1},{1,0},{2,3},{3,2},{4,5},{5,4},{6,7},{7,6},{8,9},{9,8},{10,11... | collective-permute-start | bytes 786440 | tf_op jit(solution)/shard_map/ppermute | solution.py:341
  10.9 11.8 %copy-start.3 = (f32[256,256]{1,0:T(8,128)S(1)}, f32[256,256]{1,0:T(8,128)}, u32[]{:S(2)}) copy-start(f32[256,256]{1,0:T(8,128)} %get-tuple-element.45.refs_0_) | copy-start | bytes 786436
  10.9 13.1 %copy-start.5 = (bf16[256,896]{1,0:T(8,128)(2,1)S(1)}, bf16[256,896]{1,0:T(8,128)(2,1)}, u32[]{:S(2)}) copy-start(bf16[256,896]{1,0:T(8,128)(2,1)} %q_ref.1) | copy-start | bytes 1376260
  10.9 13.1 %copy-start.6 = (bf16[256,896]{1,0:T(8,128)(2,1)S(1)}, bf16[256,896]{1,0:T(8,128)(2,1)}, u32[]{:S(2)}) copy-start(bf16[256,896]{1,0:T(8,128)(2,1)} %t_ref.1) | copy-start | bytes 1376260
  16.1 17.7 %collective-permute-start.3 = (bf16[256,896]{1,0:T(8,128)(2,1)}, bf16[256,896]{1,0:T(8,128)(2,1)S(1)}, u32[]{:S(2)}, u32[]{:S(2)}) collective-permute-start(bf16[256,896]{1,0:T(8,128)(2,1)} %get-tuple-element.42), channel_id=1, source_target_pairs={{0,48},{1,193},{2,50},{3,195},{4,52},{5,197},{6,54},{7,199},{8,56}... | collective-permute-start | bytes 1376264 | tf_op jit(solution)/shard_map/ppermute | solution.py:46
  17.1 16.6 %collective-permute-start.4 = (bf16[256,896]{1,0:T(8,128)(2,1)}, bf16[256,896]{1,0:T(8,128)(2,1)S(1)}, u32[]{:S(2)}, u32[]{:S(2)}) collective-permute-start(bf16[256,896]{1,0:T(8,128)(2,1)} %get-tuple-element.43), channel_id=1, source_target_pairs={{0,16},{1,65},{2,18},{3,67},{4,20},{5,69},{6,22},{7,71},{8,24},{9,... | collective-permute-start | bytes 1376264 | tf_op jit(solution)/shard_map/ppermute | solution.py:46
  17.6 1.0 %copy-start.2 = (bf16[256,896]{1,0:T(8,128)(2,1)S(1)}, bf16[256,896]{1,0:T(8,128)(2,1)}, u32[]{:S(2)}) copy-start(bf16[256,896]{1,0:T(8,128)(2,1)} %get-tuple-element.36.refs_0_) | copy-start | bytes 1376260
  18.7 15.0 %collective-permute-start.2 = (bf16[256,896]{1,0:T(8,128)(2,1)S(1)}, bf16[256,896]{1,0:T(8,128)(2,1)S(1)}, u32[]{:S(2)}, u32[]{:S(2)}) collective-permute-start(bf16[256,896]{1,0:T(8,128)(2,1)S(1)} %shard_map.93), channel_id=1, source_target_pairs={{0,16},{1,65},{2,18},{3,67},{4,20},{5,69},{6,22},{7,71},{8,24},{9,... | collective-permute-start | bytes 1376264 | tf_op jit(solution)/shard_map/ppermute | solution.py:46
  18.8 1.0 %copy-start.1 = (bf16[256,896]{1,0:T(8,128)(2,1)S(1)}, bf16[256,896]{1,0:T(8,128)(2,1)}, u32[]{:S(2)}) copy-start(bf16[256,896]{1,0:T(8,128)(2,1)} %get-tuple-element.37.refs_0_) | copy-start | bytes 1376260
  20.0 13.8 %collective-permute-start.5 = (bf16[256,896]{1,0:T(8,128)(2,1)S(1)}, bf16[256,896]{1,0:T(8,128)(2,1)S(1)}, u32[]{:S(2)}, u32[]{:S(2)}) collective-permute-start(bf16[256,896]{1,0:T(8,128)(2,1)S(1)} %shard_map.94), channel_id=1, source_target_pairs={{0,48},{1,193},{2,50},{3,195},{4,52},{5,197},{6,54},{7,199},{8,56}... | collective-permute-start | bytes 1376264 | tf_op jit(solution)/shard_map/ppermute | solution.py:46
  22.7 7.0 %collective-permute-start.7 = (f32[256,256]{1,0:T(8,128)S(1)}, f32[256,256]{1,0:T(8,128)S(1)}, u32[]{:S(2)}, u32[]{:S(2)}) collective-permute-start(f32[256,256]{1,0:T(8,128)S(1)} %shard_map.97.refs_0_), channel_id=1, source_target_pairs={{0,2},{2,0},{4,6},{6,4},{1,3},{3,1},{5,7},{7,5},{8,10},{10,8},{12,... | collective-permute-start | bytes 786440 | tf_op jit(solution)/shard_map/ppermute | solution.py:341
  24.0 2.8 %copy-start.4 = (bf16[896,3584]{1,0:T(8,128)(2,1)S(1)}, bf16[896,3584]{1,0:T(8,128)(2,1)}, u32[]{:S(2)}) copy-start(bf16[896,3584]{1,0:T(8,128)(2,1)} %b_ref.1) | copy-start | bytes 19267588
  28.1 13.0 %copy-start = (bf16[3584,256]{1,0:T(8,128)(2,1)S(1)}, bf16[3584,256]{1,0:T(8,128)(2,1)}, u32[]{:S(2)}) copy-start(bf16[3584,256]{1,0:T(8,128)(2,1)} %refs_3_.1) | copy-start | bytes 5505028
  29.8 9.9 %collective-permute-start.8 = (bf16[256,256]{1,0:T(8,128)(2,1)S(1)}, bf16[256,256]{1,0:T(8,128)(2,1)S(1)}, u32[]{:S(2)}, u32[]{:S(2)}) collective-permute-start(bf16[256,256]{1,0:T(8,128)(2,1)S(1)} %shard_map.99), channel_id=1, source_target_pairs={{0,4},{2,6},{4,0},{6,2},{1,5},{3,7},{5,1},{7,3},{8,12},{10,14},{12... | collective-permute-start | bytes 393224 | tf_op jit(solution)/shard_map/ppermute | solution.py:341
  34.1 10.0 %collective-permute-start.10 = (bf16[128,896]{1,0:T(8,128)(2,1)S(1)}, bf16[128,896]{1,0:T(8,128)(2,1)S(1)}, u32[]{:S(2)}, u32[]{:S(2)}) collective-permute-start(bf16[128,896]{1,0:T(8,128)(2,1)S(1)} %get-tuple-element.47), channel_id=1, source_target_pairs={{0,128},{1,33},{2,130},{3,35},{4,132},{5,37},{6,134},{7,39},{8,136... | collective-permute-start | bytes 688136 | tf_op jit(solution)/shard_map/ppermute | solution.py:46
  36.1 8.1 %collective-permute-start.11 = (bf16[128,896]{1,0:T(8,128)(2,1)S(1)}, bf16[128,896]{1,0:T(8,128)(2,1)S(1)}, u32[]{:S(2)}, u32[]{:S(2)}) collective-permute-start(bf16[128,896]{1,0:T(8,128)(2,1)S(1)} %get-tuple-element.50), channel_id=1, source_target_pairs={{0,64},{1,17},{2,66},{3,19},{4,68},{5,21},{6,70},{7,23},{8,72},{9,... | collective-permute-start | bytes 688136 | tf_op jit(solution)/shard_map/ppermute | solution.py:46
  36.1 10.8 %collective-permute-start.12 = (bf16[128,896]{1,0:T(8,128)(2,1)S(1)}, bf16[128,896]{1,0:T(8,128)(2,1)S(1)}, u32[]{:S(2)}, u32[]{:S(2)}) collective-permute-start(bf16[128,896]{1,0:T(8,128)(2,1)S(1)} %get-tuple-element.51), channel_id=1, source_target_pairs={{0,192},{1,49},{2,194},{3,51},{4,196},{5,53},{6,198},{7,55},{8,200... | collective-permute-start | bytes 688136 | tf_op jit(solution)/shard_map/ppermute | solution.py:46
  39.8 2.3 %collective-permute-start.9 = (bf16[256,256]{1,0:T(8,128)(2,1)S(1)}, bf16[256,256]{1,0:T(8,128)(2,1)S(1)}, u32[]{:S(2)}, u32[]{:S(2)}) collective-permute-start(bf16[256,256]{1,0:T(8,128)(2,1)S(1)} %shard_map.100.mine), channel_id=1, source_target_pairs={{0,1},{1,0},{2,3},{3,2},{4,5},{5,4},{6,7},{7,6},{8,9},{9,8},{10,11... | collective-permute-start | bytes 393224 | tf_op jit(solution)/shard_map/ppermute | solution.py:341
  41.3 11.8 %collective-permute-start.17 = (bf16[1344,256]{1,0:T(8,128)(2,1)S(1)}, bf16[1344,256]{1,0:T(8,128)(2,1)S(1)}, u32[]{:S(2)}, u32[]{:S(2)}) collective-permute-start(bf16[1344,256]{1,0:T(8,128)(2,1)S(1)} %get-tuple-element.58), channel_id=1, source_target_pairs={{0,16},{1,65},{2,18},{3,67},{4,20},{5,69},{6,22},{7,71},{8,24},{9,... | collective-permute-start | bytes 2064392 | tf_op jit(solution)/shard_map/ppermute | solution.py:46
  42.1 11.0 %collective-permute-start.19 = (bf16[1344,256]{1,0:T(8,128)(2,1)S(1)}, bf16[1344,256]{1,0:T(8,128)(2,1)S(1)}, u32[]{:S(2)}, u32[]{:S(2)}) collective-permute-start(bf16[1344,256]{1,0:T(8,128)(2,1)S(1)} %get-tuple-element.60), channel_id=1, source_target_pairs={{0,48},{1,193},{2,50},{3,195},{4,52},{5,197},{6,54},{7,199},{8,56}... | collective-permute-start | bytes 2064392 | tf_op jit(solution)/shard_map/ppermute | solution.py:46
  44.1 11.4 %collective-permute-start.18 = (bf16[512,256]{1,0:T(8,128)(2,1)S(1)}, bf16[512,256]{1,0:T(8,128)(2,1)S(1)}, u32[]{:S(2)}, u32[]{:S(2)}) collective-permute-start(bf16[512,256]{1,0:T(8,128)(2,1)S(1)} %shard_map.101.refs_5_), channel_id=1, source_target_pairs={{0,16},{1,65},{2,18},{3,67},{4,20},{5,69},{6,22},{7,71},{8,24},{9,... | collective-permute-start | bytes 786440 | tf_op jit(solution)/shard_map/ppermute | solution.py:46
  44.2 11.3 %collective-permute-start.20 = (bf16[512,256]{1,0:T(8,128)(2,1)S(1)}, bf16[512,256]{1,0:T(8,128)(2,1)S(1)}, u32[]{:S(2)}, u32[]{:S(2)}) collective-permute-start(bf16[512,256]{1,0:T(8,128)(2,1)S(1)} %shard_map.101.refs_5_), channel_id=1, source_target_pairs={{0,48},{1,193},{2,50},{3,195},{4,52},{5,197},{6,54},{7,199},{8,56}... | collective-permute-start | bytes 786440 | tf_op jit(solution)/shard_map/ppermute | solution.py:46
  47.0 13.8 %collective-permute-start.13 = (bf16[128,896]{1,0:T(8,128)(2,1)S(1)}, bf16[128,896]{1,0:T(8,128)(2,1)S(1)}, u32[]{:S(2)}, u32[]{:S(2)}) collective-permute-start(bf16[128,896]{1,0:T(8,128)(2,1)S(1)} %shard_map.103), channel_id=1, source_target_pairs={{0,8},{8,0},{1,9},{9,1},{2,10},{10,2},{3,11},{11,3},{4,12},{12,4},... | collective-permute-start | bytes 688136 | tf_op jit(solution)/shard_map/ppermute | solution.py:341
  55.6 15.1 %collective-permute-start.21 = (bf16[704,256]{1,0:T(8,128)(2,1)S(1)}, bf16[704,256]{1,0:T(8,128)(2,1)S(1)}, u32[]{:S(2)}, u32[]{:S(2)}) collective-permute-start(bf16[704,256]{1,0:T(8,128)(2,1)S(1)} %get-tuple-element.61), channel_id=1, source_target_pairs={{0,16},{1,65},{2,18},{3,67},{4,20},{5,69},{6,22},{7,71},{8,24},{9,... | collective-permute-start | bytes 1081352 | tf_op jit(solution)/shard_map/ppermute | solution.py:46
  55.6 15.1 %copy-start.7 = (s32[2]{0:T(128)S(1)}, s32[2]{0:T(128)}, u32[]{:S(2)}) copy-start(s32[2]{0:T(128)} %pick.1) | copy-start | bytes 28
  55.7 15.1 %copy-start.8 = (f32[16]{0:T(128)S(1)}, f32[16]{0:T(128)}, u32[]{:S(2)}) copy-start(f32[16]{0:T(128)} %grid.1) | copy-start | bytes 196
  55.7 15.0 %collective-permute-start.22 = (bf16[704,256]{1,0:T(8,128)(2,1)S(1)}, bf16[704,256]{1,0:T(8,128)(2,1)S(1)}, u32[]{:S(2)}, u32[]{:S(2)}) collective-permute-start(bf16[704,256]{1,0:T(8,128)(2,1)S(1)} %get-tuple-element.62), channel_id=1, source_target_pairs={{0,48},{1,193},{2,50},{3,195},{4,52},{5,197},{6,54},{7,199},{8,56}... | collective-permute-start | bytes 1081352 | tf_op jit(solution)/shard_map/ppermute | solution.py:46
  60.8 7.6 %collective-permute-start.14 = (bf16[128,896]{1,0:T(8,128)(2,1)S(1)}, bf16[128,896]{1,0:T(8,128)(2,1)S(1)}, u32[]{:S(2)}, u32[]{:S(2)}) collective-permute-start(bf16[128,896]{1,0:T(8,128)(2,1)S(1)} %shard_map.104.refs_0_), channel_id=1, source_target_pairs={{0,128},{1,33},{2,130},{3,35},{4,132},{5,37},{6,134},{7,39},{8,136... | collective-permute-start | bytes 688136 | tf_op jit(solution)/shard_map/ppermute | solution.py:46
  62.4 8.3 %collective-permute-start.15 = (bf16[128,896]{1,0:T(8,128)(2,1)S(1)}, bf16[128,896]{1,0:T(8,128)(2,1)S(1)}, u32[]{:S(2)}, u32[]{:S(2)}) collective-permute-start(bf16[128,896]{1,0:T(8,128)(2,1)S(1)} %shard_map.104.refs_0_), channel_id=1, source_target_pairs={{0,64},{1,17},{2,66},{3,19},{4,68},{5,21},{6,70},{7,23},{8,72},{9,... | collective-permute-start | bytes 688136 | tf_op jit(solution)/shard_map/ppermute | solution.py:46
  62.9 7.8 %collective-permute-start.16 = (bf16[128,896]{1,0:T(8,128)(2,1)S(1)}, bf16[128,896]{1,0:T(8,128)(2,1)S(1)}, u32[]{:S(2)}, u32[]{:S(2)}) collective-permute-start(bf16[128,896]{1,0:T(8,128)(2,1)S(1)} %shard_map.104.refs_0_), channel_id=1, source_target_pairs={{0,192},{1,49},{2,194},{3,51},{4,196},{5,53},{6,198},{7,55},{8,200... | collective-permute-start | bytes 688136 | tf_op jit(solution)/shard_map/ppermute | solution.py:46

commit v5 on v4

--- a/solution.py
+++ b/solution.py
@@ -264,23 +264,21 @@
     )(me.reshape(1), mine, other)
 
 
-def onward_kernel(low, in_low, high, in_high, up, down):
-    part = in_low.shape[0] // 2
-    half = up.shape[0] - part
-    for n, (eig, rot_in, dst) in enumerate(((low, in_low, up), (high, in_high, down))):
-        dst[:part, :] = rot_in[n * part : (n + 1) * part, :]
-        dst[part:, :] = eig[2 * half :, :]
-
-
-def onward(low, in_low, high, in_high):
-    out = jax.ShapeDtypeStruct((low.shape[0] // 3 + in_low.shape[0] // 2, low.shape[1]), low.dtype)
-    return pl.pallas_call(
-        onward_kernel,
-        in_specs=[VMEM] * 4,
-        out_specs=[VMEM] * 2,
-        out_shape=[out] * 2,
+def onward_kernel(n, eig, rot_in, out):
+    part = rot_in.shape[0] // 2
+    out[:part, :] = rot_in[n * part : (n + 1) * part, :]
+    out[part:, :] = eig[eig.shape[0] - out.shape[0] + part :, :]
+
+
+def onward(n, eig, rot_in):
+    rows = eig.shape[0] // 3 + rot_in.shape[0] // 2
+    return pl.pallas_call(
+        functools.partial(onward_kernel, n),
+        in_specs=[VMEM] * 2,
+        out_specs=VMEM,
+        out_shape=jax.ShapeDtypeStruct((rows, eig.shape[1]), eig.dtype),
         **params(8, 0.1),
-    )(low, in_low, high, in_high)
+    )(eig, rot_in)
 
 
 def score_kernel(me, pick, grid, *refs):
@@ -368,9 +366,9 @@
     in_half = add(BF, in_half, tie(far_half, send[0]))
     rot_in = join(c, in_half, swap(in_half, "c", 1))
     in_low, in_high = move(rot_in, FIRST[1]), move(rot_in, FIRST[3])
-    total = add(F32, tie(keep, rot_in), *got, us=8)
+    total = add(F32, keep, *got, us=8)
     near = add(BF, total)
-    up, down = onward(low, in_low, high, in_high)
+    up, down = onward(0, low, in_low), onward(1, high, in_high)
     messages = low, in_low, high, in_high, move(up, FIRST[1]), move(down, FIRST[3])
     total = add(BF, total, swap(near, "zh", 1), us=4)
     pieces = [total] + [move(total, SECOND[k]) for k in HOPS]

time: 99.4 us -> 99.4 us (level)
  transfers between devices with their start and end apart: 23 -> 23, of which waited for: 7 -> 7; matrix products, arithmetic and copies ran while one was open for 0% -> 0% of each run, Pallas kernels for 7% -> 8%
where the time goes in v5:
time: 99.4 us; the launch traced here: 99.2 us
  starting transfers between devices  40.1 us (40%)
  blocking collectives  25.3 us (25%)
  Pallas kernels  14.9 us (15%)
  waiting for transfers between devices  13.1 us (13%)
  local copies, waits for them, and re-layouts  4.9 us (5%)
    ppermute x18, starting transfers between devices, move(): return lax.ppermute(value, ALL, pairs)  24.7 us
    all_to_all x1, blocking collectives, body(): lax.all_to_all(part, ('zh', 'zl', 'c'), 0, 0, tiled=True)  15.8 us
    ppermute x5, starting transfers between devices, swap(): return lax.ppermute(value, axis, [(i, i ^ bit) for i in range(size)])  15.4 us
    all_to_all x1, blocking collectives, body(): return jnp.sum(lax.all_to_all(over, ('y', 'x'), 0, 0, tiled=True), axis=0)  9.48 us
    ppermute x18, waiting for transfers between devices, move(): return lax.ppermute(value, ALL, pairs)  7.37 us
    ppermute x5, waiting for transfers between devices, swap(): return lax.ppermute(value, axis, [(i, i ^ bit) for i in range(size)])  5.71 us
    pallas_call x1, Pallas kernels, lead_mm(): pl.pallas_call(functools.partial(lead_kernel, hops), in_specs=[SMEM, hbm,...  5.11 us
    unnamed x18, local copies, waits for them, and re-layouts  4.88 us
  transfers between devices with their start and end apart: 23, of which 7 were waited for; matrix products, arithmetic and copies ran while one was open for 0% of the time, Pallas kernels for 8%

profile of v5, /device:TPU:1, one launch (start us, length us, event | category | flops | bytes accessed | tf_op | source)
XLA Modules:
  0.0 99.2 jit_solution(6977848924588287317)
XLA Ops:
  0.0 4.4 %shard_map.91 = (bf16[256,896]{1,0:T(8,128)(2,1)}, bf16[256,896]{1,0:T(8,128)(2,1)}, f32[256,256]{1,0:T(8,128)}, f32[256,256]{1,0:T(8,128)}) custom-call(s32[1]{0:T(128)} %bitcast.1.at, s32[1]{0:T(128)} %bitcast.2.core_at.at, bf16[256,896]{1,0:T(8,128)(2,1)} %q_ref.1, bf16[256,896]{1,0:T(8,128)(2,1)} %t_ref.1, bf16[896,3584]{1,0:T(8,128)(2,1)} %b_ref.1, ...), custom_call_target="tpu_custom_call" | custom-call | flops 5175000064 | tf_op jit(solution)/shard_map/pallas_call | solution.py:122
  4.4 2.2 %collective-permute-start = (bf16[256,896]{1,0:T(8,128)(2,1)}, bf16[256,896]{1,0:T(8,128)(2,1)S(1)}, u32[]{:S(2)}, u32[]{:S(2)}) collective-permute-start(bf16[256,896]{1,0:T(8,128)(2,1)} %get-tuple-element.31), channel_id=1, source_target_pairs={{0,16},{1,65},{2,18},{3,67},{4,20},{5,69},{6,22},{7,71},{8,24},{9,... | collective-permute-start | bytes 1376264 | tf_op jit(solution)/shard_map/ppermute | solution.py:46
  6.6 1.5 %collective-permute-start.1 = (bf16[256,896]{1,0:T(8,128)(2,1)}, bf16[256,896]{1,0:T(8,128)(2,1)S(1)}, u32[]{:S(2)}, u32[]{:S(2)}) collective-permute-start(bf16[256,896]{1,0:T(8,128)(2,1)} %get-tuple-element.35), channel_id=1, source_target_pairs={{0,48},{1,193},{2,50},{3,195},{4,52},{5,197},{6,54},{7,199},{8,56}... | collective-permute-start | bytes 1376264 | tf_op jit(solution)/shard_map/ppermute | solution.py:46
  8.1 2.8 %collective-permute-start.13 = (f32[256,256]{1,0:T(8,128)}, f32[256,256]{1,0:T(8,128)S(1)}, u32[]{:S(2)}, u32[]{:S(2)}) collective-permute-start(f32[256,256]{1,0:T(8,128)} %get-tuple-element.48), channel_id=1, source_target_pairs={{0,1},{1,0},{2,3},{3,2},{4,5},{5,4},{6,7},{7,6},{8,9},{9,8},{10,11... | collective-permute-start | bytes 786440 | tf_op jit(solution)/shard_map/ppermute | solution.py:339
  11.0 5.1 %shard_map.92 = (bf16[256,896]{1,0:T(8,128)(2,1)}, bf16[256,896]{1,0:T(8,128)(2,1)}, bf16[256,896]{1,0:T(8,128)(2,1)}, bf16[256,896]{1,0:T(8,128)(2,1)}) custom-call(s32[1]{0:T(128)} %bitcast.3.at, bf16[256,896]{1,0:T(8,128)(2,1)} %q_ref.1, bf16[256,896]{1,0:T(8,128)(2,1)} %t_ref.1, bf16[896,3584]{1,0:T(8,128)(2,1)} %b_ref.1), custom_call_target="tpu_custom_call" | custom-call | flops 5750000128 | tf_op jit(solution)/shard_map/pallas_call | solution.py:81
  16.1 1.1 %collective-permute-start.3 = (bf16[256,896]{1,0:T(8,128)(2,1)}, bf16[256,896]{1,0:T(8,128)(2,1)S(1)}, u32[]{:S(2)}, u32[]{:S(2)}) collective-permute-start(bf16[256,896]{1,0:T(8,128)(2,1)} %get-tuple-element.39), channel_id=1, source_target_pairs={{0,48},{1,193},{2,50},{3,195},{4,52},{5,197},{6,54},{7,199},{8,56}... | collective-permute-start | bytes 1376264 | tf_op jit(solution)/shard_map/ppermute | solution.py:46
  17.6 1.0 %copy-done.2 = bf16[256,896]{1,0:T(8,128)(2,1)S(1)} copy-done((bf16[256,896]{1,0:T(8,128)(2,1)S(1)}, bf16[256,896]{1,0:T(8,128)(2,1)}, u32[]{:S(2)}) %copy-start.2) | copy-done | bytes 458776
  18.9 1.0 %copy-done.1 = bf16[256,896]{1,0:T(8,128)(2,1)S(1)} copy-done((bf16[256,896]{1,0:T(8,128)(2,1)S(1)}, bf16[256,896]{1,0:T(8,128)(2,1)}, u32[]{:S(2)}) %copy-start.1) | copy-done | bytes 458776
  20.0 2.7 %collective-permute-start.5 = (bf16[256,896]{1,0:T(8,128)(2,1)S(1)}, bf16[256,896]{1,0:T(8,128)(2,1)S(1)}, u32[]{:S(2)}, u32[]{:S(2)}) collective-permute-start(bf16[256,896]{1,0:T(8,128)(2,1)S(1)} %shard_map.94), channel_id=1, source_target_pairs={{0,48},{1,193},{2,50},{3,195},{4,52},{5,197},{6,54},{7,199},{8,56}... | collective-permute-start | bytes 1376264 | tf_op jit(solution)/shard_map/ppermute | solution.py:46
  22.8 1.3 %collective-permute-start.14 = (f32[256,256]{1,0:T(8,128)S(1)}, f32[256,256]{1,0:T(8,128)S(1)}, u32[]{:S(2)}, u32[]{:S(2)}) collective-permute-start(f32[256,256]{1,0:T(8,128)S(1)} %shard_map.101.refs_0_), channel_id=1, source_target_pairs={{0,2},{2,0},{4,6},{6,4},{1,3},{3,1},{5,7},{7,5},{8,10},{10,8},{12,... | collective-permute-start | bytes 786440 | tf_op jit(solution)/shard_map/ppermute | solution.py:339
  24.0 2.8 %copy-done.4 = bf16[896,3584]{1,0:T(8,128)(2,1)S(1)} copy-done((bf16[896,3584]{1,0:T(8,128)(2,1)S(1)}, bf16[896,3584]{1,0:T(8,128)(2,1)}, u32[]{:S(2)}) %copy-start.4) | copy-done | bytes 6422552
  26.9 1.2 %shard_map.95 = (f32[256,896]{1,0:T(8,128)S(1)}, f32[256,896]{1,0:T(8,128)S(1)}) custom-call(s32[1]{0:T(128)} %bitcast.4.at, bf16[256,896]{1,0:T(8,128)(2,1)S(1)} %copy-done.5, bf16[256,896]{1,0:T(8,128)(2,1)S(1)} %copy-done.6, bf16[896,3584]{1,0:T(8,128)(2,1)S(1)} %copy-done.4), custom_call_target="tpu_custom_call" | custom-call | flops 4600000000 | tf_op jit(solution)/shard_map/pallas_call | solution.py:153
  28.1 1.6 %collective-permute-done.14.refs_1_ = f32[256,256]{1,0:T(8,128)S(1)} collective-permute-done((f32[256,256]{1,0:T(8,128)S(1)}, f32[256,256]{1,0:T(8,128)S(1)}, u32[]{:S(2)}, u32[]{:S(2)}) %collective-permute-start.14) | collective-permute-done | bytes 262176 | tf_op jit(solution)/shard_map/ppermute | solution.py:339
  29.8 3.9 %collective-permute-start.15 = (bf16[256,256]{1,0:T(8,128)(2,1)S(1)}, bf16[256,256]{1,0:T(8,128)(2,1)S(1)}, u32[]{:S(2)}, u32[]{:S(2)}) collective-permute-start(bf16[256,256]{1,0:T(8,128)(2,1)S(1)} %shard_map.103), channel_id=1, source_target_pairs={{0,4},{2,6},{4,0},{6,2},{1,5},{3,7},{5,1},{7,3},{8,12},{10,14},{12... | collective-permute-start | bytes 393224 | tf_op jit(solution)/shard_map/ppermute | solution.py:339
  34.1 2.0 %collective-permute-start.6 = (bf16[128,896]{1,0:T(8,128)(2,1)S(1)}, bf16[128,896]{1,0:T(8,128)(2,1)S(1)}, u32[]{:S(2)}, u32[]{:S(2)}) collective-permute-start(bf16[128,896]{1,0:T(8,128)(2,1)S(1)} %get-tuple-element.42), channel_id=1, source_target_pairs={{0,128},{1,33},{2,130},{3,35},{4,132},{5,37},{6,134},{7,39},{8,136... | collective-permute-start | bytes 688136 | tf_op jit(solution)/shard_map/ppermute | solution.py:46
  36.1 2.7 %collective-permute-start.8 = (bf16[128,896]{1,0:T(8,128)(2,1)S(1)}, bf16[128,896]{1,0:T(8,128)(2,1)S(1)}, u32[]{:S(2)}, u32[]{:S(2)}) collective-permute-start(bf16[128,896]{1,0:T(8,128)(2,1)S(1)} %get-tuple-element.44), channel_id=1, source_target_pairs={{0,192},{1,49},{2,194},{3,51},{4,196},{5,53},{6,198},{7,55},{8,200... | collective-permute-start | bytes 688136 | tf_op jit(solution)/shard_map/ppermute | solution.py:46
  38.8 1.0 collective-permute-done.15.refs_1_
  39.8 1.3 %collective-permute-start.16 = (bf16[256,256]{1,0:T(8,128)(2,1)S(1)}, bf16[256,256]{1,0:T(8,128)(2,1)S(1)}, u32[]{:S(2)}, u32[]{:S(2)}) collective-permute-start(bf16[256,256]{1,0:T(8,128)(2,1)S(1)} %shard_map.104.mine), channel_id=1, source_target_pairs={{0,1},{1,0},{2,3},{3,2},{4,5},{5,4},{6,7},{7,6},{8,9},{9,8},{10,11... | collective-permute-start | bytes 393224 | tf_op jit(solution)/shard_map/ppermute | solution.py:339
  41.4 0.7 collective-permute-done.16.other
  42.1 2.0 %collective-permute-start.19 = (bf16[1344,256]{1,0:T(8,128)(2,1)S(1)}, bf16[1344,256]{1,0:T(8,128)(2,1)S(1)}, u32[]{:S(2)}, u32[]{:S(2)}) collective-permute-start(bf16[1344,256]{1,0:T(8,128)(2,1)S(1)} %get-tuple-element.56), channel_id=1, source_target_pairs={{0,48},{1,193},{2,50},{3,195},{4,52},{5,197},{6,54},{7,199},{8,56}... | collective-permute-start | bytes 2064392 | tf_op jit(solution)/shard_map/ppermute | solution.py:46
  44.2 2.7 %collective-permute-start.20 = (bf16[512,256]{1,0:T(8,128)(2,1)S(1)}, bf16[512,256]{1,0:T(8,128)(2,1)S(1)}, u32[]{:S(2)}, u32[]{:S(2)}) collective-permute-start(bf16[512,256]{1,0:T(8,128)(2,1)S(1)} %shard_map.105.refs_5_), channel_id=1, source_target_pairs={{0,48},{1,193},{2,50},{3,195},{4,52},{5,197},{6,54},{7,199},{8,56}... | collective-permute-start | bytes 786440 | tf_op jit(solution)/shard_map/ppermute | solution.py:46
  47.0 6.1 %collective-permute-start.9 = (bf16[128,896]{1,0:T(8,128)(2,1)S(1)}, bf16[128,896]{1,0:T(8,128)(2,1)S(1)}, u32[]{:S(2)}, u32[]{:S(2)}) collective-permute-start(bf16[128,896]{1,0:T(8,128)(2,1)S(1)} %shard_map.98), channel_id=1, source_target_pairs={{0,8},{8,0},{1,9},{9,1},{2,10},{10,2},{3,11},{11,3},{4,12},{12,4},... | collective-permute-start | bytes 688136 | tf_op jit(solution)/shard_map/ppermute | solution.py:339
  53.1 2.4 %collective-permute-done.18.rot_in.refs_7_ = bf16[512,256]{1,0:T(8,128)(2,1)S(1)} collective-permute-done((bf16[512,256]{1,0:T(8,128)(2,1)S(1)}, bf16[512,256]{1,0:T(8,128)(2,1)S(1)}, u32[]{:S(2)}, u32[]{:S(2)}) %collective-permute-start.18) | collective-permute-done | bytes 262176 | tf_op jit(solution)/shard_map/ppermute | solution.py:46
  55.7 2.7 %collective-permute-start.22 = (bf16[704,256]{1,0:T(8,128)(2,1)S(1)}, bf16[704,256]{1,0:T(8,128)(2,1)S(1)}, u32[]{:S(2)}, u32[]{:S(2)}) collective-permute-start(bf16[704,256]{1,0:T(8,128)(2,1)S(1)} %shard_map.108), channel_id=1, source_target_pairs={{0,48},{1,193},{2,50},{3,195},{4,52},{5,197},{6,54},{7,199},{8,56}... | collective-permute-start | bytes 1081352 | tf_op jit(solution)/shard_map/ppermute | solution.py:46
  58.4 2.4 %collective-permute-done.9.refs_1_ = bf16[128,896]{1,0:T(8,128)(2,1)S(1)} collective-permute-done((bf16[128,896]{1,0:T(8,128)(2,1)S(1)}, bf16[128,896]{1,0:T(8,128)(2,1)S(1)}, u32[]{:S(2)}, u32[]{:S(2)}) %collective-permute-start.9) | collective-permute-done | bytes 229408 | tf_op jit(solution)/shard_map/ppermute | solution.py:339
  60.9 1.6 %collective-permute-start.10 = (bf16[128,896]{1,0:T(8,128)(2,1)S(1)}, bf16[128,896]{1,0:T(8,128)(2,1)S(1)}, u32[]{:S(2)}, u32[]{:S(2)}) collective-permute-start(bf16[128,896]{1,0:T(8,128)(2,1)S(1)} %shard_map.99.refs_0_), channel_id=1, source_target_pairs={{0,128},{1,33},{2,130},{3,35},{4,132},{5,37},{6,134},{7,39},{8,136... | collective-permute-start | bytes 688136 | tf_op jit(solution)/shard_map/ppermute | solution.py:46
  63.0 2.2 %collective-permute-start.12 = (bf16[128,896]{1,0:T(8,128)(2,1)S(1)}, bf16[128,896]{1,0:T(8,128)(2,1)S(1)}, u32[]{:S(2)}, u32[]{:S(2)}) collective-permute-start(bf16[128,896]{1,0:T(8,128)(2,1)S(1)} %shard_map.99.refs_0_), channel_id=1, source_target_pairs={{0,192},{1,49},{2,194},{3,51},{4,196},{5,53},{6,198},{7,55},{8,200... | collective-permute-start | bytes 688136 | tf_op jit(solution)/shard_map/ppermute | solution.py:46
  65.2 2.3 %collective-permute-done.10.refs_1_ = bf16[128,896]{1,0:T(8,128)(2,1)S(1)} collective-permute-done((bf16[128,896]{1,0:T(8,128)(2,1)S(1)}, bf16[128,896]{1,0:T(8,128)(2,1)S(1)}, u32[]{:S(2)}, u32[]{:S(2)}) %collective-permute-start.10) | collective-permute-done | bytes 229408 | tf_op jit(solution)/shard_map/ppermute | solution.py:46
  67.5 2.6 %collective-permute-done.11.refs_2_ = bf16[128,896]{1,0:T(8,128)(2,1)S(1)} collective-permute-done((bf16[128,896]{1,0:T(8,128)(2,1)S(1)}, bf16[128,896]{1,0:T(8,128)(2,1)S(1)}, u32[]{:S(2)}, u32[]{:S(2)}) %collective-permute-start.11) | collective-permute-done | bytes 229408 | tf_op jit(solution)/shard_map/ppermute | solution.py:46
  70.2 3.0 %shard_map.109 = f32[16,2,256]{2,1,0:T(2,128)S(1)} custom-call(s32[1]{0:T(128)} %bitcast.at.me, s32[2]{0:T(128)S(1)} %copy-done.7, f32[16]{0:T(128)S(1)} %copy-done.8, bf16[128,896]{1,0:T(8,128)(2,1)S(1)} %shard_map.99.refs_0_, bf16[128,896]{1,0:T(8,128)(2,1)S(1)} %collective-permute-done.10.refs_1_, bf16[128,896]{1,0:T(8,128)(2,1)S(1)} %collective-permute-done.11.refs_2_, ...), custom_call_target="tpu_custom_call" | custom-call | flops 3449999872 | tf_op jit(solution)/shard_map/pallas_call | solution.py:317
  73.2 15.8 %all_to_all.10 = f32[16,2,256]{2,1,0:T(2,128)S(1)} all-to-all(f32[16,2,256]{2,1,0:T(2,128)S(1)} %shard_map.109), channel_id=1, replica_groups=mesh['y'=4,'x'=4,'zh'=2,'zl'=4,'c'=2] {'zh','zl','c'}, dimensions={0} | all-to-all | bytes 65536 | tf_op jit(solution)/shard_map/all_to_all | solution.py:377
  89.1 9.5 %all_to_all.11 = f32[16,2,256]{2,1,0:T(2,128)S(1)} all-to-all(f32[16,2,256]{2,1,0:T(2,128)S(1)} %broadcast_in_dim.2), channel_id=1, replica_groups=mesh['y'=4,'x'=4,'zh'=2,'zl'=4,'c'=2] {'y','x'}, dimensions={0} | all-to-all | bytes 65536 | tf_op jit(solution)/shard_map/all_to_all | solution.py:379
  (56 shorter events, 3.1 us)
Async XLA Ops:
  4.4 13.2 %collective-permute-start = (bf16[256,896]{1,0:T(8,128)(2,1)}, bf16[256,896]{1,0:T(8,128)(2,1)S(1)}, u32[]{:S(2)}, u32[]{:S(2)}) collective-permute-start(bf16[256,896]{1,0:T(8,128)(2,1)} %get-tuple-element.31), channel_id=1, source_target_pairs={{0,16},{1,65},{2,18},{3,67},{4,20},{5,69},{6,22},{7,71},{8,24},{9,... | collective-permute-start | bytes 1376264 | tf_op jit(solution)/shard_map/ppermute | solution.py:46
  6.6 12.3 %collective-permute-start.1 = (bf16[256,896]{1,0:T(8,128)(2,1)}, bf16[256,896]{1,0:T(8,128)(2,1)S(1)}, u32[]{:S(2)}, u32[]{:S(2)}) collective-permute-start(bf16[256,896]{1,0:T(8,128)(2,1)} %get-tuple-element.35), channel_id=1, source_target_pairs={{0,48},{1,193},{2,50},{3,195},{4,52},{5,197},{6,54},{7,199},{8,56}... | collective-permute-start | bytes 1376264 | tf_op jit(solution)/shard_map/ppermute | solution.py:46
  8.1 14.6 %collective-permute-start.13 = (f32[256,256]{1,0:T(8,128)}, f32[256,256]{1,0:T(8,128)S(1)}, u32[]{:S(2)}, u32[]{:S(2)}) collective-permute-start(f32[256,256]{1,0:T(8,128)} %get-tuple-element.48), channel_id=1, source_target_pairs={{0,1},{1,0},{2,3},{3,2},{4,5},{5,4},{6,7},{7,6},{8,9},{9,8},{10,11... | collective-permute-start | bytes 786440 | tf_op jit(solution)/shard_map/ppermute | solution.py:339
  11.0 11.8 %copy-start.3 = (f32[256,256]{1,0:T(8,128)S(1)}, f32[256,256]{1,0:T(8,128)}, u32[]{:S(2)}) copy-start(f32[256,256]{1,0:T(8,128)} %get-tuple-element.47.refs_0_) | copy-start | bytes 786436
  11.0 13.1 %copy-start.5 = (bf16[256,896]{1,0:T(8,128)(2,1)S(1)}, bf16[256,896]{1,0:T(8,128)(2,1)}, u32[]{:S(2)}) copy-start(bf16[256,896]{1,0:T(8,128)(2,1)} %q_ref.1) | copy-start | bytes 1376260
  11.0 13.1 %copy-start.6 = (bf16[256,896]{1,0:T(8,128)(2,1)S(1)}, bf16[256,896]{1,0:T(8,128)(2,1)}, u32[]{:S(2)}) copy-start(bf16[256,896]{1,0:T(8,128)(2,1)} %t_ref.1) | copy-start | bytes 1376260
  16.1 17.7 %collective-permute-start.3 = (bf16[256,896]{1,0:T(8,128)(2,1)}, bf16[256,896]{1,0:T(8,128)(2,1)S(1)}, u32[]{:S(2)}, u32[]{:S(2)}) collective-permute-start(bf16[256,896]{1,0:T(8,128)(2,1)} %get-tuple-element.39), channel_id=1, source_target_pairs={{0,48},{1,193},{2,50},{3,195},{4,52},{5,197},{6,54},{7,199},{8,56}... | collective-permute-start | bytes 1376264 | tf_op jit(solution)/shard_map/ppermute | solution.py:46
  17.2 16.6 %collective-permute-start.4 = (bf16[256,896]{1,0:T(8,128)(2,1)}, bf16[256,896]{1,0:T(8,128)(2,1)S(1)}, u32[]{:S(2)}, u32[]{:S(2)}) collective-permute-start(bf16[256,896]{1,0:T(8,128)(2,1)} %get-tuple-element.40), channel_id=1, source_target_pairs={{0,16},{1,65},{2,18},{3,67},{4,20},{5,69},{6,22},{7,71},{8,24},{9,... | collective-permute-start | bytes 1376264 | tf_op jit(solution)/shard_map/ppermute | solution.py:46
  17.6 1.0 %copy-start.2 = (bf16[256,896]{1,0:T(8,128)(2,1)S(1)}, bf16[256,896]{1,0:T(8,128)(2,1)}, u32[]{:S(2)}) copy-start(bf16[256,896]{1,0:T(8,128)(2,1)} %get-tuple-element.33.refs_0_) | copy-start | bytes 1376260
  18.8 15.0 %collective-permute-start.2 = (bf16[256,896]{1,0:T(8,128)(2,1)S(1)}, bf16[256,896]{1,0:T(8,128)(2,1)S(1)}, u32[]{:S(2)}, u32[]{:S(2)}) collective-permute-start(bf16[256,896]{1,0:T(8,128)(2,1)S(1)} %shard_map.93), channel_id=1, source_target_pairs={{0,16},{1,65},{2,18},{3,67},{4,20},{5,69},{6,22},{7,71},{8,24},{9,... | collective-permute-start | bytes 1376264 | tf_op jit(solution)/shard_map/ppermute | solution.py:46
  18.9 1.0 %copy-start.1 = (bf16[256,896]{1,0:T(8,128)(2,1)S(1)}, bf16[256,896]{1,0:T(8,128)(2,1)}, u32[]{:S(2)}) copy-start(bf16[256,896]{1,0:T(8,128)(2,1)} %get-tuple-element.34.refs_0_) | copy-start | bytes 1376260
  20.0 13.8 %collective-permute-start.5 = (bf16[256,896]{1,0:T(8,128)(2,1)S(1)}, bf16[256,896]{1,0:T(8,128)(2,1)S(1)}, u32[]{:S(2)}, u32[]{:S(2)}) collective-permute-start(bf16[256,896]{1,0:T(8,128)(2,1)S(1)} %shard_map.94), channel_id=1, source_target_pairs={{0,48},{1,193},{2,50},{3,195},{4,52},{5,197},{6,54},{7,199},{8,56}... | collective-permute-start | bytes 1376264 | tf_op jit(solution)/shard_map/ppermute | solution.py:46
  22.8 7.0 %collective-permute-start.14 = (f32[256,256]{1,0:T(8,128)S(1)}, f32[256,256]{1,0:T(8,128)S(1)}, u32[]{:S(2)}, u32[]{:S(2)}) collective-permute-start(f32[256,256]{1,0:T(8,128)S(1)} %shard_map.101.refs_0_), channel_id=1, source_target_pairs={{0,2},{2,0},{4,6},{6,4},{1,3},{3,1},{5,7},{7,5},{8,10},{10,8},{12,... | collective-permute-start | bytes 786440 | tf_op jit(solution)/shard_map/ppermute | solution.py:339
  24.0 2.8 %copy-start.4 = (bf16[896,3584]{1,0:T(8,128)(2,1)S(1)}, bf16[896,3584]{1,0:T(8,128)(2,1)}, u32[]{:S(2)}) copy-start(bf16[896,3584]{1,0:T(8,128)(2,1)} %b_ref.1) | copy-start | bytes 19267588
  28.1 13.0 %copy-start = (bf16[3584,256]{1,0:T(8,128)(2,1)S(1)}, bf16[3584,256]{1,0:T(8,128)(2,1)}, u32[]{:S(2)}) copy-start(bf16[3584,256]{1,0:T(8,128)(2,1)} %refs_3_.1) | copy-start | bytes 5505028
  29.8 9.9 %collective-permute-start.15 = (bf16[256,256]{1,0:T(8,128)(2,1)S(1)}, bf16[256,256]{1,0:T(8,128)(2,1)S(1)}, u32[]{:S(2)}, u32[]{:S(2)}) collective-permute-start(bf16[256,256]{1,0:T(8,128)(2,1)S(1)} %shard_map.103), channel_id=1, source_target_pairs={{0,4},{2,6},{4,0},{6,2},{1,5},{3,7},{5,1},{7,3},{8,12},{10,14},{12... | collective-permute-start | bytes 393224 | tf_op jit(solution)/shard_map/ppermute | solution.py:339
  34.1 10.0 %collective-permute-start.6 = (bf16[128,896]{1,0:T(8,128)(2,1)S(1)}, bf16[128,896]{1,0:T(8,128)(2,1)S(1)}, u32[]{:S(2)}, u32[]{:S(2)}) collective-permute-start(bf16[128,896]{1,0:T(8,128)(2,1)S(1)} %get-tuple-element.42), channel_id=1, source_target_pairs={{0,128},{1,33},{2,130},{3,35},{4,132},{5,37},{6,134},{7,39},{8,136... | collective-permute-start | bytes 688136 | tf_op jit(solution)/shard_map/ppermute | solution.py:46
  36.1 8.1 %collective-permute-start.7 = (bf16[128,896]{1,0:T(8,128)(2,1)S(1)}, bf16[128,896]{1,0:T(8,128)(2,1)S(1)}, u32[]{:S(2)}, u32[]{:S(2)}) collective-permute-start(bf16[128,896]{1,0:T(8,128)(2,1)S(1)} %get-tuple-element.43), channel_id=1, source_target_pairs={{0,64},{1,17},{2,66},{3,19},{4,68},{5,21},{6,70},{7,23},{8,72},{9,... | collective-permute-start | bytes 688136 | tf_op jit(solution)/shard_map/ppermute | solution.py:46
  36.1 10.8 %collective-permute-start.8 = (bf16[128,896]{1,0:T(8,128)(2,1)S(1)}, bf16[128,896]{1,0:T(8,128)(2,1)S(1)}, u32[]{:S(2)}, u32[]{:S(2)}) collective-permute-start(bf16[128,896]{1,0:T(8,128)(2,1)S(1)} %get-tuple-element.44), channel_id=1, source_target_pairs={{0,192},{1,49},{2,194},{3,51},{4,196},{5,53},{6,198},{7,55},{8,200... | collective-permute-start | bytes 688136 | tf_op jit(solution)/shard_map/ppermute | solution.py:46
  39.8 2.3 %collective-permute-start.16 = (bf16[256,256]{1,0:T(8,128)(2,1)S(1)}, bf16[256,256]{1,0:T(8,128)(2,1)S(1)}, u32[]{:S(2)}, u32[]{:S(2)}) collective-permute-start(bf16[256,256]{1,0:T(8,128)(2,1)S(1)} %shard_map.104.mine), channel_id=1, source_target_pairs={{0,1},{1,0},{2,3},{3,2},{4,5},{5,4},{6,7},{7,6},{8,9},{9,8},{10,11... | collective-permute-start | bytes 393224 | tf_op jit(solution)/shard_map/ppermute | solution.py:339
  41.3 11.8 %collective-permute-start.17 = (bf16[1344,256]{1,0:T(8,128)(2,1)S(1)}, bf16[1344,256]{1,0:T(8,128)(2,1)S(1)}, u32[]{:S(2)}, u32[]{:S(2)}) collective-permute-start(bf16[1344,256]{1,0:T(8,128)(2,1)S(1)} %get-tuple-element.54), channel_id=1, source_target_pairs={{0,16},{1,65},{2,18},{3,67},{4,20},{5,69},{6,22},{7,71},{8,24},{9,... | collective-permute-start | bytes 2064392 | tf_op jit(solution)/shard_map/ppermute | solution.py:46
  42.1 13.5 %collective-permute-start.19 = (bf16[1344,256]{1,0:T(8,128)(2,1)S(1)}, bf16[1344,256]{1,0:T(8,128)(2,1)S(1)}, u32[]{:S(2)}, u32[]{:S(2)}) collective-permute-start(bf16[1344,256]{1,0:T(8,128)(2,1)S(1)} %get-tuple-element.56), channel_id=1, source_target_pairs={{0,48},{1,193},{2,50},{3,195},{4,52},{5,197},{6,54},{7,199},{8,56}... | collective-permute-start | bytes 2064392 | tf_op jit(solution)/shard_map/ppermute | solution.py:46
  44.1 11.4 %collective-permute-start.18 = (bf16[512,256]{1,0:T(8,128)(2,1)S(1)}, bf16[512,256]{1,0:T(8,128)(2,1)S(1)}, u32[]{:S(2)}, u32[]{:S(2)}) collective-permute-start(bf16[512,256]{1,0:T(8,128)(2,1)S(1)} %shard_map.105.refs_5_), channel_id=1, source_target_pairs={{0,16},{1,65},{2,18},{3,67},{4,20},{5,69},{6,22},{7,71},{8,24},{9,... | collective-permute-start | bytes 786440 | tf_op jit(solution)/shard_map/ppermute | solution.py:46
  44.2 11.4 %collective-permute-start.20 = (bf16[512,256]{1,0:T(8,128)(2,1)S(1)}, bf16[512,256]{1,0:T(8,128)(2,1)S(1)}, u32[]{:S(2)}, u32[]{:S(2)}) collective-permute-start(bf16[512,256]{1,0:T(8,128)(2,1)S(1)} %shard_map.105.refs_5_), channel_id=1, source_target_pairs={{0,48},{1,193},{2,50},{3,195},{4,52},{5,197},{6,54},{7,199},{8,56}... | collective-permute-start | bytes 786440 | tf_op jit(solution)/shard_map/ppermute | solution.py:46
  47.0 13.8 %collective-permute-start.9 = (bf16[128,896]{1,0:T(8,128)(2,1)S(1)}, bf16[128,896]{1,0:T(8,128)(2,1)S(1)}, u32[]{:S(2)}, u32[]{:S(2)}) collective-permute-start(bf16[128,896]{1,0:T(8,128)(2,1)S(1)} %shard_map.98), channel_id=1, source_target_pairs={{0,8},{8,0},{1,9},{9,1},{2,10},{10,2},{3,11},{11,3},{4,12},{12,4},... | collective-permute-start | bytes 688136 | tf_op jit(solution)/shard_map/ppermute | solution.py:339
  55.6 14.6 %collective-permute-start.21 = (bf16[704,256]{1,0:T(8,128)(2,1)S(1)}, bf16[704,256]{1,0:T(8,128)(2,1)S(1)}, u32[]{:S(2)}, u32[]{:S(2)}) collective-permute-start(bf16[704,256]{1,0:T(8,128)(2,1)S(1)} %shard_map.107), channel_id=1, source_target_pairs={{0,16},{1,65},{2,18},{3,67},{4,20},{5,69},{6,22},{7,71},{8,24},{9,... | collective-permute-start | bytes 1081352 | tf_op jit(solution)/shard_map/ppermute | solution.py:46
  55.7 14.4 %copy-start.7 = (s32[2]{0:T(128)S(1)}, s32[2]{0:T(128)}, u32[]{:S(2)}) copy-start(s32[2]{0:T(128)} %pick.1) | copy-start | bytes 28
  55.7 14.4 %copy-start.8 = (f32[16]{0:T(128)S(1)}, f32[16]{0:T(128)}, u32[]{:S(2)}) copy-start(f32[16]{0:T(128)} %grid.1) | copy-start | bytes 196
  55.7 14.4 %collective-permute-start.22 = (bf16[704,256]{1,0:T(8,128)(2,1)S(1)}, bf16[704,256]{1,0:T(8,128)(2,1)S(1)}, u32[]{:S(2)}, u32[]{:S(2)}) collective-permute-start(bf16[704,256]{1,0:T(8,128)(2,1)S(1)} %shard_map.108), channel_id=1, source_target_pairs={{0,48},{1,193},{2,50},{3,195},{4,52},{5,197},{6,54},{7,199},{8,56}... | collective-permute-start | bytes 1081352 | tf_op jit(solution)/shard_map/ppermute | solution.py:46
  60.9 6.6 %collective-permute-start.10 = (bf16[128,896]{1,0:T(8,128)(2,1)S(1)}, bf16[128,896]{1,0:T(8,128)(2,1)S(1)}, u32[]{:S(2)}, u32[]{:S(2)}) collective-permute-start(bf16[128,896]{1,0:T(8,128)(2,1)S(1)} %shard_map.99.refs_0_), channel_id=1, source_target_pairs={{0,128},{1,33},{2,130},{3,35},{4,132},{5,37},{6,134},{7,39},{8,136... | collective-permute-start | bytes 688136 | tf_op jit(solution)/shard_map/ppermute | solution.py:46
  62.5 7.6 %collective-permute-start.11 = (bf16[128,896]{1,0:T(8,128)(2,1)S(1)}, bf16[128,896]{1,0:T(8,128)(2,1)S(1)}, u32[]{:S(2)}, u32[]{:S(2)}) collective-permute-start(bf16[128,896]{1,0:T(8,128)(2,1)S(1)} %shard_map.99.refs_0_), channel_id=1, source_target_pairs={{0,64},{1,17},{2,66},{3,19},{4,68},{5,21},{6,70},{7,23},{8,72},{9,... | collective-permute-start | bytes 688136 | tf_op jit(solution)/shard_map/ppermute | solution.py:46
  63.0 7.1 %collective-permute-start.12 = (bf16[128,896]{1,0:T(8,128)(2,1)S(1)}, bf16[128,896]{1,0:T(8,128)(2,1)S(1)}, u32[]{:S(2)}, u32[]{:S(2)}) collective-permute-start(bf16[128,896]{1,0:T(8,128)(2,1)S(1)} %shard_map.99.refs_0_), channel_id=1, source_target_pairs={{0,192},{1,49},{2,194},{3,51},{4,196},{5,53},{6,198},{7,55},{8,200... | collective-permute-start | bytes 688136 | tf_op jit(solution)/shard_map/ppermute | solution.py:46

commit v6 on v5

--- a/solution.py
+++ b/solution.py
@@ -201,6 +201,21 @@
         out_shape=[small, small, small, jax.ShapeDtypeStruct((rows // 2, cols), F32)],
         **params(12, 1.6),
     )(me.reshape(1), *parts)
+
+
+def relay_kernel(up, from_up, down, from_down, up_out, down_out):
+    up_out[...] = (up[...].astype(F32) + from_up[...].astype(F32)).astype(BF)
+    down_out[...] = (down[...].astype(F32) + from_down[...].astype(F32)).astype(BF)
+
+
+def relay(*parts):
+    return pl.pallas_call(
+        relay_kernel,
+        in_specs=[VMEM] * 4,
+        out_specs=[VMEM] * 2,
+        out_shape=[jax.ShapeDtypeStruct(parts[0].shape, BF)] * 2,
+        **params(8, 0.1),
+    )(*parts)
 
 
 def gather_rows(me, pieces, whole):
@@ -352,7 +367,7 @@
     up_q, up_t, down_q, down_t = lead_mm(*grads, basis_out, tie(first, two_q), (1, 3), width)
     from_down_t, from_up_q = move(up_t, FIRST[1]), move(down_q, FIRST[3])
     in_half = add(F32, in_chip, swap(in_chip, "zl", 1))
-    up_q, down_t = add(BF, up_q, relay_q), add(BF, down_t, relay_t)
+    up_q, down_t = relay(up_q, relay_q, down_t, relay_t)
     from_down_q, from_up_t = move(up_q, FIRST[1]), move(down_t, FIRST[3])
     eig_own, *eigs = pick_blocks(eig, tie(first, up_q), width)
     up, down = pack(*eigs)

time: 99.4 us -> 99.5 us (level)
  transfers between devices with their start and end apart: 23 -> 23, of which waited for: 7 -> 7; matrix products, arithmetic and copies ran while one was open for 0% -> 0% of each run, Pallas kernels for 8% -> 7%
where the time goes in v6:
time: 99.5 us; the launch traced here: 99.2 us
  starting transfers between devices  39.9 us (40%)
  blocking collectives  25.4 us (26%)
  Pallas kernels  14.8 us (15%)
  waiting for transfers between devices  13.2 us (13%)
  local copies, waits for them, and re-layouts  4.9 us (5%)
    ppermute x18, starting transfers between devices, move(): return lax.ppermute(value, ALL, pairs)  24.4 us
    all_to_all x1, blocking collectives, body(): lax.all_to_all(part, ('zh', 'zl', 'c'), 0, 0, tiled=True)  15.8 us
    ppermute x5, starting transfers between devices, swap(): return lax.ppermute(value, axis, [(i, i ^ bit) for i in range(size)])  15.5 us
    all_to_all x1, blocking collectives, body(): return jnp.sum(lax.all_to_all(over, ('y', 'x'), 0, 0, tiled=True), axis=0)  9.58 us
    ppermute x18, waiting for transfers between devices, move(): return lax.ppermute(value, ALL, pairs)  7.35 us
    ppermute x5, waiting for transfers between devices, swap(): return lax.ppermute(value, axis, [(i, i ^ bit) for i in range(size)])  5.88 us
    pallas_call x1, Pallas kernels, lead_mm(): pl.pallas_call(functools.partial(lead_kernel, hops), in_specs=[SMEM, hbm,...  5.11 us
    unnamed x18, local copies, waits for them, and re-layouts  4.89 us
  transfers between devices with their start and end apart: 23, of which 7 were waited for; matrix products, arithmetic and copies ran while one was open for 0% of the time, Pallas kernels for 7%

profile of v6, /device:TPU:1, one launch (start us, length us, event | category | flops | bytes accessed | tf_op | source)
XLA Modules:
  0.0 99.2 jit_solution(11440385834387439763)
XLA Ops:
  0.0 4.4 %shard_map.91 = (bf16[256,896]{1,0:T(8,128)(2,1)}, bf16[256,896]{1,0:T(8,128)(2,1)}, f32[256,256]{1,0:T(8,128)}, f32[256,256]{1,0:T(8,128)}) custom-call(s32[1]{0:T(128)} %bitcast.1.at, s32[1]{0:T(128)} %bitcast.2.core_at.at, bf16[256,896]{1,0:T(8,128)(2,1)} %q_ref.1, bf16[256,896]{1,0:T(8,128)(2,1)} %t_ref.1, bf16[896,3584]{1,0:T(8,128)(2,1)} %b_ref.1, ...), custom_call_target="tpu_custom_call" | custom-call | flops 5175000064 | tf_op jit(solution)/shard_map/pallas_call | solution.py:122
  4.4 2.2 %collective-permute-start = (bf16[256,896]{1,0:T(8,128)(2,1)}, bf16[256,896]{1,0:T(8,128)(2,1)S(1)}, u32[]{:S(2)}, u32[]{:S(2)}) collective-permute-start(bf16[256,896]{1,0:T(8,128)(2,1)} %get-tuple-element.33), channel_id=1, source_target_pairs={{0,16},{1,65},{2,18},{3,67},{4,20},{5,69},{6,22},{7,71},{8,24},{9,... | collective-permute-start | bytes 1376264 | tf_op jit(solution)/shard_map/ppermute | solution.py:46
  6.6 1.5 %collective-permute-start.1 = (bf16[256,896]{1,0:T(8,128)(2,1)}, bf16[256,896]{1,0:T(8,128)(2,1)S(1)}, u32[]{:S(2)}, u32[]{:S(2)}) collective-permute-start(bf16[256,896]{1,0:T(8,128)(2,1)} %get-tuple-element.37), channel_id=1, source_target_pairs={{0,48},{1,193},{2,50},{3,195},{4,52},{5,197},{6,54},{7,199},{8,56}... | collective-permute-start | bytes 1376264 | tf_op jit(solution)/shard_map/ppermute | solution.py:46
  8.1 2.8 %collective-permute-start.13 = (f32[256,256]{1,0:T(8,128)}, f32[256,256]{1,0:T(8,128)S(1)}, u32[]{:S(2)}, u32[]{:S(2)}) collective-permute-start(f32[256,256]{1,0:T(8,128)} %get-tuple-element.52), channel_id=1, source_target_pairs={{0,1},{1,0},{2,3},{3,2},{4,5},{5,4},{6,7},{7,6},{8,9},{9,8},{10,11... | collective-permute-start | bytes 786440 | tf_op jit(solution)/shard_map/ppermute | solution.py:354
  11.0 5.1 %shard_map.92 = (bf16[256,896]{1,0:T(8,128)(2,1)}, bf16[256,896]{1,0:T(8,128)(2,1)}, bf16[256,896]{1,0:T(8,128)(2,1)}, bf16[256,896]{1,0:T(8,128)(2,1)}) custom-call(s32[1]{0:T(128)} %bitcast.3.at, bf16[256,896]{1,0:T(8,128)(2,1)} %q_ref.1, bf16[256,896]{1,0:T(8,128)(2,1)} %t_ref.1, bf16[896,3584]{1,0:T(8,128)(2,1)} %b_ref.1), custom_call_target="tpu_custom_call" | custom-call | flops 5750000128 | tf_op jit(solution)/shard_map/pallas_call | solution.py:81
  16.1 1.1 %collective-permute-start.3 = (bf16[256,896]{1,0:T(8,128)(2,1)}, bf16[256,896]{1,0:T(8,128)(2,1)S(1)}, u32[]{:S(2)}, u32[]{:S(2)}) collective-permute-start(bf16[256,896]{1,0:T(8,128)(2,1)} %get-tuple-element.43), channel_id=1, source_target_pairs={{0,48},{1,193},{2,50},{3,195},{4,52},{5,197},{6,54},{7,199},{8,56}... | collective-permute-start | bytes 1376264 | tf_op jit(solution)/shard_map/ppermute | solution.py:46
  17.6 1.0 %copy-done.1 = bf16[256,896]{1,0:T(8,128)(2,1)S(1)} copy-done((bf16[256,896]{1,0:T(8,128)(2,1)S(1)}, bf16[256,896]{1,0:T(8,128)(2,1)}, u32[]{:S(2)}) %copy-start.1) | copy-done | bytes 458776
  18.6 1.0 %copy-done.2 = bf16[256,896]{1,0:T(8,128)(2,1)S(1)} copy-done((bf16[256,896]{1,0:T(8,128)(2,1)S(1)}, bf16[256,896]{1,0:T(8,128)(2,1)}, u32[]{:S(2)}) %copy-start.2) | copy-done | bytes 458776
  20.0 2.7 %collective-permute-start.5 = (bf16[256,896]{1,0:T(8,128)(2,1)S(1)}, bf16[256,896]{1,0:T(8,128)(2,1)S(1)}, u32[]{:S(2)}, u32[]{:S(2)}) collective-permute-start(bf16[256,896]{1,0:T(8,128)(2,1)S(1)} %get-tuple-element.39), channel_id=1, source_target_pairs={{0,48},{1,193},{2,50},{3,195},{4,52},{5,197},{6,54},{7,199},{8,56}... | collective-permute-start | bytes 1376264 | tf_op jit(solution)/shard_map/ppermute | solution.py:46
  22.7 1.3 %collective-permute-start.14 = (f32[256,256]{1,0:T(8,128)S(1)}, f32[256,256]{1,0:T(8,128)S(1)}, u32[]{:S(2)}, u32[]{:S(2)}) collective-permute-start(f32[256,256]{1,0:T(8,128)S(1)} %shard_map.100.refs_0_), channel_id=1, source_target_pairs={{0,2},{2,0},{4,6},{6,4},{1,3},{3,1},{5,7},{7,5},{8,10},{10,8},{12,... | collective-permute-start | bytes 786440 | tf_op jit(solution)/shard_map/ppermute | solution.py:354
  24.0 2.8 %copy-done.4 = bf16[896,3584]{1,0:T(8,128)(2,1)S(1)} copy-done((bf16[896,3584]{1,0:T(8,128)(2,1)S(1)}, bf16[896,3584]{1,0:T(8,128)(2,1)}, u32[]{:S(2)}) %copy-start.4) | copy-done | bytes 6422552
  26.8 1.2 %shard_map.94 = (f32[256,896]{1,0:T(8,128)S(1)}, f32[256,896]{1,0:T(8,128)S(1)}) custom-call(s32[1]{0:T(128)} %bitcast.4.at, bf16[256,896]{1,0:T(8,128)(2,1)S(1)} %copy-done.5, bf16[256,896]{1,0:T(8,128)(2,1)S(1)} %copy-done.6, bf16[896,3584]{1,0:T(8,128)(2,1)S(1)} %copy-done.4), custom_call_target="tpu_custom_call" | custom-call | flops 4600000000 | tf_op jit(solution)/shard_map/pallas_call | solution.py:153
  28.1 1.6 %collective-permute-done.14.refs_1_ = f32[256,256]{1,0:T(8,128)S(1)} collective-permute-done((f32[256,256]{1,0:T(8,128)S(1)}, f32[256,256]{1,0:T(8,128)S(1)}, u32[]{:S(2)}, u32[]{:S(2)}) %collective-permute-start.14) | collective-permute-done | bytes 262176 | tf_op jit(solution)/shard_map/ppermute | solution.py:354
  29.8 3.9 %collective-permute-start.15 = (bf16[256,256]{1,0:T(8,128)(2,1)S(1)}, bf16[256,256]{1,0:T(8,128)(2,1)S(1)}, u32[]{:S(2)}, u32[]{:S(2)}) collective-permute-start(bf16[256,256]{1,0:T(8,128)(2,1)S(1)} %shard_map.102), channel_id=1, source_target_pairs={{0,4},{2,6},{4,0},{6,2},{1,5},{3,7},{5,1},{7,3},{8,12},{10,14},{12... | collective-permute-start | bytes 393224 | tf_op jit(solution)/shard_map/ppermute | solution.py:354
  34.1 1.8 %collective-permute-start.6 = (bf16[128,896]{1,0:T(8,128)(2,1)S(1)}, bf16[128,896]{1,0:T(8,128)(2,1)S(1)}, u32[]{:S(2)}, u32[]{:S(2)}) collective-permute-start(bf16[128,896]{1,0:T(8,128)(2,1)S(1)} %get-tuple-element.46), channel_id=1, source_target_pairs={{0,128},{1,33},{2,130},{3,35},{4,132},{5,37},{6,134},{7,39},{8,136... | collective-permute-start | bytes 688136 | tf_op jit(solution)/shard_map/ppermute | solution.py:46
  35.9 2.7 %collective-permute-start.8 = (bf16[128,896]{1,0:T(8,128)(2,1)S(1)}, bf16[128,896]{1,0:T(8,128)(2,1)S(1)}, u32[]{:S(2)}, u32[]{:S(2)}) collective-permute-start(bf16[128,896]{1,0:T(8,128)(2,1)S(1)} %get-tuple-element.48), channel_id=1, source_target_pairs={{0,192},{1,49},{2,194},{3,51},{4,196},{5,53},{6,198},{7,55},{8,200... | collective-permute-start | bytes 688136 | tf_op jit(solution)/shard_map/ppermute | solution.py:46
  38.6 1.2 %collective-permute-done.15.refs_1_ = bf16[256,256]{1,0:T(8,128)(2,1)S(1)} collective-permute-done((bf16[256,256]{1,0:T(8,128)(2,1)S(1)}, bf16[256,256]{1,0:T(8,128)(2,1)S(1)}, u32[]{:S(2)}, u32[]{:S(2)}) %collective-permute-start.15) | collective-permute-done | bytes 131104 | tf_op jit(solution)/shard_map/ppermute | solution.py:354
  39.8 1.3 %collective-permute-start.16 = (bf16[256,256]{1,0:T(8,128)(2,1)S(1)}, bf16[256,256]{1,0:T(8,128)(2,1)S(1)}, u32[]{:S(2)}, u32[]{:S(2)}) collective-permute-start(bf16[256,256]{1,0:T(8,128)(2,1)S(1)} %shard_map.103.mine), channel_id=1, source_target_pairs={{0,1},{1,0},{2,3},{3,2},{4,5},{5,4},{6,7},{7,6},{8,9},{9,8},{10,11... | collective-permute-start | bytes 393224 | tf_op jit(solution)/shard_map/ppermute | solution.py:354
  42.1 2.0 %collective-permute-start.19 = (bf16[1344,256]{1,0:T(8,128)(2,1)S(1)}, bf16[1344,256]{1,0:T(8,128)(2,1)S(1)}, u32[]{:S(2)}, u32[]{:S(2)}) collective-permute-start(bf16[1344,256]{1,0:T(8,128)(2,1)S(1)} %get-tuple-element.60), channel_id=1, source_target_pairs={{0,48},{1,193},{2,50},{3,195},{4,52},{5,197},{6,54},{7,199},{8,56}... | collective-permute-start | bytes 2064392 | tf_op jit(solution)/shard_map/ppermute | solution.py:46
  44.2 2.7 %collective-permute-start.20 = (bf16[512,256]{1,0:T(8,128)(2,1)S(1)}, bf16[512,256]{1,0:T(8,128)(2,1)S(1)}, u32[]{:S(2)}, u32[]{:S(2)}) collective-permute-start(bf16[512,256]{1,0:T(8,128)(2,1)S(1)} %shard_map.104.refs_5_), channel_id=1, source_target_pairs={{0,48},{1,193},{2,50},{3,195},{4,52},{5,197},{6,54},{7,199},{8,56}... | collective-permute-start | bytes 786440 | tf_op jit(solution)/shard_map/ppermute | solution.py:46
  47.0 6.1 %collective-permute-start.9 = (bf16[128,896]{1,0:T(8,128)(2,1)S(1)}, bf16[128,896]{1,0:T(8,128)(2,1)S(1)}, u32[]{:S(2)}, u32[]{:S(2)}) collective-permute-start(bf16[128,896]{1,0:T(8,128)(2,1)S(1)} %shard_map.97), channel_id=1, source_target_pairs={{0,8},{8,0},{1,9},{9,1},{2,10},{10,2},{3,11},{11,3},{4,12},{12,4},... | collective-permute-start | bytes 688136 | tf_op jit(solution)/shard_map/ppermute | solution.py:354
  53.1 2.4 %collective-permute-done.18.rot_in.refs_7_ = bf16[512,256]{1,0:T(8,128)(2,1)S(1)} collective-permute-done((bf16[512,256]{1,0:T(8,128)(2,1)S(1)}, bf16[512,256]{1,0:T(8,128)(2,1)S(1)}, u32[]{:S(2)}, u32[]{:S(2)}) %collective-permute-start.18) | collective-permute-done | bytes 262176 | tf_op jit(solution)/shard_map/ppermute | solution.py:46
  55.7 2.7 %collective-permute-start.22 = (bf16[704,256]{1,0:T(8,128)(2,1)S(1)}, bf16[704,256]{1,0:T(8,128)(2,1)S(1)}, u32[]{:S(2)}, u32[]{:S(2)}) collective-permute-start(bf16[704,256]{1,0:T(8,128)(2,1)S(1)} %shard_map.107), channel_id=1, source_target_pairs={{0,48},{1,193},{2,50},{3,195},{4,52},{5,197},{6,54},{7,199},{8,56}... | collective-permute-start | bytes 1081352 | tf_op jit(solution)/shard_map/ppermute | solution.py:46
  58.4 2.4 %collective-permute-done.9.refs_1_ = bf16[128,896]{1,0:T(8,128)(2,1)S(1)} collective-permute-done((bf16[128,896]{1,0:T(8,128)(2,1)S(1)}, bf16[128,896]{1,0:T(8,128)(2,1)S(1)}, u32[]{:S(2)}, u32[]{:S(2)}) %collective-permute-start.9) | collective-permute-done | bytes 229408 | tf_op jit(solution)/shard_map/ppermute | solution.py:354
  60.9 1.6 %collective-permute-start.10 = (bf16[128,896]{1,0:T(8,128)(2,1)S(1)}, bf16[128,896]{1,0:T(8,128)(2,1)S(1)}, u32[]{:S(2)}, u32[]{:S(2)}) collective-permute-start(bf16[128,896]{1,0:T(8,128)(2,1)S(1)} %shard_map.98.refs_0_), channel_id=1, source_target_pairs={{0,128},{1,33},{2,130},{3,35},{4,132},{5,37},{6,134},{7,39},{8,136... | collective-permute-start | bytes 688136 | tf_op jit(solution)/shard_map/ppermute | solution.py:46
  62.5 0.8 collective-permute-start.11
  63.3 1.9 %collective-permute-start.12 = (bf16[128,896]{1,0:T(8,128)(2,1)S(1)}, bf16[128,896]{1,0:T(8,128)(2,1)S(1)}, u32[]{:S(2)}, u32[]{:S(2)}) collective-permute-start(bf16[128,896]{1,0:T(8,128)(2,1)S(1)} %shard_map.98.refs_0_), channel_id=1, source_target_pairs={{0,192},{1,49},{2,194},{3,51},{4,196},{5,53},{6,198},{7,55},{8,200... | collective-permute-start | bytes 688136 | tf_op jit(solution)/shard_map/ppermute | solution.py:46
  65.2 2.3 %collective-permute-done.10.refs_1_ = bf16[128,896]{1,0:T(8,128)(2,1)S(1)} collective-permute-done((bf16[128,896]{1,0:T(8,128)(2,1)S(1)}, bf16[128,896]{1,0:T(8,128)(2,1)S(1)}, u32[]{:S(2)}, u32[]{:S(2)}) %collective-permute-start.10) | collective-permute-done | bytes 229408 | tf_op jit(solution)/shard_map/ppermute | solution.py:46
  67.4 2.6 %collective-permute-done.11.refs_2_ = bf16[128,896]{1,0:T(8,128)(2,1)S(1)} collective-permute-done((bf16[128,896]{1,0:T(8,128)(2,1)S(1)}, bf16[128,896]{1,0:T(8,128)(2,1)S(1)}, u32[]{:S(2)}, u32[]{:S(2)}) %collective-permute-start.11) | collective-permute-done | bytes 229408 | tf_op jit(solution)/shard_map/ppermute | solution.py:46
  70.1 3.0 %shard_map.108 = f32[16,2,256]{2,1,0:T(2,128)S(1)} custom-call(s32[1]{0:T(128)} %bitcast.at.me, s32[2]{0:T(128)S(1)} %copy-done.7, f32[16]{0:T(128)S(1)} %copy-done.8, bf16[128,896]{1,0:T(8,128)(2,1)S(1)} %shard_map.98.refs_0_, bf16[128,896]{1,0:T(8,128)(2,1)S(1)} %collective-permute-done.10.refs_1_, bf16[128,896]{1,0:T(8,128)(2,1)S(1)} %collective-permute-done.11.refs_2_, ...), custom_call_target="tpu_custom_call" | custom-call | flops 3449999872 | tf_op jit(solution)/shard_map/pallas_call | solution.py:332
  73.1 15.8 %all_to_all.10 = f32[16,2,256]{2,1,0:T(2,128)S(1)} all-to-all(f32[16,2,256]{2,1,0:T(2,128)S(1)} %shard_map.108), channel_id=1, replica_groups=mesh['y'=4,'x'=4,'zh'=2,'zl'=4,'c'=2] {'zh','zl','c'}, dimensions={0} | all-to-all | bytes 65536 | tf_op jit(solution)/shard_map/all_to_all | solution.py:392
  89.0 9.6 %all_to_all.11 = f32[16,2,256]{2,1,0:T(2,128)S(1)} all-to-all(f32[16,2,256]{2,1,0:T(2,128)S(1)} %broadcast_in_dim.2), channel_id=1, replica_groups=mesh['y'=4,'x'=4,'zh'=2,'zl'=4,'c'=2] {'y','x'}, dimensions={0} | all-to-all | bytes 65536 | tf_op jit(solution)/shard_map/all_to_all | solution.py:394
  (55 shorter events, 3.3 us)
Async XLA Ops:
  4.4 13.2 %collective-permute-start = (bf16[256,896]{1,0:T(8,128)(2,1)}, bf16[256,896]{1,0:T(8,128)(2,1)S(1)}, u32[]{:S(2)}, u32[]{:S(2)}) collective-permute-start(bf16[256,896]{1,0:T(8,128)(2,1)} %get-tuple-element.33), channel_id=1, source_target_pairs={{0,16},{1,65},{2,18},{3,67},{4,20},{5,69},{6,22},{7,71},{8,24},{9,... | collective-permute-start | bytes 1376264 | tf_op jit(solution)/shard_map/ppermute | solution.py:46
  6.6 11.0 %collective-permute-start.1 = (bf16[256,896]{1,0:T(8,128)(2,1)}, bf16[256,896]{1,0:T(8,128)(2,1)S(1)}, u32[]{:S(2)}, u32[]{:S(2)}) collective-permute-start(bf16[256,896]{1,0:T(8,128)(2,1)} %get-tuple-element.37), channel_id=1, source_target_pairs={{0,48},{1,193},{2,50},{3,195},{4,52},{5,197},{6,54},{7,199},{8,56}... | collective-permute-start | bytes 1376264 | tf_op jit(solution)/shard_map/ppermute | solution.py:46
  8.1 14.5 %collective-permute-start.13 = (f32[256,256]{1,0:T(8,128)}, f32[256,256]{1,0:T(8,128)S(1)}, u32[]{:S(2)}, u32[]{:S(2)}) collective-permute-start(f32[256,256]{1,0:T(8,128)} %get-tuple-element.52), channel_id=1, source_target_pairs={{0,1},{1,0},{2,3},{3,2},{4,5},{5,4},{6,7},{7,6},{8,9},{9,8},{10,11... | collective-permute-start | bytes 786440 | tf_op jit(solution)/shard_map/ppermute | solution.py:354
  10.9 11.7 %copy-start.3 = (f32[256,256]{1,0:T(8,128)S(1)}, f32[256,256]{1,0:T(8,128)}, u32[]{:S(2)}) copy-start(f32[256,256]{1,0:T(8,128)} %get-tuple-element.51.refs_0_) | copy-start | bytes 786436
  10.9 13.1 %copy-start.5 = (bf16[256,896]{1,0:T(8,128)(2,1)S(1)}, bf16[256,896]{1,0:T(8,128)(2,1)}, u32[]{:S(2)}) copy-start(bf16[256,896]{1,0:T(8,128)(2,1)} %q_ref.1) | copy-start | bytes 1376260
  11.0 13.1 %copy-start.6 = (bf16[256,896]{1,0:T(8,128)(2,1)S(1)}, bf16[256,896]{1,0:T(8,128)(2,1)}, u32[]{:S(2)}) copy-start(bf16[256,896]{1,0:T(8,128)(2,1)} %t_ref.1) | copy-start | bytes 1376260
  16.1 17.7 %collective-permute-start.3 = (bf16[256,896]{1,0:T(8,128)(2,1)}, bf16[256,896]{1,0:T(8,128)(2,1)S(1)}, u32[]{:S(2)}, u32[]{:S(2)}) collective-permute-start(bf16[256,896]{1,0:T(8,128)(2,1)} %get-tuple-element.43), channel_id=1, source_target_pairs={{0,48},{1,193},{2,50},{3,195},{4,52},{5,197},{6,54},{7,199},{8,56}... | collective-permute-start | bytes 1376264 | tf_op jit(solution)/shard_map/ppermute | solution.py:46
  17.1 16.6 %collective-permute-start.4 = (bf16[256,896]{1,0:T(8,128)(2,1)}, bf16[256,896]{1,0:T(8,128)(2,1)S(1)}, u32[]{:S(2)}, u32[]{:S(2)}) collective-permute-start(bf16[256,896]{1,0:T(8,128)(2,1)} %get-tuple-element.44), channel_id=1, source_target_pairs={{0,16},{1,65},{2,18},{3,67},{4,20},{5,69},{6,22},{7,71},{8,24},{9,... | collective-permute-start | bytes 1376264 | tf_op jit(solution)/shard_map/ppermute | solution.py:46
  17.6 1.0 %copy-start.1 = (bf16[256,896]{1,0:T(8,128)(2,1)S(1)}, bf16[256,896]{1,0:T(8,128)(2,1)}, u32[]{:S(2)}) copy-start(bf16[256,896]{1,0:T(8,128)(2,1)} %get-tuple-element.35.up) | copy-start | bytes 1376260
  18.6 1.0 %copy-start.2 = (bf16[256,896]{1,0:T(8,128)(2,1)S(1)}, bf16[256,896]{1,0:T(8,128)(2,1)}, u32[]{:S(2)}) copy-start(bf16[256,896]{1,0:T(8,128)(2,1)} %get-tuple-element.36.down) | copy-start | bytes 1376260
  19.9 13.8 %collective-permute-start.2 = (bf16[256,896]{1,0:T(8,128)(2,1)S(1)}, bf16[256,896]{1,0:T(8,128)(2,1)S(1)}, u32[]{:S(2)}, u32[]{:S(2)}) collective-permute-start(bf16[256,896]{1,0:T(8,128)(2,1)S(1)} %get-tuple-element.38), channel_id=1, source_target_pairs={{0,16},{1,65},{2,18},{3,67},{4,20},{5,69},{6,22},{7,71},{8,24},{9,... | collective-permute-start | bytes 1376264 | tf_op jit(solution)/shard_map/ppermute | solution.py:46
  20.0 13.8 %collective-permute-start.5 = (bf16[256,896]{1,0:T(8,128)(2,1)S(1)}, bf16[256,896]{1,0:T(8,128)(2,1)S(1)}, u32[]{:S(2)}, u32[]{:S(2)}) collective-permute-start(bf16[256,896]{1,0:T(8,128)(2,1)S(1)} %get-tuple-element.39), channel_id=1, source_target_pairs={{0,48},{1,193},{2,50},{3,195},{4,52},{5,197},{6,54},{7,199},{8,56}... | collective-permute-start | bytes 1376264 | tf_op jit(solution)/shard_map/ppermute | solution.py:46
  22.7 7.1 %collective-permute-start.14 = (f32[256,256]{1,0:T(8,128)S(1)}, f32[256,256]{1,0:T(8,128)S(1)}, u32[]{:S(2)}, u32[]{:S(2)}) collective-permute-start(f32[256,256]{1,0:T(8,128)S(1)} %shard_map.100.refs_0_), channel_id=1, source_target_pairs={{0,2},{2,0},{4,6},{6,4},{1,3},{3,1},{5,7},{7,5},{8,10},{10,8},{12,... | collective-permute-start | bytes 786440 | tf_op jit(solution)/shard_map/ppermute | solution.py:354
  24.0 2.8 %copy-start.4 = (bf16[896,3584]{1,0:T(8,128)(2,1)S(1)}, bf16[896,3584]{1,0:T(8,128)(2,1)}, u32[]{:S(2)}) copy-start(bf16[896,3584]{1,0:T(8,128)(2,1)} %b_ref.1) | copy-start | bytes 19267588
  28.1 13.0 %copy-start = (bf16[3584,256]{1,0:T(8,128)(2,1)S(1)}, bf16[3584,256]{1,0:T(8,128)(2,1)}, u32[]{:S(2)}) copy-start(bf16[3584,256]{1,0:T(8,128)(2,1)} %refs_3_.1) | copy-start | bytes 5505028
  29.8 9.9 %collective-permute-start.15 = (bf16[256,256]{1,0:T(8,128)(2,1)S(1)}, bf16[256,256]{1,0:T(8,128)(2,1)S(1)}, u32[]{:S(2)}, u32[]{:S(2)}) collective-permute-start(bf16[256,256]{1,0:T(8,128)(2,1)S(1)} %shard_map.102), channel_id=1, source_target_pairs={{0,4},{2,6},{4,0},{6,2},{1,5},{3,7},{5,1},{7,3},{8,12},{10,14},{12... | collective-permute-start | bytes 393224 | tf_op jit(solution)/shard_map/ppermute | solution.py:354
  34.1 10.0 %collective-permute-start.6 = (bf16[128,896]{1,0:T(8,128)(2,1)S(1)}, bf16[128,896]{1,0:T(8,128)(2,1)S(1)}, u32[]{:S(2)}, u32[]{:S(2)}) collective-permute-start(bf16[128,896]{1,0:T(8,128)(2,1)S(1)} %get-tuple-element.46), channel_id=1, source_target_pairs={{0,128},{1,33},{2,130},{3,35},{4,132},{5,37},{6,134},{7,39},{8,136... | collective-permute-start | bytes 688136 | tf_op jit(solution)/shard_map/ppermute | solution.py:46
  35.9 8.3 %collective-permute-start.7 = (bf16[128,896]{1,0:T(8,128)(2,1)S(1)}, bf16[128,896]{1,0:T(8,128)(2,1)S(1)}, u32[]{:S(2)}, u32[]{:S(2)}) collective-permute-start(bf16[128,896]{1,0:T(8,128)(2,1)S(1)} %get-tuple-element.47), channel_id=1, source_target_pairs={{0,64},{1,17},{2,66},{3,19},{4,68},{5,21},{6,70},{7,23},{8,72},{9,... | collective-permute-start | bytes 688136 | tf_op jit(solution)/shard_map/ppermute | solution.py:46
  35.9 11.0 %collective-permute-start.8 = (bf16[128,896]{1,0:T(8,128)(2,1)S(1)}, bf16[128,896]{1,0:T(8,128)(2,1)S(1)}, u32[]{:S(2)}, u32[]{:S(2)}) collective-permute-start(bf16[128,896]{1,0:T(8,128)(2,1)S(1)} %get-tuple-element.48), channel_id=1, source_target_pairs={{0,192},{1,49},{2,194},{3,51},{4,196},{5,53},{6,198},{7,55},{8,200... | collective-permute-start | bytes 688136 | tf_op jit(solution)/shard_map/ppermute | solution.py:46
  39.8 2.3 %collective-permute-start.16 = (bf16[256,256]{1,0:T(8,128)(2,1)S(1)}, bf16[256,256]{1,0:T(8,128)(2,1)S(1)}, u32[]{:S(2)}, u32[]{:S(2)}) collective-permute-start(bf16[256,256]{1,0:T(8,128)(2,1)S(1)} %shard_map.103.mine), channel_id=1, source_target_pairs={{0,1},{1,0},{2,3},{3,2},{4,5},{5,4},{6,7},{7,6},{8,9},{9,8},{10,11... | collective-permute-start | bytes 393224 | tf_op jit(solution)/shard_map/ppermute | solution.py:354
  41.3 11.8 %collective-permute-start.17 = (bf16[1344,256]{1,0:T(8,128)(2,1)S(1)}, bf16[1344,256]{1,0:T(8,128)(2,1)S(1)}, u32[]{:S(2)}, u32[]{:S(2)}) collective-permute-start(bf16[1344,256]{1,0:T(8,128)(2,1)S(1)} %get-tuple-element.58), channel_id=1, source_target_pairs={{0,16},{1,65},{2,18},{3,67},{4,20},{5,69},{6,22},{7,71},{8,24},{9,... | collective-permute-start | bytes 2064392 | tf_op jit(solution)/shard_map/ppermute | solution.py:46
  42.1 13.5 %collective-permute-start.19 = (bf16[1344,256]{1,0:T(8,128)(2,1)S(1)}, bf16[1344,256]{1,0:T(8,128)(2,1)S(1)}, u32[]{:S(2)}, u32[]{:S(2)}) collective-permute-start(bf16[1344,256]{1,0:T(8,128)(2,1)S(1)} %get-tuple-element.60), channel_id=1, source_target_pairs={{0,48},{1,193},{2,50},{3,195},{4,52},{5,197},{6,54},{7,199},{8,56}... | collective-permute-start | bytes 2064392 | tf_op jit(solution)/shard_map/ppermute | solution.py:46
  44.1 11.4 %collective-permute-start.18 = (bf16[512,256]{1,0:T(8,128)(2,1)S(1)}, bf16[512,256]{1,0:T(8,128)(2,1)S(1)}, u32[]{:S(2)}, u32[]{:S(2)}) collective-permute-start(bf16[512,256]{1,0:T(8,128)(2,1)S(1)} %shard_map.104.refs_5_), channel_id=1, source_target_pairs={{0,16},{1,65},{2,18},{3,67},{4,20},{5,69},{6,22},{7,71},{8,24},{9,... | collective-permute-start | bytes 786440 | tf_op jit(solution)/shard_map/ppermute | solution.py:46
  44.2 11.4 %collective-permute-start.20 = (bf16[512,256]{1,0:T(8,128)(2,1)S(1)}, bf16[512,256]{1,0:T(8,128)(2,1)S(1)}, u32[]{:S(2)}, u32[]{:S(2)}) collective-permute-start(bf16[512,256]{1,0:T(8,128)(2,1)S(1)} %shard_map.104.refs_5_), channel_id=1, source_target_pairs={{0,48},{1,193},{2,50},{3,195},{4,52},{5,197},{6,54},{7,199},{8,56}... | collective-permute-start | bytes 786440 | tf_op jit(solution)/shard_map/ppermute | solution.py:46
  47.0 13.8 %collective-permute-start.9 = (bf16[128,896]{1,0:T(8,128)(2,1)S(1)}, bf16[128,896]{1,0:T(8,128)(2,1)S(1)}, u32[]{:S(2)}, u32[]{:S(2)}) collective-permute-start(bf16[128,896]{1,0:T(8,128)(2,1)S(1)} %shard_map.97), channel_id=1, source_target_pairs={{0,8},{8,0},{1,9},{9,1},{2,10},{10,2},{3,11},{11,3},{4,12},{12,4},... | collective-permute-start | bytes 688136 | tf_op jit(solution)/shard_map/ppermute | solution.py:354
  55.5 14.6 %collective-permute-start.21 = (bf16[704,256]{1,0:T(8,128)(2,1)S(1)}, bf16[704,256]{1,0:T(8,128)(2,1)S(1)}, u32[]{:S(2)}, u32[]{:S(2)}) collective-permute-start(bf16[704,256]{1,0:T(8,128)(2,1)S(1)} %shard_map.106), channel_id=1, source_target_pairs={{0,16},{1,65},{2,18},{3,67},{4,20},{5,69},{6,22},{7,71},{8,24},{9,... | collective-permute-start | bytes 1081352 | tf_op jit(solution)/shard_map/ppermute | solution.py:46
  55.7 14.4 %copy-start.7 = (s32[2]{0:T(128)S(1)}, s32[2]{0:T(128)}, u32[]{:S(2)}) copy-start(s32[2]{0:T(128)} %pick.1) | copy-start | bytes 28
  55.7 14.4 %copy-start.8 = (f32[16]{0:T(128)S(1)}, f32[16]{0:T(128)}, u32[]{:S(2)}) copy-start(f32[16]{0:T(128)} %grid.1) | copy-start | bytes 196
  55.7 14.4 %collective-permute-start.22 = (bf16[704,256]{1,0:T(8,128)(2,1)S(1)}, bf16[704,256]{1,0:T(8,128)(2,1)S(1)}, u32[]{:S(2)}, u32[]{:S(2)}) collective-permute-start(bf16[704,256]{1,0:T(8,128)(2,1)S(1)} %shard_map.107), channel_id=1, source_target_pairs={{0,48},{1,193},{2,50},{3,195},{4,52},{5,197},{6,54},{7,199},{8,56}... | collective-permute-start | bytes 1081352 | tf_op jit(solution)/shard_map/ppermute | solution.py:46
  60.9 6.6 %collective-permute-start.10 = (bf16[128,896]{1,0:T(8,128)(2,1)S(1)}, bf16[128,896]{1,0:T(8,128)(2,1)S(1)}, u32[]{:S(2)}, u32[]{:S(2)}) collective-permute-start(bf16[128,896]{1,0:T(8,128)(2,1)S(1)} %shard_map.98.refs_0_), channel_id=1, source_target_pairs={{0,128},{1,33},{2,130},{3,35},{4,132},{5,37},{6,134},{7,39},{8,136... | collective-permute-start | bytes 688136 | tf_op jit(solution)/shard_map/ppermute | solution.py:46
  62.5 7.6 %collective-permute-start.11 = (bf16[128,896]{1,0:T(8,128)(2,1)S(1)}, bf16[128,896]{1,0:T(8,128)(2,1)S(1)}, u32[]{:S(2)}, u32[]{:S(2)}) collective-permute-start(bf16[128,896]{1,0:T(8,128)(2,1)S(1)} %shard_map.98.refs_0_), channel_id=1, source_target_pairs={{0,64},{1,17},{2,66},{3,19},{4,68},{5,21},{6,70},{7,23},{8,72},{9,... | collective-permute-start | bytes 688136 | tf_op jit(solution)/shard_map/ppermute | solution.py:46
  63.3 6.8 %collective-permute-start.12 = (bf16[128,896]{1,0:T(8,128)(2,1)S(1)}, bf16[128,896]{1,0:T(8,128)(2,1)S(1)}, u32[]{:S(2)}, u32[]{:S(2)}) collective-permute-start(bf16[128,896]{1,0:T(8,128)(2,1)S(1)} %shard_map.98.refs_0_), channel_id=1, source_target_pairs={{0,192},{1,49},{2,194},{3,51},{4,196},{5,53},{6,198},{7,55},{8,200... | collective-permute-start | bytes 688136 | tf_op jit(solution)/shard_map/ppermute | solution.py:46
